TPU v7x, 32 devices: a whole 2x2x4 slice. The times are simulated.
32 devices in a mesh: row: 2 (over core), col: 16 (over z, y, x).
Axes of the slice: x: 2, y: 2, z: 4, core: 2. Of those that a mesh axis runs over, the one named last changes fastest.
Arguments:
- features: bfloat16 [16384, 128], P(('row', 'col')), may hold values from -6 to 6
- weight: bfloat16 [128, 128], replicated, may hold values from -0.5 to 0.5
- bias: float32 [128], replicated, may hold values from -3 to 3
- cotangent: bfloat16 [16384, 128], P(('row', 'col')), may hold values from -6 to 6
- block_count: int32 [2, 16], P('row', 'col'), may hold values from 64 to 512
- block_rows: int32 [2, 16, 512], P('row', 'col'), may hold values from 0 to 63
- block_cols: int32 [2, 16, 512], P('row', 'col'), may hold values from 0 to 7
- edge_offsets: int32 [2, 16, 512, 128], P('row', 'col'), may hold values from 0 to 16383, as said below
- edge_weight: bfloat16 [2, 16, 512, 128], P('row', 'col'), may hold values from 0.0099487305 to 0.099609375
Outputs:
- output: bfloat16 [16384, 128], P(('row', 'col'))
- grad_features: bfloat16 [16384, 128], P(('row', 'col'))
- grad_weight: float32 [128, 128], replicated
- grad_bias: float32 [128], replicated
Inputs may be any that keep to these rules, and one draw needn't show every extreme that they name: `edge_offsets`: the offsets within one slot are distinct.
All inputs are finite; a program needn't handle non-finite values.
Results may differ from a plain program's by a relative error of at most 0.013.
The roundings to bfloat16 on the way count: a program that leaves them out, or rounds other values in their place, can miss the bound.
Values may be sent and summed in bfloat16 or wider, within the bound.
No kernel may reach another device: no remote copies, remote signals or barrier semaphores. Data moves between devices by JAX's collectives and lax.ppermute only.
A program may use at most 128 MiB of HBM per device.

v0:
```python
import functools
import functools
import jax
import jax.numpy as jnp
from jax import lax
from jax.experimental import pallas as pl
from jax.experimental.pallas import tpu as pltpu
from jax.sharding import PartitionSpec as P


def swap(x, axis, bit):
    n = lax.axis_size(axis)
    return lax.ppermute(x, axis, [(i, i ^ bit) for i in range(n)])


def bits_of(axis):
    n = lax.axis_size(axis)
    return [1 << k for k in range(n.bit_length() - 1)]


def scatter_sum(x, axis):
    for bit in bits_of(axis):
        pairs = x.reshape((x.shape[0] // 2, 2) + x.shape[1:])
        x = pairs[:, 0] + swap(pairs[:, 1], axis, bit)
    return x[0]


def part_orders(per):
    bits = bits_of("col")[::-1]
    turned = bits[:-2] + bits[-1:] + bits[-2:-1]
    return [bits, turned] if per % 2 == 0 and len(bits) > 1 else [bits]


def gather_pieces(blocks, beside):
    orders = part_orders(blocks.shape[0])
    size = blocks.shape[0] // len(orders)
    near = [0]
    for bit in orders[0][:-2]:
        near = near + [far | bit for far in near]
    whole = [blocks if far == 0 else swap(blocks, "col", far) for far in near]
    (whole,) = beside(0, [jnp.stack(whole)])
    held = [whole[:, i * size : (i + 1) * size] for i in range(len(orders))]
    if len(orders[0]) > 1:
        came = [swap(x, "col", order[-2]) for x, order in zip(held, orders)]
        held = beside(1, [jnp.concatenate([x, y], axis=0) for x, y in zip(held, came)])
    came = [swap(x, "col", order[-1]) for x, order in zip(held, orders)]
    shape = (-1,) + blocks.shape[1:]
    return [[x.reshape(shape), y.reshape(shape)] for x, y in zip(held, came)]


def piece_index(per, far, block, rho=0, n_row=1):
    orders = part_orders(per)
    size = per // len(orders)
    half = lax.axis_size("col") // 2
    result = 0
    for i, order in enumerate(orders):
        spot = sum(((far & bit) > 0).astype(jnp.int32) << t for t, bit in enumerate(order))
        piece = (i * n_row + rho) * 2 + spot // half
        here = (piece * half + spot % half) * size + block % size
        result = jnp.where(block // size == i, here, result)
    return result


def split_rows(x):
    n, mine = lax.axis_size("row"), lax.axis_index("row")
    size = -(-x.shape[0] // (8 * n)) * 8
    x = jnp.pad(x, ((0, n * size - x.shape[0]), (0, 0)))
    parts = [lax.dynamic_slice_in_dim(x, (mine ^ k) * size, size, 0) for k in range(n)]
    return scatter_sum(jnp.stack(parts), "row")


def join_rows(x):
    n, mine = lax.axis_size("row"), lax.axis_index("row")
    parts = [x]
    for bit in bits_of("row"):
        parts = parts + [swap(part, "row", bit) for part in parts]
    parts = jnp.stack(parts)
    return jnp.concatenate(
        [lax.dynamic_index_in_dim(parts, mine ^ k, 0, keepdims=False) for k in range(n)]
    )


GROUP = 8
TURN = 4 * GROUP
DEPTH = 5
ROOM = 64
SPARE = 8
FIELD = 1 << 16
UNIT = 2.0**-14


def tile_rows():
    shape = (8, 16, 128)
    rows = 16 * lax.broadcasted_iota(jnp.int32, shape, 0) + lax.broadcasted_iota(jnp.int32, shape, 1)
    return rows.astype(jnp.float32).astype(jnp.bfloat16)


def block_of(code, rows):
    def tile(x):
        return jnp.broadcast_to(x.astype(jnp.float32), (16, 128)).astype(jnp.bfloat16)[None]

    o = code >> 16
    zero = jnp.zeros((), jnp.bfloat16)
    one = jnp.ones((), jnp.bfloat16)
    w = tile((code & (FIELD - 1)).astype(jnp.float32) * UNIT)
    left = jnp.where(rows == tile(o >> 7), w, zero).reshape(128, 128)
    right = jnp.where(rows == tile(o & 127), one, zero).reshape(128, 128)
    return lax.dot_general(
        left, right, (((1,), (1,)), ((), ())), preferred_element_type=jnp.float32
    ).astype(jnp.bfloat16)


def pack_kernel(meta, pos, codes, labels, out):
    out[...] = jnp.zeros_like(out)
    stride = ROOM + SPARE
    for k in range(labels.shape[0]):
        out[pl.ds(k * stride + ROOM, 1), :] = labels[pl.ds(k, 1), :]

    def turn(i, _):
        for u in range(GROUP):
            s = i * GROUP + u
            out[pl.ds(pos[s], 1), :] = codes[pl.ds(s, 1), :]
        return 0

    lax.fori_loop(0, meta[0], turn, 0)


def build_kernel(meta, order, codes, *refs):
    dense, dbuf, sems = refs[-3:]
    start, turns = meta[0], meta[1]
    rows = tile_rows()

    def out_copy(i):
        slot = lax.rem(i, DEPTH)
        return pltpu.make_async_copy(
            dbuf.at[slot], dense.at[pl.ds(i * TURN, TURN)], sems.at[slot]
        )

    def turn(i, _):
        slot = lax.rem(i, DEPTH)

        @pl.when(i >= start + DEPTH)
        def _():
            out_copy(i - DEPTH).wait()

        lines = [codes[pl.ds(order[i * TURN + u], 1), :] for u in range(TURN)]
        for u in range(0, TURN, GROUP):
            blocks = [block_of(line, rows) for line in lines[u : u + GROUP]]
            for k, block in enumerate(blocks):
                dbuf[slot, u + k] = block
        out_copy(i).start()
        return 0

    lax.fori_loop(start, turns, turn, 0)

    def finish(i, _):
        out_copy(i).wait()
        return 0

    lax.fori_loop(jnp.maximum(turns - DEPTH, start), turns, finish, 0)


def fetch(pieces, into, sems):
    size = pieces[0].shape[0]
    copies = [
        pltpu.make_async_copy(piece, into.at[pl.ds(i * size, size)], sems.at[i])
        for i, piece in enumerate(pieces)
    ]
    for copy in copies:
        copy.start()
    return copies


def read_dense(turns, dense, dbuf, sems, product, prepare):
    def in_copy(i):
        slot = lax.rem(i, DEPTH)
        return pltpu.make_async_copy(
            dense.at[pl.ds(i * TURN, TURN)], dbuf.at[slot], sems.at[slot]
        )

    def begin(i, _):
        in_copy(i).start()
        return 0

    lax.fori_loop(0, jnp.minimum(turns, DEPTH - 1), begin, 0)
    prepare()

    def turn(i, _):
        @pl.when(i + DEPTH - 1 < turns)
        def _():
            in_copy(i + DEPTH - 1).start()

        in_copy(i).wait()
        product(i, lax.rem(i, DEPTH))
        return 0

    lax.fori_loop(0, turns, turn, 0)


def add_pairs(i, owner, one, into):
    groups = TURN // GROUP
    for g in range(0, groups, 2):
        added = [one(g), one(g + 1)]
        for k in range(2):
            into[owner[i * groups + g + k]] += added[k]


def forward_kernel(n, meta, col, owner, weight, bias, cotangent, dense, *refs):
    pieces, refs = refs[:n], refs[n:]
    output, turned, local, totals, feat, proj, dbuf, piece_sems, sems = refs
    copies = fetch(pieces, feat, piece_sems)
    size, _, width = pieces[0].shape
    batch = 8 if size % 8 == 0 else 1

    def project(t, _):
        spot = pl.ds(t * batch, batch)
        held = feat[spot].reshape(batch * 128, width)
        low = jnp.dot(held, weight[...], preferred_element_type=jnp.float32)
        proj[spot] = low.astype(jnp.bfloat16).reshape(batch, 128, width)
        return 0

    def prepare():
        totals[...] = jnp.zeros_like(totals)
        for i, copy in enumerate(copies):
            copy.wait()
            lax.fori_loop(i * size // batch, (i + 1) * size // batch, project, 0)

    def product(i, slot):
        def one(g):
            spots = [col[i * TURN + g * GROUP + u] for u in range(GROUP)]
            left = jnp.concatenate([dbuf[slot, g * GROUP + u] for u in range(GROUP)], axis=1)
            right = jnp.concatenate(
                [jnp.concatenate([proj[c], feat[c]], axis=1) for c in spots], axis=0
            )
            return jnp.dot(left, right, preferred_element_type=jnp.float32)

        add_pairs(i, owner, one, totals)

    read_dense(meta[1], dense, dbuf, sems, product, prepare)

    weight_sum, bias_sum = 0.0, 0.0
    for q in range(totals.shape[0]):
        lines = pl.ds(q * 128, 128)
        pre = totals[q, :, :width] + bias[...]
        output[lines, :] = jnp.maximum(pre, 0.0).astype(jnp.bfloat16)
        grad = jnp.where(pre > 0, cotangent[lines, :].astype(jnp.float32), 0.0)
        turned[q] = grad.T.astype(jnp.bfloat16)
        weight_sum += lax.dot_general(
            totals[q, :, width:].astype(jnp.bfloat16),
            grad.astype(jnp.bfloat16),
            (((0,), (0,)), ((), ())),
            preferred_element_type=jnp.float32,
        )
        bias_sum += jnp.sum(grad, axis=0, keepdims=True)
    local[pl.ds(0, width), :] = weight_sum
    local[pl.ds(width, 8), :] = jnp.broadcast_to(bias_sum, (8, width))


def tile_kernel(meta, order, dst, col, codes, panel, totals):
    rows = tile_rows()
    totals[...] = jnp.zeros_like(totals)

    def turn(i, _):
        for u in range(GROUP):
            p = i * GROUP + u
            block = block_of(codes[pl.ds(order[p], 1), :], rows)
            totals[dst[p]] += jnp.dot(block, panel[col[p]], preferred_element_type=jnp.float32)
        return 0

    lax.fori_loop(0, meta[0], turn, 0)


def backward_kernel(n, meta, src, owner, dense, *refs):
    pieces, (acc, grad, dbuf, piece_sems, sems) = refs[:n], refs[n:]
    copies = fetch(pieces, grad, piece_sems)

    def prepare():
        acc[...] = jnp.zeros_like(acc)
        for copy in copies:
            copy.wait()

    def product(i, slot):
        def one(g):
            spots = [src[i * TURN + g * GROUP + u] for u in range(GROUP)]
            left = jnp.concatenate([grad[c] for c in spots], axis=1)
            right = dbuf[slot, pl.ds(g * GROUP, GROUP)].reshape(GROUP * 128, 128)
            return jnp.dot(left, right, preferred_element_type=jnp.float32)

        add_pairs(i, owner, one, acc)

    read_dense(meta[1], dense, dbuf, sems, product, prepare)


SMEM = pl.BlockSpec(memory_space=pltpu.SMEM)
VMEM = pl.BlockSpec(memory_space=pltpu.VMEM)
HBM = pl.BlockSpec(memory_space=pl.ANY)
PARAMS = pltpu.CompilerParams(vmem_limit_bytes=48 * 1024 * 1024)


def cost(slots, products):
    flops = 2 * slots * products * 128**3
    return pl.CostEstimate(flops=flops, bytes_accessed=slots * 128 * 128 * 2, transcendentals=0)


def run_tile(meta, order, dst, col, codes, panel, row_blocks):
    return pl.pallas_call(
        tile_kernel,
        out_shape=jax.ShapeDtypeStruct((row_blocks, 128, panel.shape[-1]), jnp.float32),
        in_specs=[SMEM] * 4 + [VMEM] * 2,
        out_specs=VMEM,
        compiler_params=PARAMS,
    )(meta, order, dst, col, codes, panel)


def run_pack(meta, pos, codes, labels):
    length = labels.shape[0] * (ROOM + SPARE)
    return pl.pallas_call(
        pack_kernel,
        out_shape=jax.ShapeDtypeStruct((length, 128), jnp.int32),
        in_specs=[SMEM] * 2 + [VMEM] * 2,
        out_specs=VMEM,
        compiler_params=PARAMS,
    )(meta, pos, codes, labels)


def run_build(meta, order, codes, after, dense):
    others = after if dense is None else after + [dense]
    return pl.pallas_call(
        build_kernel,
        out_shape=jax.ShapeDtypeStruct((order.shape[0], 128, 128), jnp.bfloat16),
        in_specs=[SMEM] * 2 + [VMEM] + [HBM] * len(others),
        out_specs=HBM,
        scratch_shapes=[
            pltpu.VMEM((DEPTH, TURN, 128, 128), jnp.bfloat16),
            pltpu.SemaphoreType.DMA((DEPTH,)),
        ],
        input_output_aliases={} if dense is None else {2 + len(others): 0},
        compiler_params=PARAMS,
        cost_estimate=cost(order.shape[0], 2),
    )(meta, order, codes, *others)


def run_forward(meta, col, owner, weight, bias, cotangent, dense, feat):
    n = len(feat)
    size, _, width = feat[0].shape
    row_blocks = cotangent.shape[0] // 128
    return pl.pallas_call(
        functools.partial(forward_kernel, n),
        out_shape=(
            jax.ShapeDtypeStruct(cotangent.shape, jnp.bfloat16),
            jax.ShapeDtypeStruct((row_blocks, width, 128), jnp.bfloat16),
            jax.ShapeDtypeStruct((width + 8, width), jnp.float32),
        ),
        in_specs=[SMEM] * 3 + [VMEM] * 3 + [HBM] * (n + 1),
        out_specs=[VMEM] * 3,
        scratch_shapes=[
            pltpu.VMEM((row_blocks, 128, 2 * width), jnp.float32),
            pltpu.VMEM((n * size, 128, width), jnp.bfloat16),
            pltpu.VMEM((n * size, 128, width), jnp.bfloat16),
            pltpu.VMEM((DEPTH, TURN, 128, 128), jnp.bfloat16),
            pltpu.SemaphoreType.DMA((n,)),
            pltpu.SemaphoreType.DMA((DEPTH,)),
        ],
        compiler_params=PARAMS,
        cost_estimate=cost(col.shape[0], 4),
    )(meta, col, owner, weight, bias, cotangent, dense, *feat)


def run_backward(meta, src, owner, pieces, dense, col_blocks):
    n = len(pieces)
    size, width, _ = pieces[0].shape
    return pl.pallas_call(
        functools.partial(backward_kernel, n),
        out_shape=jax.ShapeDtypeStruct((col_blocks, width, 128), jnp.float32),
        in_specs=[SMEM] * 3 + [HBM] * (n + 1),
        out_specs=VMEM,
        scratch_shapes=[
            pltpu.VMEM((n * size, width, 128), jnp.bfloat16),
            pltpu.VMEM((DEPTH, TURN, 128, 128), jnp.bfloat16),
            pltpu.SemaphoreType.DMA((n,)),
            pltpu.SemaphoreType.DMA((DEPTH,)),
        ],
        compiler_params=PARAMS,
        cost_estimate=cost(src.shape[0], 4),
    )(meta, src, owner, dense, *pieces)


def grouped(key, live, value, fill, keys):
    ids = jnp.arange(key.shape[0], dtype=jnp.int32)
    names = jnp.arange(keys, dtype=jnp.int32)
    key = jnp.where(live, key, keys)
    before = (key[:, None] == key[None, :]) & (ids[:, None] < ids[None, :])
    rank = jnp.sum(before.astype(jnp.int32), axis=0)
    counts = jnp.sum((key[:, None] == names[None, :]).astype(jnp.int32), axis=0)
    filled = (counts + GROUP - 1) // GROUP * GROUP
    base = jnp.sum(jnp.where(names[:, None] < key[None, :], filled[:, None], 0), axis=0)
    pos = jnp.where(live, base + rank, -1)
    ends = jnp.sum(jnp.where(names[:, None] <= names[None, :], filled[:, None], 0), axis=0)
    length = -(-(key.shape[0] + keys * GROUP) // TURN) * TURN
    first = jnp.arange(length // GROUP, dtype=jnp.int32) * GROUP
    group_key = jnp.sum((ends[:, None] <= first[None, :]).astype(jnp.int32), axis=0)
    turns = (jnp.sum(filled) + TURN - 1) // TURN
    return place(pos, value, length, fill), jnp.minimum(group_key, keys - 1), turns


def place(pos, value, length, fill):
    spots = jnp.arange(length, dtype=jnp.int32)
    hit = pos[:, None] == spots[None, :]
    return jnp.sum(jnp.where(hit, value[:, None] - fill, 0), axis=0) + fill


def shards(
    features,
    weight,
    bias,
    cotangent,
    block_count,
    block_rows,
    block_cols,
    edge_offsets,
    edge_weight,
):
    node_dev, width = features.shape
    n_row = lax.axis_size("row")
    n_col = lax.axis_size("col")
    slots = block_rows.shape[2]
    count = block_count[0, 0]
    mine = lax.axis_index("col")
    mine_row = lax.axis_index("row")
    per = node_dev // 128
    row_blocks = per * n_col
    col_blocks = per * n_row
    by_owner = n_row * n_col * node_dev * width * 2 <= 8 * 1024 * 1024

    brow = block_rows[0, 0]
    bcol = block_cols[0, 0]
    ids = jnp.arange(slots, dtype=jnp.int32)
    live = ids < count
    codes = edge_offsets[0, 0] * FIELD + (
        edge_weight[0, 0].astype(jnp.float32) * (1.0 / UNIT)
    ).astype(jnp.int32)
    codes = jnp.pad(codes, ((0, 8), (0, 0)))
    home = brow // per
    turns_plain = ((count + GROUP - 1) // GROUP).reshape(1)

    def tile_plan():
        wide = lax.all_gather(features, "row", axis=0, tiled=True)
        low = jnp.dot(wide, weight, preferred_element_type=jnp.float32).astype(jnp.bfloat16)
        panel = jnp.concatenate([low, wide], axis=1).reshape(col_blocks, 128, 2 * width)
        order = jnp.where(live, ids, slots)
        dst = jnp.where(live, (home ^ mine) * per + brow % per, 0)
        totals = run_tile(turns_plain, order, dst, bcol, codes, panel, row_blocks)
        own = scatter_sum(totals.reshape(n_col, node_dev, 2 * width), "col")
        pre = own[:, :width] + bias
        output = jnp.maximum(pre, 0.0).astype(jnp.bfloat16)
        grad = jnp.where(pre > 0, cotangent.astype(jnp.float32), 0.0)
        turned = jnp.swapaxes(grad.astype(jnp.bfloat16).reshape(per, 128, width), 1, 2)
        weight_sum = lax.dot_general(
            own[:, width:].astype(jnp.bfloat16),
            grad.astype(jnp.bfloat16),
            (((0,), (0,)), ((), ())),
            preferred_element_type=jnp.float32,
        )
        bias_sum = jnp.broadcast_to(jnp.sum(grad, axis=0), (8, width))
        return output, turned, jnp.concatenate([weight_sum, bias_sum], axis=0)

    source = piece_index(per, home ^ mine, brow % per)
    back_list, back_owner, back_turns = grouped(
        bcol, live, ids * FIELD + source, slots * FIELD, col_blocks
    )
    back_span = jnp.stack([jnp.zeros_like(back_turns), back_turns])
    state = {"dense": None}

    def build(held, start, end):
        span = jnp.stack([back_turns * start // 8, back_turns * end // 8])
        state["dense"] = run_build(
            span, back_list // FIELD, codes, held, state["dense"]
        )

    if by_owner:
        same = live[:, None] & (home[:, None] == home[None, :]) & (ids[:, None] < ids[None, :])
        rank = jnp.sum(same.astype(jnp.int32), axis=0)
        over = jnp.any(live & (rank >= ROOM)).astype(jnp.int32)
        fits = live & (rank < ROOM)
        label = 1 + (brow % per) * col_blocks + bcol
        labels = place(jnp.where(fits, home * ROOM + rank, -1), label, n_col * ROOM, 0)
        labels = jnp.concatenate(
            [labels.reshape(n_col, ROOM), jnp.full((n_col, 128 - ROOM), over)], axis=1
        )
        stride = ROOM + SPARE
        pos = jnp.where(fits, home * stride + rank, ROOM + SPARE - 1)
        packed = run_pack(turns_plain, pos, codes, labels)
        came = lax.all_to_all(
            packed.reshape(n_col, stride, 128), "col", split_axis=0, concat_axis=0, tiled=True
        )
        spread = jnp.max(came[:, ROOM, ROOM:], axis=0)[None]
        for bit in bits_of("row"):
            spread = spread + swap(spread, "row", bit)
        any_over = jnp.max(spread) > 0

        got = came[:, ROOM, :ROOM]
        sources = jnp.arange(n_col, dtype=jnp.int32)[:, None]
        places = jnp.arange(ROOM, dtype=jnp.int32)[None, :]
        row_here = ((got - 1) // col_blocks).reshape(-1)
        col_there = (got - 1) % col_blocks
        col_there = piece_index(
            per, sources ^ mine, col_there % per, (col_there // per) ^ mine_row, n_row
        )
        line = sources * stride + places
        listed, owner, turns = grouped(
            row_here, (got > 0).reshape(-1), (line * FIELD + col_there).reshape(-1), (ROOM + 1) * FIELD, per
        )
        span = jnp.stack([jnp.zeros_like(turns), turns])
        lists = [listed, owner, span]

        def prepare(step, held):
            nonlocal lists
            if step == 0:
                build(held, 0, 4)
            if step == 1:
                held, lists, state["dense"] = lax.optimization_barrier(
                    (held, lists, state["dense"])
                )
            return held

        pairs = gather_pieces(features.reshape(per, 128, width), prepare)
        listed, owner, span = lists
        here = run_build(span, listed // FIELD, came.reshape(n_col * stride, 128), [], None)
        last, here = lax.optimization_barrier(([pair[1] for pair in pairs], here))
        feat = []
        for pair in [[pair[0], x] for pair, x in zip(pairs, last)]:
            rows = [pair]
            for bit in bits_of("row"):
                rows = rows + [[swap(x, "row", bit) for x in pair] for pair in rows]
            feat += [x for pair in rows for x in pair]
        done = run_forward(
            span, listed % FIELD, owner, weight, bias[None], cotangent, here, feat
        )
        done = lax.cond(any_over, tile_plan, lambda: tuple(done))
    else:
        build([features], 0, 4)
        done = tile_plan()

    output, turned, total = done
    steps = bits_of("col")[::-1]

    def add_total():
        state["total"] = state["total"] + swap(state["total"], "col", steps.pop(0))

    def beside(step, held):
        held, state["total"], state["dense"] = lax.optimization_barrier(
            (held, state["total"], state["dense"])
        )
        if steps:
            add_total()
        build(held, 4 + 2 * step, 6 + 2 * step)
        return held

    state["total"] = split_rows(total)
    while len(steps) > 3:
        add_total()
    grad = [x for pair in gather_pieces(turned, beside) for x in pair]
    grad, state["total"] = lax.optimization_barrier((grad, state["total"]))
    while steps:
        add_total()
    acc = run_backward(
        back_span, back_list % FIELD, back_owner, grad, state["dense"], col_blocks
    )
    acc, total = lax.optimization_barrier((acc, state["total"]))
    total = join_rows(total)
    back = jnp.swapaxes(acc, 1, 2).reshape(col_blocks * 128, width)
    grad_proj = scatter_sum(
        jnp.stack(
            [
                lax.dynamic_slice_in_dim(back, (mine_row ^ k) * node_dev, node_dev, 0)
                for k in range(n_row)
            ]
        ),
        "row",
    ).astype(jnp.bfloat16)
    grad_features = lax.dot_general(
        grad_proj, weight, (((1,), (1,)), ((), ())), preferred_element_type=jnp.float32
    ).astype(jnp.bfloat16)
    scale = (node_dev * n_row * n_col) ** (-0.5)
    return (
        output,
        grad_features,
        total[: weight.shape[0]] * scale,
        total[weight.shape[0]] * scale,
    )


def solution(mesh):
    return jax.shard_map(
        shards,
        mesh=mesh,
        in_specs=(
            P(("row", "col"), None),
            P(),
            P(),
            P(("row", "col"), None),
            P("row", "col"),
            P("row", "col", None),
            P("row", "col", None),
            P("row", "col", None, None),
            P("row", "col", None, None),
        ),
        out_specs=(P(("row", "col"), None), P(("row", "col"), None), P(), P()),
        check_vma=False,
    )
```

profile of v0, /device:TPU:7, one launch (start us, length us, event | category | flops | bytes accessed | tf_op | source)
XLA Modules:
  0.0 120.3 jit_solution(8682863784814468650)
XLA Ops:
  0.6 3.4 %collective-permute-start.7 = (bf16[4,128,128]{2,1,0:T(8,128)(2,1)}, bf16[4,128,128]{2,1,0:T(8,128)(2,1)S(1)}, u32[]{:S(2)}, u32[]{:S(2)}) collective-permute-start(bf16[4,128,128]{2,1,0:T(8,128)(2,1)} %bitcast.157), channel_id=1, source_target_pairs={{0,12},{1,13},{2,14},{3,15},{4,8},{5,9},{6,10},{7,11},{8,4},{9,5},... | collective-permute-start | bytes 393224 | tf_op jit(solution)/shard_map/ppermute | solution.py:13
  6.8 1.1 add_bitcast_fusion
  9.8 1.6 %shard_map.120 = s32[1152,128]{1,0:T(8,128)} custom-call(s32[1]{0:T(128)} %bitcast.17.meta, s32[512]{0:T(512)S(1)} %get-tuple-element.223.pos, s32[520,128]{1,0:T(8,128)S(1)} %pad.13.codes, s32[16,128]{1,0:T(8,128)S(1)} %concatenate.24.labels), custom_call_target="tpu_custom_call" | custom-call | tf_op jit(solution)/shard_map/pallas_call | solution.py:317
  11.4 6.5 %all-to-all-start = ((s32[16,72,128]{2,1,0:T(8,128)}), s32[16,72,128]{2,1,0:T(8,128)S(1)}, u32[]{:S(2)}, u32[]{:S(2)}) async-start(s32[16,72,128]{2,1,0:T(8,128)} %bitcast.21), calls=%async_computation | async-start | bytes 1179648 | tf_op jit(solution)/shard_map/all_to_all | solution.py:493
  20.3 1.0 pad_maximum_fusion.2.refs_0_
  21.8 3.3 %shard_map.121.refs_1_ = bf16[576,128,128]{2,1,0:T(8,128)(2,1)} custom-call(s32[2]{0:T(128)S(1)} %pad_add_fusion.1.meta, s32[576]{0:T(1024)S(1)} %get-tuple-element.219.order, s32[520,128]{1,0:T(8,128)S(1)} %pad.13.codes, bf16[4,4,128,128]{3,2,1,0:T(8,128)(2,1)S(1)} %pad_maximum_fusion.2.refs_0_), custom_call_target="tpu_custom_call" | custom-call | flops 4831838208 | bytes 18874368 | tf_op jit(solution)/shard_map/pallas_call | solution.py:328
  25.1 5.8 %collective-permute-done.8 = bf16[4,2,128,128]{3,2,1,0:T(8,128)(2,1)S(1)} collective-permute-done((bf16[4,2,128,128]{3,2,1,0:T(8,128)(2,1)S(1)}, bf16[4,2,128,128]{3,2,1,0:T(8,128)(2,1)S(1)}, u32[]{:S(2)}, u32[]{:S(2)}) %collective-permute-start.8) | collective-permute-done | bytes 262176 | tf_op jit(solution)/shard_map/ppermute | solution.py:13
  36.4 3.2 %collective-permute-start.12 = (bf16[16,128,128]{2,1,0:T(8,128)(2,1)S(1)}, bf16[16,128,128]{2,1,0:T(8,128)(2,1)S(1)}, u32[]{:S(2)}, u32[]{:S(2)}) collective-permute-start(bf16[16,128,128]{2,1,0:T(8,128)(2,1)S(1)} %bitcast.138), channel_id=1, source_target_pairs={{0,16},{16,0},{1,17},{17,1},{2,18},{18,2},{3,19},{19,3},{4,20},{20... | collective-permute-start | bytes 1572872 | tf_op jit(solution)/shard_map/ppermute | solution.py:13
  39.6 8.5 %shard_map.122.dense = bf16[1056,128,128]{2,1,0:T(8,128)(2,1)} custom-call(s32[2]{0:T(128)S(1)} %pad_add_fusion.2.meta, s32[1056]{0:T(1024)S(1)} %get-tuple-element.216.order, s32[1152,128]{1,0:T(8,128)S(1)} %bitcast.134), custom_call_target="tpu_custom_call" | custom-call | flops 8858370048 | bytes 34603008 | tf_op jit(solution)/shard_map/pallas_call | solution.py:328
  48.1 1.7 %collective-permute-start.13 = (bf16[16,128,128]{2,1,0:T(8,128)(2,1)S(1)}, bf16[16,128,128]{2,1,0:T(8,128)(2,1)S(1)}, u32[]{:S(2)}, u32[]{:S(2)}) collective-permute-start(bf16[16,128,128]{2,1,0:T(8,128)(2,1)S(1)} %bitcast.143), channel_id=1, source_target_pairs={{0,16},{16,0},{1,17},{17,1},{2,18},{18,2},{3,19},{19,3},{4,20},{20... | collective-permute-start | bytes 1572872 | tf_op jit(solution)/shard_map/ppermute | solution.py:13
  50.5 1.6 %collective-permute-done.4 = s32[1,64]{1,0:T(1,128)S(1)} collective-permute-done((s32[1,64]{1,0:T(1,128)S(1)}, s32[1,64]{1,0:T(1,128)S(1)}, u32[]{:S(2)}, u32[]{:S(2)}) %collective-permute-start.4) | collective-permute-done | bytes 288 | tf_op jit(solution)/shard_map/ppermute | solution.py:13
  53.4 9.8 %shard_map.123 = (bf16[512,128]{1,0:T(8,128)(2,1)}, bf16[4,128,128]{2,1,0:T(8,128)(2,1)}, f32[136,128]{1,0:T(8,128)S(1)}) custom-call(s32[2]{0:T(128)S(1)} %pad_add_fusion.2.meta, s32[1056]{0:T(1024)S(1)} %get-tuple-element.217.col, s32[132]{0:T(256)S(1)} %broadcast_minimum_fusion.owner, bf16[128,128]{1,0:T(8,128)(2,1)S(1)} %copy-done.2, ...), custom_call_target="tpu_custom_call" | custom-call | flops 17716740096 | bytes 34603008 | tf_op jit(solution)/shard_map/pallas_call | solution.py:347
  63.9 2.9 %collective-permute-start.18 = (bf16[4,128,128]{2,1,0:T(8,128)(2,1)}, bf16[4,128,128]{2,1,0:T(8,128)(2,1)S(1)}, u32[]{:S(2)}, u32[]{:S(2)}) collective-permute-start(bf16[4,128,128]{2,1,0:T(8,128)(2,1)} %get-tuple-element.192), channel_id=1, source_target_pairs={{0,12},{1,13},{2,14},{3,15},{4,8},{5,9},{6,10},{7,11},{8,4},{9,5},... | collective-permute-start | bytes 393224 | tf_op jit(solution)/shard_map/ppermute | solution.py:13
  67.4 1.8 %collective-permute-start.20 = (f32[72,128]{1,0:T(8,128)S(1)}, f32[72,128]{1,0:T(8,128)S(1)}, u32[]{:S(2)}, u32[]{:S(2)}) collective-permute-start(f32[72,128]{1,0:T(8,128)S(1)} %fusion.27), channel_id=1, source_target_pairs={{0,8},{1,9},{2,10},{3,11},{4,12},{5,13},{6,14},{7,15},{8,0},{9,1},... | collective-permute-start | bytes 110600 | tf_op jit(solution)/shard_map/ppermute | solution.py:13
  69.3 11.6 %collective-permute-done.20 = f32[72,128]{1,0:T(8,128)S(1)} collective-permute-done((f32[72,128]{1,0:T(8,128)S(1)}, f32[72,128]{1,0:T(8,128)S(1)}, u32[]{:S(2)}, u32[]{:S(2)}) %collective-permute-start.20) | collective-permute-done | bytes 36896 | tf_op jit(solution)/shard_map/ppermute | solution.py:13
  82.6 1.8 %collective-permute-start.22 = (bf16[4,2,128,128]{3,2,1,0:T(8,128)(2,1)S(1)}, bf16[4,2,128,128]{3,2,1,0:T(8,128)(2,1)S(1)}, u32[]{:S(2)}, u32[]{:S(2)}) collective-permute-start(bf16[4,2,128,128]{3,2,1,0:T(8,128)(2,1)S(1)} %get-tuple-element.208), channel_id=1, source_target_pairs={{0,1},{1,0},{2,3},{3,2},{4,5},{5,4},{6,7},{7,6},{8,9},{9,8},{10,11... | collective-permute-start | bytes 786440 | tf_op jit(solution)/shard_map/ppermute | solution.py:13
  84.5 2.7 %shard_map.124.refs_2_ = bf16[576,128,128]{2,1,0:T(8,128)(2,1)} custom-call(s32[2]{0:T(128)S(1)} %pad_add_fusion.4.meta, s32[576]{0:T(1024)S(1)} %get-tuple-element.219.order, s32[520,128]{1,0:T(8,128)S(1)} %pad.13.codes, bf16[4,4,128,128]{3,2,1,0:T(8,128)(2,1)S(1)} %pad_maximum_fusion.5.refs_0_, ...), custom_call_target="tpu_custom_call", output_to_operand_aliasing={{}: (4, {})} | custom-call | flops 4831838208 | bytes 18874368 | tf_op jit(solution)/shard_map/pallas_call | solution.py:328
  87.6 1.5 %collective-permute-done.21 = bf16[4,2,128,128]{3,2,1,0:T(8,128)(2,1)S(1)} collective-permute-done((bf16[4,2,128,128]{3,2,1,0:T(8,128)(2,1)S(1)}, bf16[4,2,128,128]{3,2,1,0:T(8,128)(2,1)S(1)}, u32[]{:S(2)}, u32[]{:S(2)}) %collective-permute-start.21) | collective-permute-done | bytes 262176 | tf_op jit(solution)/shard_map/ppermute | solution.py:13
  90.0 1.6 %collective-permute-start.24 = (bf16[8,2,128,128]{3,2,1,0:T(8,128)(2,1)S(1)}, bf16[8,2,128,128]{3,2,1,0:T(8,128)(2,1)S(1)}, u32[]{:S(2)}, u32[]{:S(2)}) collective-permute-start(bf16[8,2,128,128]{3,2,1,0:T(8,128)(2,1)S(1)} %pad_maximum_fusion.6.refs_0_), channel_id=1, source_target_pairs={{0,1},{1,0},{2,3},{3,2},{4,5},{5,4},{6,7},{7,6},{8,9},{9,8},{10,11... | collective-permute-start | bytes 1572872 | tf_op jit(solution)/shard_map/ppermute | solution.py:13
  92.1 1.1 collective-permute-start.26
  93.2 3.3 %shard_map.125.dense = bf16[576,128,128]{2,1,0:T(8,128)(2,1)} custom-call(s32[2]{0:T(128)S(1)} %pad_add_fusion.3.meta, s32[576]{0:T(1024)S(1)} %get-tuple-element.219.order, s32[520,128]{1,0:T(8,128)S(1)} %pad.13.codes, bf16[8,2,128,128]{3,2,1,0:T(8,128)(2,1)S(1)} %pad_maximum_fusion.6.refs_0_, ...), custom_call_target="tpu_custom_call", output_to_operand_aliasing={{}: (5, {})} | custom-call | flops 4831838208 | bytes 18874368 | tf_op jit(solution)/shard_map/pallas_call | solution.py:328
  96.5 7.4 %collective-permute-done.26 = f32[72,128]{1,0:T(8,128)S(1)} collective-permute-done((f32[72,128]{1,0:T(8,128)S(1)}, f32[72,128]{1,0:T(8,128)S(1)}, u32[]{:S(2)}, u32[]{:S(2)}) %collective-permute-start.26) | collective-permute-done | bytes 36896 | tf_op jit(solution)/shard_map/ppermute | solution.py:13
  104.2 4.2 %shard_map.126 = f32[8,128,128]{2,1,0:T(8,128)S(1)} custom-call(s32[2]{0:T(128)S(1)} %pad_add_fusion.meta, s32[576]{0:T(1024)S(1)} %get-tuple-element.218.src, s32[72]{0:T(128)S(1)} %broadcast_minimum_fusion.1.owner, bf16[576,128,128]{2,1,0:T(8,128)(2,1)} %shard_map.125.dense, bf16[16,128,128]{2,1,0:T(8,128)(2,1)S(1)} %bitcast.135, ...), custom_call_target="tpu_custom_call" | custom-call | flops 9663676416 | bytes 18874368 | tf_op jit(solution)/shard_map/pallas_call | solution.py:372
  108.6 8.8 %collective-permute-start.29 = (f32[72,128]{1,0:T(8,128)S(1)}, f32[72,128]{1,0:T(8,128)S(1)}, u32[]{:S(2)}, u32[]{:S(2)}) collective-permute-start(f32[72,128]{1,0:T(8,128)S(1)} %add.695), channel_id=1, source_target_pairs={{0,16},{16,0},{1,17},{17,1},{2,18},{18,2},{3,19},{19,3},{4,20},{20... | collective-permute-start | bytes 110600 | tf_op jit(solution)/shard_map/ppermute | solution.py:13
  (127 shorter events, 19.8 us)
Async XLA Ops:
  0.6 19.6 %collective-permute-start.7 = (bf16[4,128,128]{2,1,0:T(8,128)(2,1)}, bf16[4,128,128]{2,1,0:T(8,128)(2,1)S(1)}, u32[]{:S(2)}, u32[]{:S(2)}) collective-permute-start(bf16[4,128,128]{2,1,0:T(8,128)(2,1)} %bitcast.157), channel_id=1, source_target_pairs={{0,12},{1,13},{2,14},{3,15},{4,8},{5,9},{6,10},{7,11},{8,4},{9,5},... | collective-permute-start | bytes 393224 | tf_op jit(solution)/shard_map/ppermute | solution.py:13
  4.0 16.2 %collective-permute-start.6 = (bf16[4,128,128]{2,1,0:T(8,128)(2,1)}, bf16[4,128,128]{2,1,0:T(8,128)(2,1)S(1)}, u32[]{:S(2)}, u32[]{:S(2)}) collective-permute-start(bf16[4,128,128]{2,1,0:T(8,128)(2,1)} %bitcast.158), channel_id=1, source_target_pairs={{0,4},{1,5},{2,6},{3,7},{4,0},{5,1},{6,2},{7,3},{8,12},{9,13},{10,... | collective-permute-start | bytes 393224 | tf_op jit(solution)/shard_map/ppermute | solution.py:13
  4.0 16.2 %collective-permute-start.5 = (bf16[4,128,128]{2,1,0:T(8,128)(2,1)}, bf16[4,128,128]{2,1,0:T(8,128)(2,1)S(1)}, u32[]{:S(2)}, u32[]{:S(2)}) collective-permute-start(bf16[4,128,128]{2,1,0:T(8,128)(2,1)} %bitcast.159), channel_id=1, source_target_pairs={{0,8},{1,9},{2,10},{3,11},{4,12},{5,13},{6,14},{7,15},{8,0},{9,1},... | collective-permute-start | bytes 393224 | tf_op jit(solution)/shard_map/ppermute | solution.py:13
  11.4 20.4 %all-to-all-start = ((s32[16,72,128]{2,1,0:T(8,128)}), s32[16,72,128]{2,1,0:T(8,128)S(1)}, u32[]{:S(2)}, u32[]{:S(2)}) async-start(s32[16,72,128]{2,1,0:T(8,128)} %bitcast.21), calls=%async_computation | async-start | bytes 1179648 | tf_op jit(solution)/shard_map/all_to_all | solution.py:493
  21.3 9.6 %collective-permute-start.8 = (bf16[4,2,128,128]{3,2,1,0:T(8,128)(2,1)S(1)}, bf16[4,2,128,128]{3,2,1,0:T(8,128)(2,1)S(1)}, u32[]{:S(2)}, u32[]{:S(2)}) collective-permute-start(bf16[4,2,128,128]{3,2,1,0:T(8,128)(2,1)S(1)} %get-tuple-element.211), channel_id=1, source_target_pairs={{0,2},{1,3},{2,0},{3,1},{4,6},{5,7},{6,4},{7,5},{8,10},{9,11},{10,... | collective-permute-start | bytes 786440 | tf_op jit(solution)/shard_map/ppermute | solution.py:13
  21.6 10.1 %collective-permute-start.9 = (bf16[4,2,128,128]{3,2,1,0:T(8,128)(2,1)S(1)}, bf16[4,2,128,128]{3,2,1,0:T(8,128)(2,1)S(1)}, u32[]{:S(2)}, u32[]{:S(2)}) collective-permute-start(bf16[4,2,128,128]{3,2,1,0:T(8,128)(2,1)S(1)} %get-tuple-element.210), channel_id=1, source_target_pairs={{0,1},{1,0},{2,3},{3,2},{4,5},{5,4},{6,7},{7,6},{8,9},{9,8},{10,11... | collective-permute-start | bytes 786440 | tf_op jit(solution)/shard_map/ppermute | solution.py:13
  34.9 13.2 %collective-permute-start.10 = (bf16[8,2,128,128]{3,2,1,0:T(8,128)(2,1)S(1)}, bf16[8,2,128,128]{3,2,1,0:T(8,128)(2,1)S(1)}, u32[]{:S(2)}, u32[]{:S(2)}) collective-permute-start(bf16[8,2,128,128]{3,2,1,0:T(8,128)(2,1)S(1)} %pad_maximum_fusion.3), channel_id=1, source_target_pairs={{0,1},{1,0},{2,3},{3,2},{4,5},{5,4},{6,7},{7,6},{8,9},{9,8},{10,11... | collective-permute-start | bytes 1572872 | tf_op jit(solution)/shard_map/ppermute | solution.py:13
  35.5 12.6 %collective-permute-start.11 = (bf16[8,2,128,128]{3,2,1,0:T(8,128)(2,1)S(1)}, bf16[8,2,128,128]{3,2,1,0:T(8,128)(2,1)S(1)}, u32[]{:S(2)}, u32[]{:S(2)}) collective-permute-start(bf16[8,2,128,128]{3,2,1,0:T(8,128)(2,1)S(1)} %pad_maximum_fusion.4), channel_id=1, source_target_pairs={{0,2},{1,3},{2,0},{3,1},{4,6},{5,7},{6,4},{7,5},{8,10},{9,11},{10,... | collective-permute-start | bytes 1572872 | tf_op jit(solution)/shard_map/ppermute | solution.py:13
  36.4 16.9 %collective-permute-start.12 = (bf16[16,128,128]{2,1,0:T(8,128)(2,1)S(1)}, bf16[16,128,128]{2,1,0:T(8,128)(2,1)S(1)}, u32[]{:S(2)}, u32[]{:S(2)}) collective-permute-start(bf16[16,128,128]{2,1,0:T(8,128)(2,1)S(1)} %bitcast.138), channel_id=1, source_target_pairs={{0,16},{16,0},{1,17},{17,1},{2,18},{18,2},{3,19},{19,3},{4,20},{20... | collective-permute-start | bytes 1572872 | tf_op jit(solution)/shard_map/ppermute | solution.py:13
  39.6 13.8 %collective-permute-start.14 = (bf16[16,128,128]{2,1,0:T(8,128)(2,1)S(1)}, bf16[16,128,128]{2,1,0:T(8,128)(2,1)}, u32[]{:S(2)}, u32[]{:S(2)}) collective-permute-start(bf16[16,128,128]{2,1,0:T(8,128)(2,1)S(1)} %bitcast.140), channel_id=1, source_target_pairs={{0,16},{16,0},{1,17},{17,1},{2,18},{18,2},{3,19},{19,3},{4,20},{20... | collective-permute-start | bytes 1572872 | tf_op jit(solution)/shard_map/ppermute | solution.py:13
  48.1 5.2 %collective-permute-start.13 = (bf16[16,128,128]{2,1,0:T(8,128)(2,1)S(1)}, bf16[16,128,128]{2,1,0:T(8,128)(2,1)S(1)}, u32[]{:S(2)}, u32[]{:S(2)}) collective-permute-start(bf16[16,128,128]{2,1,0:T(8,128)(2,1)S(1)} %bitcast.143), channel_id=1, source_target_pairs={{0,16},{16,0},{1,17},{17,1},{2,18},{18,2},{3,19},{19,3},{4,20},{20... | collective-permute-start | bytes 1572872 | tf_op jit(solution)/shard_map/ppermute | solution.py:13
  49.8 3.6 %collective-permute-start.15 = (bf16[16,128,128]{2,1,0:T(8,128)(2,1)S(1)}, bf16[16,128,128]{2,1,0:T(8,128)(2,1)}, u32[]{:S(2)}, u32[]{:S(2)}) collective-permute-start(bf16[16,128,128]{2,1,0:T(8,128)(2,1)S(1)} %bitcast.145), channel_id=1, source_target_pairs={{0,16},{16,0},{1,17},{17,1},{2,18},{18,2},{3,19},{19,3},{4,20},{20... | collective-permute-start | bytes 1572872 | tf_op jit(solution)/shard_map/ppermute | solution.py:13
  63.4 4.1 %collective-permute-start.19 = (f32[1,72,128]{2,1,0:T(8,128)S(1)}, f32[1,72,128]{2,1,0:T(8,128)S(1)}, u32[]{:S(2)}, u32[]{:S(2)}) collective-permute-start(f32[1,72,128]{2,1,0:T(8,128)S(1)} %slice_bitcast_fusion.10), channel_id=1, source_target_pairs={{0,16},{16,0},{1,17},{17,1},{2,18},{18,2},{3,19},{19,3},{4,20},{20... | collective-permute-start | bytes 110600 | tf_op jit(solution)/shard_map/ppermute | solution.py:13
  63.9 17.0 %collective-permute-start.18 = (bf16[4,128,128]{2,1,0:T(8,128)(2,1)}, bf16[4,128,128]{2,1,0:T(8,128)(2,1)S(1)}, u32[]{:S(2)}, u32[]{:S(2)}) collective-permute-start(bf16[4,128,128]{2,1,0:T(8,128)(2,1)} %get-tuple-element.192), channel_id=1, source_target_pairs={{0,12},{1,13},{2,14},{3,15},{4,8},{5,9},{6,10},{7,11},{8,4},{9,5},... | collective-permute-start | bytes 393224 | tf_op jit(solution)/shard_map/ppermute | solution.py:13
  66.7 14.1 %collective-permute-start.17 = (bf16[4,128,128]{2,1,0:T(8,128)(2,1)}, bf16[4,128,128]{2,1,0:T(8,128)(2,1)S(1)}, u32[]{:S(2)}, u32[]{:S(2)}) collective-permute-start(bf16[4,128,128]{2,1,0:T(8,128)(2,1)} %get-tuple-element.192), channel_id=1, source_target_pairs={{0,4},{1,5},{2,6},{3,7},{4,0},{5,1},{6,2},{7,3},{8,12},{9,13},{10,... | collective-permute-start | bytes 393224 | tf_op jit(solution)/shard_map/ppermute | solution.py:13
  66.8 14.1 %collective-permute-start.16 = (bf16[4,128,128]{2,1,0:T(8,128)(2,1)}, bf16[4,128,128]{2,1,0:T(8,128)(2,1)S(1)}, u32[]{:S(2)}, u32[]{:S(2)}) collective-permute-start(bf16[4,128,128]{2,1,0:T(8,128)(2,1)} %get-tuple-element.192), channel_id=1, source_target_pairs={{0,8},{1,9},{2,10},{3,11},{4,12},{5,13},{6,14},{7,15},{8,0},{9,1},... | collective-permute-start | bytes 393224 | tf_op jit(solution)/shard_map/ppermute | solution.py:13
  67.4 13.4 %collective-permute-start.20 = (f32[72,128]{1,0:T(8,128)S(1)}, f32[72,128]{1,0:T(8,128)S(1)}, u32[]{:S(2)}, u32[]{:S(2)}) collective-permute-start(f32[72,128]{1,0:T(8,128)S(1)} %fusion.27), channel_id=1, source_target_pairs={{0,8},{1,9},{2,10},{3,11},{4,12},{5,13},{6,14},{7,15},{8,0},{9,1},... | collective-permute-start | bytes 110600 | tf_op jit(solution)/shard_map/ppermute | solution.py:13
  81.9 7.2 %collective-permute-start.21 = (bf16[4,2,128,128]{3,2,1,0:T(8,128)(2,1)S(1)}, bf16[4,2,128,128]{3,2,1,0:T(8,128)(2,1)S(1)}, u32[]{:S(2)}, u32[]{:S(2)}) collective-permute-start(bf16[4,2,128,128]{3,2,1,0:T(8,128)(2,1)S(1)} %get-tuple-element.209), channel_id=1, source_target_pairs={{0,2},{1,3},{2,0},{3,1},{4,6},{5,7},{6,4},{7,5},{8,10},{9,11},{10,... | collective-permute-start | bytes 786440 | tf_op jit(solution)/shard_map/ppermute | solution.py:13
  82.6 7.3 %collective-permute-start.22 = (bf16[4,2,128,128]{3,2,1,0:T(8,128)(2,1)S(1)}, bf16[4,2,128,128]{3,2,1,0:T(8,128)(2,1)S(1)}, u32[]{:S(2)}, u32[]{:S(2)}) collective-permute-start(bf16[4,2,128,128]{3,2,1,0:T(8,128)(2,1)S(1)} %get-tuple-element.208), channel_id=1, source_target_pairs={{0,1},{1,0},{2,3},{3,2},{4,5},{5,4},{6,7},{7,6},{8,9},{9,8},{10,11... | collective-permute-start | bytes 786440 | tf_op jit(solution)/shard_map/ppermute | solution.py:13
  90.0 13.9 %collective-permute-start.24 = (bf16[8,2,128,128]{3,2,1,0:T(8,128)(2,1)S(1)}, bf16[8,2,128,128]{3,2,1,0:T(8,128)(2,1)S(1)}, u32[]{:S(2)}, u32[]{:S(2)}) collective-permute-start(bf16[8,2,128,128]{3,2,1,0:T(8,128)(2,1)S(1)} %pad_maximum_fusion.6.refs_0_), channel_id=1, source_target_pairs={{0,1},{1,0},{2,3},{3,2},{4,5},{5,4},{6,7},{7,6},{8,9},{9,8},{10,11... | collective-permute-start | bytes 1572872 | tf_op jit(solution)/shard_map/ppermute | solution.py:13
  91.7 12.3 %collective-permute-start.25 = (bf16[8,2,128,128]{3,2,1,0:T(8,128)(2,1)S(1)}, bf16[8,2,128,128]{3,2,1,0:T(8,128)(2,1)S(1)}, u32[]{:S(2)}, u32[]{:S(2)}) collective-permute-start(bf16[8,2,128,128]{3,2,1,0:T(8,128)(2,1)S(1)} %pad_maximum_fusion.7.refs_1_), channel_id=1, source_target_pairs={{0,2},{1,3},{2,0},{3,1},{4,6},{5,7},{6,4},{7,5},{8,10},{9,11},{10,... | collective-permute-start | bytes 1572872 | tf_op jit(solution)/shard_map/ppermute | solution.py:13
  92.1 11.8 %collective-permute-start.26 = (f32[72,128]{1,0:T(8,128)S(1)}, f32[72,128]{1,0:T(8,128)S(1)}, u32[]{:S(2)}, u32[]{:S(2)}) collective-permute-start(f32[72,128]{1,0:T(8,128)S(1)} %add.693), channel_id=1, source_target_pairs={{0,2},{1,3},{2,0},{3,1},{4,6},{5,7},{6,4},{7,5},{8,10},{9,11},{10,... | collective-permute-start | bytes 110600 | tf_op jit(solution)/shard_map/ppermute | solution.py:13
  104.0 4.5 %collective-permute-start.27 = (f32[72,128]{1,0:T(8,128)S(1)}, f32[72,128]{1,0:T(8,128)S(1)}, u32[]{:S(2)}, u32[]{:S(2)}) collective-permute-start(f32[72,128]{1,0:T(8,128)S(1)} %add.694), channel_id=1, source_target_pairs={{0,1},{1,0},{2,3},{3,2},{4,5},{5,4},{6,7},{7,6},{8,9},{9,8},{10,11... | collective-permute-start | bytes 110600 | tf_op jit(solution)/shard_map/ppermute | solution.py:13
  108.6 9.6 %collective-permute-start.29 = (f32[72,128]{1,0:T(8,128)S(1)}, f32[72,128]{1,0:T(8,128)S(1)}, u32[]{:S(2)}, u32[]{:S(2)}) collective-permute-start(f32[72,128]{1,0:T(8,128)S(1)} %add.695), channel_id=1, source_target_pairs={{0,16},{16,0},{1,17},{17,1},{2,18},{18,2},{3,19},{19,3},{4,20},{20... | collective-permute-start | bytes 110600 | tf_op jit(solution)/shard_map/ppermute | solution.py:13
  (7 other events, 51.0 us)
where the time goes:
time: 121 us; the launch traced here: 120 us
  starting transfers between devices  38.1 us (31%)
  Pallas kernels  33.5 us (28%)
  waiting for transfers between devices  30.6 us (25%)
  other arithmetic  11.6 us (10%)
  between operations  4.41 us (4%)
  local copies, waits for them, and re-layouts  1.27 us (1%)
    ppermute x26, starting transfers between devices, swap(): return lax.ppermute(x, axis, [(i, i ^ bit) for i in range(n)])  31.7 us
    ppermute x26, waiting for transfers between devices, swap(): return lax.ppermute(x, axis, [(i, i ^ bit) for i in range(n)])  30.6 us
    pallas_call x4, Pallas kernels, run_build(): pl.pallas_call(build_kernel, out_shape=jax.ShapeDtypeStruct((order.shape[...  17.8 us
    pallas_call x1, Pallas kernels, run_forward(): pl.pallas_call(functools.partial(forward_kernel, n), out_shape=(jax.Shape...  9.82 us
    all_to_all x1, starting transfers between devices, shards(): lax.all_to_all(packed.reshape(n_col, stride, 128), 'col', split_axis=0, c...  6.47 us
    pallas_call x1, Pallas kernels, run_backward(): pl.pallas_call(functools.partial(backward_kernel, n), out_shape=jax.Shape...  4.22 us
  transfers between devices with their start and end apart: 27, of which 9 were waited for; matrix products, arithmetic and copies ran while one was open for 8% of the time, Pallas kernels for 20%

commit v1 on v0

--- a/solution.py
+++ b/solution.py
@@ -205,7 +205,7 @@
             into[owner[i * groups + g + k]] += added[k]
 
 
-def forward_kernel(n, meta, col, owner, weight, bias, cotangent, dense, *refs):
+def forward_kernel(n, scale, meta, col, owner, weight, bias, cotangent, dense, *refs):
     pieces, refs = refs[:n], refs[n:]
     output, turned, local, totals, feat, proj, dbuf, piece_sems, sems = refs
     copies = fetch(pieces, feat, piece_sems)
@@ -252,8 +252,8 @@
             preferred_element_type=jnp.float32,
         )
         bias_sum += jnp.sum(grad, axis=0, keepdims=True)
-    local[pl.ds(0, width), :] = weight_sum
-    local[pl.ds(width, 8), :] = jnp.broadcast_to(bias_sum, (8, width))
+    local[pl.ds(0, width), :] = weight_sum * scale
+    local[pl.ds(width, 8), :] = jnp.broadcast_to(bias_sum * scale, (8, width))
 
 
 def tile_kernel(meta, order, dst, col, codes, panel, totals):
@@ -340,12 +340,12 @@
     )(meta, order, codes, *others)
 
 
-def run_forward(meta, col, owner, weight, bias, cotangent, dense, feat):
+def run_forward(scale, meta, col, owner, weight, bias, cotangent, dense, feat):
     n = len(feat)
     size, _, width = feat[0].shape
     row_blocks = cotangent.shape[0] // 128
     return pl.pallas_call(
-        functools.partial(forward_kernel, n),
+        functools.partial(forward_kernel, n, scale),
         out_shape=(
             jax.ShapeDtypeStruct(cotangent.shape, jnp.bfloat16),
             jax.ShapeDtypeStruct((row_blocks, width, 128), jnp.bfloat16),
@@ -430,6 +430,7 @@
     per = node_dev // 128
     row_blocks = per * n_col
     col_blocks = per * n_row
+    scale = (node_dev * n_row * n_col) ** (-0.5)
     by_owner = n_row * n_col * node_dev * width * 2 <= 8 * 1024 * 1024
 
     brow = block_rows[0, 0]
@@ -462,7 +463,7 @@
             preferred_element_type=jnp.float32,
         )
         bias_sum = jnp.broadcast_to(jnp.sum(grad, axis=0), (8, width))
-        return output, turned, jnp.concatenate([weight_sum, bias_sum], axis=0)
+        return output, turned, jnp.concatenate([weight_sum, bias_sum], axis=0) * scale
 
     source = piece_index(per, home ^ mine, brow % per)
     back_list, back_owner, back_turns = grouped(
@@ -472,7 +473,7 @@
     state = {"dense": None}
 
     def build(held, start, end):
-        span = jnp.stack([back_turns * start // 8, back_turns * end // 8])
+        span = jnp.stack([back_turns * start // 4, back_turns * end // 4])
         state["dense"] = run_build(
             span, back_list // FIELD, codes, held, state["dense"]
         )
@@ -496,7 +497,7 @@
         spread = jnp.max(came[:, ROOM, ROOM:], axis=0)[None]
         for bit in bits_of("row"):
             spread = spread + swap(spread, "row", bit)
-        any_over = jnp.max(spread) > 0
+        any_over = jnp.max(spread, axis=1)
 
         got = came[:, ROOM, :ROOM]
         sources = jnp.arange(n_col, dtype=jnp.int32)[:, None]
@@ -511,21 +512,20 @@
             row_here, (got > 0).reshape(-1), (line * FIELD + col_there).reshape(-1), (ROOM + 1) * FIELD, per
         )
         span = jnp.stack([jnp.zeros_like(turns), turns])
-        lists = [listed, owner, span]
+        lists = [listed, owner, span, any_over]
+        lines = came.reshape(n_col * stride, 128)
+        here = None
 
         def prepare(step, held):
-            nonlocal lists
-            if step == 0:
-                build(held, 0, 4)
+            nonlocal lists, here
             if step == 1:
-                held, lists, state["dense"] = lax.optimization_barrier(
-                    (held, lists, state["dense"])
-                )
+                held, lists, here = lax.optimization_barrier((held, lists, here))
+            half = jnp.stack([turns * step // 2, turns * (step + 1) // 2])
+            here = run_build(half, listed // FIELD, lines, held + lists[3:], here)
             return held
 
         pairs = gather_pieces(features.reshape(per, 128, width), prepare)
-        listed, owner, span = lists
-        here = run_build(span, listed // FIELD, came.reshape(n_col * stride, 128), [], None)
+        listed, owner, span, any_over = lists
         last, here = lax.optimization_barrier(([pair[1] for pair in pairs], here))
         feat = []
         for pair in [[pair[0], x] for pair, x in zip(pairs, last)]:
@@ -534,11 +534,10 @@
                 rows = rows + [[swap(x, "row", bit) for x in pair] for pair in rows]
             feat += [x for pair in rows for x in pair]
         done = run_forward(
-            span, listed % FIELD, owner, weight, bias[None], cotangent, here, feat
-        )
-        done = lax.cond(any_over, tile_plan, lambda: tuple(done))
+            scale, span, listed % FIELD, owner, weight, bias[None], cotangent, here, feat
+        )
+        done = lax.cond(any_over[0] > 0, tile_plan, lambda: tuple(done))
     else:
-        build([features], 0, 4)
         done = tile_plan()
 
     output, turned, total = done
@@ -553,12 +552,13 @@
         )
         if steps:
             add_total()
-        build(held, 4 + 2 * step, 6 + 2 * step)
+        build(held, 2 + step, 3 + step)
         return held
 
     state["total"] = split_rows(total)
     while len(steps) > 3:
         add_total()
+    build([turned], 0, 2)
     grad = [x for pair in gather_pieces(turned, beside) for x in pair]
     grad, state["total"] = lax.optimization_barrier((grad, state["total"]))
     while steps:
@@ -581,12 +581,11 @@
     grad_features = lax.dot_general(
         grad_proj, weight, (((1,), (1,)), ((), ())), preferred_element_type=jnp.float32
     ).astype(jnp.bfloat16)
-    scale = (node_dev * n_row * n_col) ** (-0.5)
     return (
         output,
         grad_features,
-        total[: weight.shape[0]] * scale,
-        total[weight.shape[0]] * scale,
+        total[: weight.shape[0]],
+        total[weight.shape[0]],
     )
 
 

time: 121 us -> 127 us (1.050)
  the two profiles are of different devices: /device:TPU:7 before, /device:TPU:0 now
where the time goes in v1:
time: 127 us; the launch traced here: 125 us
  Pallas kernels  45.1 us (36%)
  starting transfers between devices  33.1 us (26%)
  waiting for transfers between devices  29.4 us (23%)
  other arithmetic  9.81 us (8%)
  between operations  4.47 us (4%)
  local copies, waits for them, and re-layouts  1.8 us (1%)
    ppermute x26, waiting for transfers between devices, swap(): return lax.ppermute(x, axis, [(i, i ^ bit) for i in range(n)])  27.9 us
    pallas_call x5, Pallas kernels, run_build(): pl.pallas_call(build_kernel, out_shape=jax.ShapeDtypeStruct((order.shape[...  26.9 us
    ppermute x26, starting transfers between devices, swap(): return lax.ppermute(x, axis, [(i, i ^ bit) for i in range(n)])  26 us
    pallas_call x1, Pallas kernels, run_forward(): pl.pallas_call(functools.partial(forward_kernel, n, scale), out_shape=(ja...  10.6 us
    all_to_all x1, starting transfers between devices, shards(): lax.all_to_all(packed.reshape(n_col, stride, 128), 'col', split_axis=0, c...  7.08 us
    pallas_call x1, Pallas kernels, run_backward(): pl.pallas_call(functools.partial(backward_kernel, n), out_shape=jax.Shape...  5.93 us
  transfers between devices with their start and end apart: 27, of which 13 were waited for; matrix products, arithmetic and copies ran while one was open for 7% of the time, Pallas kernels for 22%

profile of v1, /device:TPU:0, one launch (start us, length us, event | category | flops | bytes accessed | tf_op | source)
XLA Modules:
  0.0 124.5 jit_solution(10382314540952389140)
XLA Ops:
  0.6 4.1 %collective-permute-start.4 = (bf16[4,128,128]{2,1,0:T(8,128)(2,1)}, bf16[4,128,128]{2,1,0:T(8,128)(2,1)S(1)}, u32[]{:S(2)}, u32[]{:S(2)}) collective-permute-start(bf16[4,128,128]{2,1,0:T(8,128)(2,1)} %bitcast.163), channel_id=1, source_target_pairs={{0,8},{1,9},{2,10},{3,11},{4,12},{5,13},{6,14},{7,15},{8,0},{9,1},... | collective-permute-start | bytes 393224 | tf_op jit(solution)/shard_map/ppermute | solution.py:13
  4.7 1.6 %collective-permute-start.5 = (bf16[4,128,128]{2,1,0:T(8,128)(2,1)}, bf16[4,128,128]{2,1,0:T(8,128)(2,1)S(1)}, u32[]{:S(2)}, u32[]{:S(2)}) collective-permute-start(bf16[4,128,128]{2,1,0:T(8,128)(2,1)} %bitcast.164), channel_id=1, source_target_pairs={{0,4},{1,5},{2,6},{3,7},{4,0},{5,1},{6,2},{7,3},{8,12},{9,13},{10,... | collective-permute-start | bytes 393224 | tf_op jit(solution)/shard_map/ppermute | solution.py:13
  11.8 1.7 %shard_map.120 = s32[1152,128]{1,0:T(8,128)} custom-call(s32[1]{0:T(128)} %bitcast.22.meta, s32[512]{0:T(512)S(1)} %get-tuple-element.225.pos, s32[520,128]{1,0:T(8,128)S(1)} %pad.13.codes, s32[16,128]{1,0:T(8,128)S(1)} %concatenate.26.labels), custom_call_target="tpu_custom_call" | custom-call | tf_op jit(solution)/shard_map/pallas_call | solution.py:317
  13.5 7.1 %all-to-all-start = ((s32[16,72,128]{2,1,0:T(8,128)}), s32[16,72,128]{2,1,0:T(8,128)S(1)}, u32[]{:S(2)}, u32[]{:S(2)}) async-start(s32[16,72,128]{2,1,0:T(8,128)} %bitcast.26), calls=%async_computation | async-start | bytes 1179648 | tf_op jit(solution)/shard_map/all_to_all | solution.py:494
  22.7 2.0 %collective-permute-start.8 = (bf16[4,2,128,128]{3,2,1,0:T(8,128)(2,1)S(1)}, bf16[4,2,128,128]{3,2,1,0:T(8,128)(2,1)S(1)}, u32[]{:S(2)}, u32[]{:S(2)}) collective-permute-start(bf16[4,2,128,128]{3,2,1,0:T(8,128)(2,1)S(1)} %get-tuple-element.212), channel_id=1, source_target_pairs={{0,1},{1,0},{2,3},{3,2},{4,5},{5,4},{6,7},{7,6},{8,9},{9,8},{10,11... | collective-permute-start | bytes 786440 | tf_op jit(solution)/shard_map/ppermute | solution.py:13
  25.4 1.5 %collective-permute-start.7 = (bf16[4,2,128,128]{3,2,1,0:T(8,128)(2,1)S(1)}, bf16[4,2,128,128]{3,2,1,0:T(8,128)(2,1)S(1)}, u32[]{:S(2)}, u32[]{:S(2)}) collective-permute-start(bf16[4,2,128,128]{3,2,1,0:T(8,128)(2,1)S(1)} %get-tuple-element.213), channel_id=1, source_target_pairs={{0,2},{1,3},{2,0},{3,1},{4,6},{5,7},{6,4},{7,5},{8,10},{9,11},{10,... | collective-permute-start | bytes 786440 | tf_op jit(solution)/shard_map/ppermute | solution.py:13
  27.1 7.1 %collective-permute-done.8 = bf16[4,2,128,128]{3,2,1,0:T(8,128)(2,1)S(1)} collective-permute-done((bf16[4,2,128,128]{3,2,1,0:T(8,128)(2,1)S(1)}, bf16[4,2,128,128]{3,2,1,0:T(8,128)(2,1)S(1)}, u32[]{:S(2)}, u32[]{:S(2)}) %collective-permute-start.8) | collective-permute-done | bytes 262176 | tf_op jit(solution)/shard_map/ppermute | solution.py:13
  34.6 1.5 %all-to-all-done = s32[16,72,128]{2,1,0:T(8,128)S(1)} async-done(((s32[16,72,128]{2,1,0:T(8,128)}), s32[16,72,128]{2,1,0:T(8,128)S(1)}, u32[]{:S(2)}, u32[]{:S(2)}) %all-to-all-start) | async-done | bytes 589856 | tf_op jit(solution)/shard_map/all_to_all | solution.py:494
  41.0 6.6 %shard_map.121.refs_3_ = bf16[1056,128,128]{2,1,0:T(8,128)(2,1)} custom-call(s32[2]{0:T(128)S(1)} %pad_add_fusion.2.meta, s32[1056]{0:T(1024)S(1)} %get-tuple-element.218.order, s32[1152,128]{1,0:T(8,128)S(1)} %bitcast.138, bf16[4,4,128,128]{3,2,1,0:T(8,128)(2,1)S(1)} %pad_maximum_fusion.1.refs_0_, s32[1]{0:T(128)} %bitcast.29.refs_1_.refs_2_), custom_call_target="tpu_custom_call" | custom-call | flops 8858370048 | bytes 34603008 | tf_op jit(solution)/shard_map/pallas_call | solution.py:328
  48.2 1.9 %collective-permute-start.11 = (bf16[8,2,128,128]{3,2,1,0:T(8,128)(2,1)S(1)}, bf16[8,2,128,128]{3,2,1,0:T(8,128)(2,1)S(1)}, u32[]{:S(2)}, u32[]{:S(2)}) collective-permute-start(bf16[8,2,128,128]{3,2,1,0:T(8,128)(2,1)S(1)} %pad_maximum_fusion.3.refs_1_), channel_id=1, source_target_pairs={{0,2},{1,3},{2,0},{3,1},{4,6},{5,7},{6,4},{7,5},{8,10},{9,11},{10,... | collective-permute-start | bytes 1572872 | tf_op jit(solution)/shard_map/ppermute | solution.py:13
  50.7 7.4 %shard_map.122.dense = bf16[1056,128,128]{2,1,0:T(8,128)(2,1)} custom-call(s32[2]{0:T(128)S(1)} %pad_add_fusion.4.meta, s32[1056]{0:T(1024)S(1)} %get-tuple-element.218.order, s32[1152,128]{1,0:T(8,128)S(1)} %bitcast.139, bf16[8,2,128,128]{3,2,1,0:T(8,128)(2,1)S(1)} %pad_maximum_fusion.2.refs_0_, ...), custom_call_target="tpu_custom_call", output_to_operand_aliasing={{}: (6, {})} | custom-call | flops 8858370048 | bytes 34603008 | tf_op jit(solution)/shard_map/pallas_call | solution.py:328
  58.1 2.7 %collective-permute-done.10 = bf16[8,2,128,128]{3,2,1,0:T(8,128)(2,1)S(1)} collective-permute-done((bf16[8,2,128,128]{3,2,1,0:T(8,128)(2,1)S(1)}, bf16[8,2,128,128]{3,2,1,0:T(8,128)(2,1)S(1)}, u32[]{:S(2)}, u32[]{:S(2)}) %collective-permute-start.10) | collective-permute-done | bytes 524320 | tf_op jit(solution)/shard_map/ppermute | solution.py:13
  63.9 10.6 %shard_map.123 = (bf16[512,128]{1,0:T(8,128)(2,1)S(1)}, bf16[4,128,128]{2,1,0:T(8,128)(2,1)S(1)}, f32[136,128]{1,0:T(8,128)S(1)}) custom-call(s32[2]{0:T(128)S(1)} %pad_add_fusion.3.meta, s32[1056]{0:T(1024)S(1)} %add_select_fusion.1.col, s32[132]{0:T(256)S(1)} %broadcast_minimum_fusion.owner, bf16[128,128]{1,0:T(8,128)(2,1)S(1)} %copy-done.3, ...), custom_call_target="tpu_custom_call" | custom-call | flops 17716740096 | bytes 34603008 | tf_op jit(solution)/shard_map/pallas_call | solution.py:347
  74.7 1.6 %collective-permute-start.16 = (bf16[4,128,128]{2,1,0:T(8,128)(2,1)S(1)}, bf16[4,128,128]{2,1,0:T(8,128)(2,1)S(1)}, u32[]{:S(2)}, u32[]{:S(2)}) collective-permute-start(bf16[4,128,128]{2,1,0:T(8,128)(2,1)S(1)} %get-tuple-element.194.refs_0_), channel_id=1, source_target_pairs={{0,8},{1,9},{2,10},{3,11},{4,12},{5,13},{6,14},{7,15},{8,0},{9,1},... | collective-permute-start | bytes 393224 | tf_op jit(solution)/shard_map/ppermute | solution.py:13
  76.3 1.4 %collective-permute-start.17 = (bf16[4,128,128]{2,1,0:T(8,128)(2,1)S(1)}, bf16[4,128,128]{2,1,0:T(8,128)(2,1)S(1)}, u32[]{:S(2)}, u32[]{:S(2)}) collective-permute-start(bf16[4,128,128]{2,1,0:T(8,128)(2,1)S(1)} %get-tuple-element.194.refs_0_), channel_id=1, source_target_pairs={{0,4},{1,5},{2,6},{3,7},{4,0},{5,1},{6,2},{7,3},{8,12},{9,13},{10,... | collective-permute-start | bytes 393224 | tf_op jit(solution)/shard_map/ppermute | solution.py:13
  79.9 5.2 %shard_map.124.refs_1_ = bf16[576,128,128]{2,1,0:T(8,128)(2,1)} custom-call(s32[2]{0:T(128)S(1)} %pad_add_fusion.meta, s32[576]{0:T(1024)S(1)} %get-tuple-element.220.order, s32[520,128]{1,0:T(8,128)S(1)} %pad.13.codes, bf16[4,128,128]{2,1,0:T(8,128)(2,1)S(1)} %get-tuple-element.194.refs_0_), custom_call_target="tpu_custom_call" | custom-call | flops 4831838208 | bytes 18874368 | tf_op jit(solution)/shard_map/pallas_call | solution.py:328
  85.1 6.4 %collective-permute-done.20 = f32[72,128]{1,0:T(8,128)S(1)} collective-permute-done((f32[72,128]{1,0:T(8,128)S(1)}, f32[72,128]{1,0:T(8,128)S(1)}, u32[]{:S(2)}, u32[]{:S(2)}) %collective-permute-start.20) | collective-permute-done | bytes 36896 | tf_op jit(solution)/shard_map/ppermute | solution.py:13
  91.8 1.5 %collective-permute-start.22 = (bf16[4,2,128,128]{3,2,1,0:T(8,128)(2,1)S(1)}, bf16[4,2,128,128]{3,2,1,0:T(8,128)(2,1)S(1)}, u32[]{:S(2)}, u32[]{:S(2)}) collective-permute-start(bf16[4,2,128,128]{3,2,1,0:T(8,128)(2,1)S(1)} %get-tuple-element.210), channel_id=1, source_target_pairs={{0,1},{1,0},{2,3},{3,2},{4,5},{5,4},{6,7},{7,6},{8,9},{9,8},{10,11... | collective-permute-start | bytes 786440 | tf_op jit(solution)/shard_map/ppermute | solution.py:13
  93.4 1.5 %collective-permute-start.21 = (bf16[4,2,128,128]{3,2,1,0:T(8,128)(2,1)S(1)}, bf16[4,2,128,128]{3,2,1,0:T(8,128)(2,1)S(1)}, u32[]{:S(2)}, u32[]{:S(2)}) collective-permute-start(bf16[4,2,128,128]{3,2,1,0:T(8,128)(2,1)S(1)} %get-tuple-element.211), channel_id=1, source_target_pairs={{0,2},{1,3},{2,0},{3,1},{4,6},{5,7},{6,4},{7,5},{8,10},{9,11},{10,... | collective-permute-start | bytes 786440 | tf_op jit(solution)/shard_map/ppermute | solution.py:13
  94.9 3.4 %shard_map.125.refs_2_ = bf16[576,128,128]{2,1,0:T(8,128)(2,1)} custom-call(s32[2]{0:T(128)S(1)} %pad_add_fusion.6.meta, s32[576]{0:T(1024)S(1)} %get-tuple-element.220.order, s32[520,128]{1,0:T(8,128)S(1)} %pad.13.codes, bf16[4,4,128,128]{3,2,1,0:T(8,128)(2,1)S(1)} %pad_maximum_fusion.4.refs_0_, ...), custom_call_target="tpu_custom_call", output_to_operand_aliasing={{}: (4, {})} | custom-call | flops 4831838208 | bytes 18874368 | tf_op jit(solution)/shard_map/pallas_call | solution.py:328
  103.4 4.3 %shard_map.126.dense = bf16[576,128,128]{2,1,0:T(8,128)(2,1)} custom-call(s32[2]{0:T(128)S(1)} %pad_add_fusion.5.meta, s32[576]{0:T(1024)S(1)} %get-tuple-element.220.order, s32[520,128]{1,0:T(8,128)S(1)} %pad.13.codes, bf16[8,2,128,128]{3,2,1,0:T(8,128)(2,1)S(1)} %pad_maximum_fusion.5.refs_0_, ...), custom_call_target="tpu_custom_call", output_to_operand_aliasing={{}: (5, {})} | custom-call | flops 4831838208 | bytes 18874368 | tf_op jit(solution)/shard_map/pallas_call | solution.py:328
  107.7 6.1 %collective-permute-done.26 = f32[72,128]{1,0:T(8,128)S(1)} collective-permute-done((f32[72,128]{1,0:T(8,128)S(1)}, f32[72,128]{1,0:T(8,128)S(1)}, u32[]{:S(2)}, u32[]{:S(2)}) %collective-permute-start.26) | collective-permute-done | bytes 36896 | tf_op jit(solution)/shard_map/ppermute | solution.py:13
  113.8 1.5 %collective-permute-start.27 = (f32[72,128]{1,0:T(8,128)S(1)}, f32[72,128]{1,0:T(8,128)S(1)}, u32[]{:S(2)}, u32[]{:S(2)}) collective-permute-start(f32[72,128]{1,0:T(8,128)S(1)} %add.697), channel_id=1, source_target_pairs={{0,1},{1,0},{2,3},{3,2},{4,5},{5,4},{6,7},{7,6},{8,9},{9,8},{10,11... | collective-permute-start | bytes 110600 | tf_op jit(solution)/shard_map/ppermute | solution.py:13
  115.2 5.9 %shard_map.127 = f32[8,128,128]{2,1,0:T(8,128)S(1)} custom-call(s32[2]{0:T(128)S(1)} %pad_add_fusion.1.meta, s32[576]{0:T(1024)S(1)} %get-tuple-element.221.src, s32[72]{0:T(128)S(1)} %broadcast_minimum_fusion.1.owner, bf16[576,128,128]{2,1,0:T(8,128)(2,1)} %shard_map.126.dense, bf16[16,128,128]{2,1,0:T(8,128)(2,1)S(1)} %bitcast.145, ...), custom_call_target="tpu_custom_call" | custom-call | flops 9663676416 | bytes 18874368 | tf_op jit(solution)/shard_map/pallas_call | solution.py:372
  (136 shorter events, 25.4 us)
Async XLA Ops:
  0.6 21.0 %collective-permute-start.4 = (bf16[4,128,128]{2,1,0:T(8,128)(2,1)}, bf16[4,128,128]{2,1,0:T(8,128)(2,1)S(1)}, u32[]{:S(2)}, u32[]{:S(2)}) collective-permute-start(bf16[4,128,128]{2,1,0:T(8,128)(2,1)} %bitcast.163), channel_id=1, source_target_pairs={{0,8},{1,9},{2,10},{3,11},{4,12},{5,13},{6,14},{7,15},{8,0},{9,1},... | collective-permute-start | bytes 393224 | tf_op jit(solution)/shard_map/ppermute | solution.py:13
  4.7 16.9 %collective-permute-start.5 = (bf16[4,128,128]{2,1,0:T(8,128)(2,1)}, bf16[4,128,128]{2,1,0:T(8,128)(2,1)S(1)}, u32[]{:S(2)}, u32[]{:S(2)}) collective-permute-start(bf16[4,128,128]{2,1,0:T(8,128)(2,1)} %bitcast.164), channel_id=1, source_target_pairs={{0,4},{1,5},{2,6},{3,7},{4,0},{5,1},{6,2},{7,3},{8,12},{9,13},{10,... | collective-permute-start | bytes 393224 | tf_op jit(solution)/shard_map/ppermute | solution.py:13
  6.3 15.3 %collective-permute-start.6 = (bf16[4,128,128]{2,1,0:T(8,128)(2,1)}, bf16[4,128,128]{2,1,0:T(8,128)(2,1)S(1)}, u32[]{:S(2)}, u32[]{:S(2)}) collective-permute-start(bf16[4,128,128]{2,1,0:T(8,128)(2,1)} %bitcast.165), channel_id=1, source_target_pairs={{0,12},{1,13},{2,14},{3,15},{4,8},{5,9},{6,10},{7,11},{8,4},{9,5},... | collective-permute-start | bytes 393224 | tf_op jit(solution)/shard_map/ppermute | solution.py:13
  13.5 22.6 %all-to-all-start = ((s32[16,72,128]{2,1,0:T(8,128)}), s32[16,72,128]{2,1,0:T(8,128)S(1)}, u32[]{:S(2)}, u32[]{:S(2)}) async-start(s32[16,72,128]{2,1,0:T(8,128)} %bitcast.26), calls=%async_computation | async-start | bytes 1179648 | tf_op jit(solution)/shard_map/all_to_all | solution.py:494
  22.7 11.5 %collective-permute-start.8 = (bf16[4,2,128,128]{3,2,1,0:T(8,128)(2,1)S(1)}, bf16[4,2,128,128]{3,2,1,0:T(8,128)(2,1)S(1)}, u32[]{:S(2)}, u32[]{:S(2)}) collective-permute-start(bf16[4,2,128,128]{3,2,1,0:T(8,128)(2,1)S(1)} %get-tuple-element.212), channel_id=1, source_target_pairs={{0,1},{1,0},{2,3},{3,2},{4,5},{5,4},{6,7},{7,6},{8,9},{9,8},{10,11... | collective-permute-start | bytes 786440 | tf_op jit(solution)/shard_map/ppermute | solution.py:13
  25.4 9.2 %collective-permute-start.7 = (bf16[4,2,128,128]{3,2,1,0:T(8,128)(2,1)S(1)}, bf16[4,2,128,128]{3,2,1,0:T(8,128)(2,1)S(1)}, u32[]{:S(2)}, u32[]{:S(2)}) collective-permute-start(bf16[4,2,128,128]{3,2,1,0:T(8,128)(2,1)S(1)} %get-tuple-element.213), channel_id=1, source_target_pairs={{0,2},{1,3},{2,0},{3,1},{4,6},{5,7},{6,4},{7,5},{8,10},{9,11},{10,... | collective-permute-start | bytes 786440 | tf_op jit(solution)/shard_map/ppermute | solution.py:13
  47.6 13.2 %collective-permute-start.10 = (bf16[8,2,128,128]{3,2,1,0:T(8,128)(2,1)S(1)}, bf16[8,2,128,128]{3,2,1,0:T(8,128)(2,1)S(1)}, u32[]{:S(2)}, u32[]{:S(2)}) collective-permute-start(bf16[8,2,128,128]{3,2,1,0:T(8,128)(2,1)S(1)} %pad_maximum_fusion.2.refs_0_), channel_id=1, source_target_pairs={{0,1},{1,0},{2,3},{3,2},{4,5},{5,4},{6,7},{7,6},{8,9},{9,8},{10,11... | collective-permute-start | bytes 1572872 | tf_op jit(solution)/shard_map/ppermute | solution.py:13
  48.2 12.9 %collective-permute-start.11 = (bf16[8,2,128,128]{3,2,1,0:T(8,128)(2,1)S(1)}, bf16[8,2,128,128]{3,2,1,0:T(8,128)(2,1)S(1)}, u32[]{:S(2)}, u32[]{:S(2)}) collective-permute-start(bf16[8,2,128,128]{3,2,1,0:T(8,128)(2,1)S(1)} %pad_maximum_fusion.3.refs_1_), channel_id=1, source_target_pairs={{0,2},{1,3},{2,0},{3,1},{4,6},{5,7},{6,4},{7,5},{8,10},{9,11},{10,... | collective-permute-start | bytes 1572872 | tf_op jit(solution)/shard_map/ppermute | solution.py:13
  50.2 12.3 %collective-permute-start.12 = (bf16[16,128,128]{2,1,0:T(8,128)(2,1)S(1)}, bf16[16,128,128]{2,1,0:T(8,128)(2,1)S(1)}, u32[]{:S(2)}, u32[]{:S(2)}) collective-permute-start(bf16[16,128,128]{2,1,0:T(8,128)(2,1)S(1)} %bitcast.142), channel_id=1, source_target_pairs={{0,16},{16,0},{1,17},{17,1},{2,18},{18,2},{3,19},{19,3},{4,20},{20... | collective-permute-start | bytes 1572872 | tf_op jit(solution)/shard_map/ppermute | solution.py:13
  50.2 12.3 %collective-permute-start.14 = (bf16[16,128,128]{2,1,0:T(8,128)(2,1)S(1)}, bf16[16,128,128]{2,1,0:T(8,128)(2,1)S(1)}, u32[]{:S(2)}, u32[]{:S(2)}) collective-permute-start(bf16[16,128,128]{2,1,0:T(8,128)(2,1)S(1)} %bitcast.140), channel_id=1, source_target_pairs={{0,16},{16,0},{1,17},{17,1},{2,18},{18,2},{3,19},{19,3},{4,20},{20... | collective-permute-start | bytes 1572872 | tf_op jit(solution)/shard_map/ppermute | solution.py:13
  61.1 2.7 %collective-permute-start.15 = (bf16[16,128,128]{2,1,0:T(8,128)(2,1)S(1)}, bf16[16,128,128]{2,1,0:T(8,128)(2,1)S(1)}, u32[]{:S(2)}, u32[]{:S(2)}) collective-permute-start(bf16[16,128,128]{2,1,0:T(8,128)(2,1)S(1)} %bitcast.150), channel_id=1, source_target_pairs={{0,16},{16,0},{1,17},{17,1},{2,18},{18,2},{3,19},{19,3},{4,20},{20... | collective-permute-start | bytes 1572872 | tf_op jit(solution)/shard_map/ppermute | solution.py:13
  74.5 4.6 %collective-permute-start.19 = (f32[1,72,128]{2,1,0:T(8,128)S(1)}, f32[1,72,128]{2,1,0:T(8,128)S(1)}, u32[]{:S(2)}, u32[]{:S(2)}) collective-permute-start(f32[1,72,128]{2,1,0:T(8,128)S(1)} %slice_bitcast_fusion.10), channel_id=1, source_target_pairs={{0,16},{16,0},{1,17},{17,1},{2,18},{18,2},{3,19},{19,3},{4,20},{20... | collective-permute-start | bytes 110600 | tf_op jit(solution)/shard_map/ppermute | solution.py:13
  74.7 16.8 %collective-permute-start.16 = (bf16[4,128,128]{2,1,0:T(8,128)(2,1)S(1)}, bf16[4,128,128]{2,1,0:T(8,128)(2,1)S(1)}, u32[]{:S(2)}, u32[]{:S(2)}) collective-permute-start(bf16[4,128,128]{2,1,0:T(8,128)(2,1)S(1)} %get-tuple-element.194.refs_0_), channel_id=1, source_target_pairs={{0,8},{1,9},{2,10},{3,11},{4,12},{5,13},{6,14},{7,15},{8,0},{9,1},... | collective-permute-start | bytes 393224 | tf_op jit(solution)/shard_map/ppermute | solution.py:13
  76.3 15.2 %collective-permute-start.17 = (bf16[4,128,128]{2,1,0:T(8,128)(2,1)S(1)}, bf16[4,128,128]{2,1,0:T(8,128)(2,1)S(1)}, u32[]{:S(2)}, u32[]{:S(2)}) collective-permute-start(bf16[4,128,128]{2,1,0:T(8,128)(2,1)S(1)} %get-tuple-element.194.refs_0_), channel_id=1, source_target_pairs={{0,4},{1,5},{2,6},{3,7},{4,0},{5,1},{6,2},{7,3},{8,12},{9,13},{10,... | collective-permute-start | bytes 393224 | tf_op jit(solution)/shard_map/ppermute | solution.py:13
  77.7 13.8 %collective-permute-start.18 = (bf16[4,128,128]{2,1,0:T(8,128)(2,1)S(1)}, bf16[4,128,128]{2,1,0:T(8,128)(2,1)S(1)}, u32[]{:S(2)}, u32[]{:S(2)}) collective-permute-start(bf16[4,128,128]{2,1,0:T(8,128)(2,1)S(1)} %get-tuple-element.194.refs_0_), channel_id=1, source_target_pairs={{0,12},{1,13},{2,14},{3,15},{4,8},{5,9},{6,10},{7,11},{8,4},{9,5},... | collective-permute-start | bytes 393224 | tf_op jit(solution)/shard_map/ppermute | solution.py:13
  79.1 12.4 %collective-permute-start.20 = (f32[72,128]{1,0:T(8,128)S(1)}, f32[72,128]{1,0:T(8,128)S(1)}, u32[]{:S(2)}, u32[]{:S(2)}) collective-permute-start(f32[72,128]{1,0:T(8,128)S(1)} %fusion.26), channel_id=1, source_target_pairs={{0,8},{1,9},{2,10},{3,11},{4,12},{5,13},{6,14},{7,15},{8,0},{9,1},... | collective-permute-start | bytes 110600 | tf_op jit(solution)/shard_map/ppermute | solution.py:13
  91.6 6.7 %collective-permute-start.23 = (f32[72,128]{1,0:T(8,128)S(1)}, f32[72,128]{1,0:T(8,128)S(1)}, u32[]{:S(2)}, u32[]{:S(2)}) collective-permute-start(f32[72,128]{1,0:T(8,128)S(1)} %add.695), channel_id=1, source_target_pairs={{0,4},{1,5},{2,6},{3,7},{4,0},{5,1},{6,2},{7,3},{8,12},{9,13},{10,... | collective-permute-start | bytes 110600 | tf_op jit(solution)/shard_map/ppermute | solution.py:13
  91.8 7.6 %collective-permute-start.22 = (bf16[4,2,128,128]{3,2,1,0:T(8,128)(2,1)S(1)}, bf16[4,2,128,128]{3,2,1,0:T(8,128)(2,1)S(1)}, u32[]{:S(2)}, u32[]{:S(2)}) collective-permute-start(bf16[4,2,128,128]{3,2,1,0:T(8,128)(2,1)S(1)} %get-tuple-element.210), channel_id=1, source_target_pairs={{0,1},{1,0},{2,3},{3,2},{4,5},{5,4},{6,7},{7,6},{8,9},{9,8},{10,11... | collective-permute-start | bytes 786440 | tf_op jit(solution)/shard_map/ppermute | solution.py:13
  93.4 7.2 %collective-permute-start.21 = (bf16[4,2,128,128]{3,2,1,0:T(8,128)(2,1)S(1)}, bf16[4,2,128,128]{3,2,1,0:T(8,128)(2,1)S(1)}, u32[]{:S(2)}, u32[]{:S(2)}) collective-permute-start(bf16[4,2,128,128]{3,2,1,0:T(8,128)(2,1)S(1)} %get-tuple-element.211), channel_id=1, source_target_pairs={{0,2},{1,3},{2,0},{3,1},{4,6},{5,7},{6,4},{7,5},{8,10},{9,11},{10,... | collective-permute-start | bytes 786440 | tf_op jit(solution)/shard_map/ppermute | solution.py:13
  100.6 13.1 %collective-permute-start.24 = (bf16[8,2,128,128]{3,2,1,0:T(8,128)(2,1)S(1)}, bf16[8,2,128,128]{3,2,1,0:T(8,128)(2,1)S(1)}, u32[]{:S(2)}, u32[]{:S(2)}) collective-permute-start(bf16[8,2,128,128]{3,2,1,0:T(8,128)(2,1)S(1)} %pad_maximum_fusion.5.refs_0_), channel_id=1, source_target_pairs={{0,1},{1,0},{2,3},{3,2},{4,5},{5,4},{6,7},{7,6},{8,9},{9,8},{10,11... | collective-permute-start | bytes 1572872 | tf_op jit(solution)/shard_map/ppermute | solution.py:13
  101.3 12.5 %collective-permute-start.25 = (bf16[8,2,128,128]{3,2,1,0:T(8,128)(2,1)S(1)}, bf16[8,2,128,128]{3,2,1,0:T(8,128)(2,1)S(1)}, u32[]{:S(2)}, u32[]{:S(2)}) collective-permute-start(bf16[8,2,128,128]{3,2,1,0:T(8,128)(2,1)S(1)} %pad_maximum_fusion.6.refs_1_), channel_id=1, source_target_pairs={{0,2},{1,3},{2,0},{3,1},{4,6},{5,7},{6,4},{7,5},{8,10},{9,11},{10,... | collective-permute-start | bytes 1572872 | tf_op jit(solution)/shard_map/ppermute | solution.py:13
  102.7 11.1 %collective-permute-start.26 = (f32[72,128]{1,0:T(8,128)S(1)}, f32[72,128]{1,0:T(8,128)S(1)}, u32[]{:S(2)}, u32[]{:S(2)}) collective-permute-start(f32[72,128]{1,0:T(8,128)S(1)} %add.696), channel_id=1, source_target_pairs={{0,2},{1,3},{2,0},{3,1},{4,6},{5,7},{6,4},{7,5},{8,10},{9,11},{10,... | collective-permute-start | bytes 110600 | tf_op jit(solution)/shard_map/ppermute | solution.py:13
  113.8 7.4 %collective-permute-start.27 = (f32[72,128]{1,0:T(8,128)S(1)}, f32[72,128]{1,0:T(8,128)S(1)}, u32[]{:S(2)}, u32[]{:S(2)}) collective-permute-start(f32[72,128]{1,0:T(8,128)S(1)} %add.697), channel_id=1, source_target_pairs={{0,1},{1,0},{2,3},{3,2},{4,5},{5,4},{6,7},{7,6},{8,9},{9,8},{10,11... | collective-permute-start | bytes 110600 | tf_op jit(solution)/shard_map/ppermute | solution.py:13
  121.6 2.0 %collective-permute-start.28 = (f32[1,512,128]{2,1,0:T(8,128)S(1)}, f32[1,512,128]{2,1,0:T(8,128)S(1)}, u32[]{:S(2)}, u32[]{:S(2)}) collective-permute-start(f32[1,512,128]{2,1,0:T(8,128)S(1)} %slice_bitcast_fusion.8), channel_id=1, source_target_pairs={{0,16},{16,0},{1,17},{17,1},{2,18},{18,2},{3,19},{19,3},{4,20},{20... | collective-permute-start | bytes 786440 | tf_op jit(solution)/shard_map/ppermute | solution.py:13
  (10 other events, 87.8 us)

commit v2 on v1

--- a/solution.py
+++ b/solution.py
@@ -5,6 +5,7 @@
 from jax import lax
 from jax.experimental import pallas as pl
 from jax.experimental.pallas import tpu as pltpu
+from jax.experimental.layout import Layout, with_layout_constraint
 from jax.sharding import PartitionSpec as P
 
 
@@ -171,7 +172,7 @@
     return copies
 
 
-def read_dense(turns, dense, dbuf, sems, product, prepare):
+def read_dense(start, turns, dense, dbuf, sems, product, prepare):
     def in_copy(i):
         slot = lax.rem(i, DEPTH)
         return pltpu.make_async_copy(
@@ -182,7 +183,7 @@
         in_copy(i).start()
         return 0
 
-    lax.fori_loop(0, jnp.minimum(turns, DEPTH - 1), begin, 0)
+    lax.fori_loop(start, jnp.minimum(turns, start + DEPTH - 1), begin, 0)
     prepare()
 
     def turn(i, _):
@@ -194,7 +195,7 @@
         product(i, lax.rem(i, DEPTH))
         return 0
 
-    lax.fori_loop(0, turns, turn, 0)
+    lax.fori_loop(start, turns, turn, 0)
 
 
 def add_pairs(i, owner, one, into):
@@ -236,7 +237,7 @@
 
         add_pairs(i, owner, one, totals)
 
-    read_dense(meta[1], dense, dbuf, sems, product, prepare)
+    read_dense(meta[0], meta[1], dense, dbuf, sems, product, prepare)
 
     weight_sum, bias_sum = 0.0, 0.0
     for q in range(totals.shape[0]):
@@ -270,12 +271,12 @@
     lax.fori_loop(0, meta[0], turn, 0)
 
 
-def backward_kernel(n, meta, src, owner, dense, *refs):
+def backward_kernel(n, meta, src, owner, before, dense, *refs):
     pieces, (acc, grad, dbuf, piece_sems, sems) = refs[:n], refs[n:]
     copies = fetch(pieces, grad, piece_sems)
 
     def prepare():
-        acc[...] = jnp.zeros_like(acc)
+        acc[...] = before[...]
         for copy in copies:
             copy.wait()
 
@@ -288,7 +289,7 @@
 
         add_pairs(i, owner, one, acc)
 
-    read_dense(meta[1], dense, dbuf, sems, product, prepare)
+    read_dense(meta[0], meta[1], dense, dbuf, sems, product, prepare)
 
 
 SMEM = pl.BlockSpec(memory_space=pltpu.SMEM)
@@ -366,13 +367,13 @@
     )(meta, col, owner, weight, bias, cotangent, dense, *feat)
 
 
-def run_backward(meta, src, owner, pieces, dense, col_blocks):
+def run_backward(meta, src, owner, before, dense, pieces):
     n = len(pieces)
     size, width, _ = pieces[0].shape
     return pl.pallas_call(
         functools.partial(backward_kernel, n),
-        out_shape=jax.ShapeDtypeStruct((col_blocks, width, 128), jnp.float32),
-        in_specs=[SMEM] * 3 + [HBM] * (n + 1),
+        out_shape=jax.ShapeDtypeStruct(before.shape, jnp.float32),
+        in_specs=[SMEM] * 3 + [VMEM] + [HBM] * (n + 1),
         out_specs=VMEM,
         scratch_shapes=[
             pltpu.VMEM((n * size, width, 128), jnp.bfloat16),
@@ -382,10 +383,10 @@
         ],
         compiler_params=PARAMS,
         cost_estimate=cost(src.shape[0], 4),
-    )(meta, src, owner, dense, *pieces)
-
-
-def grouped(key, live, value, fill, keys):
+    )(meta, src, owner, before, dense, *pieces)
+
+
+def grouped(key, live, value, fill, keys, split):
     ids = jnp.arange(key.shape[0], dtype=jnp.int32)
     names = jnp.arange(keys, dtype=jnp.int32)
     key = jnp.where(live, key, keys)
@@ -393,14 +394,17 @@
     rank = jnp.sum(before.astype(jnp.int32), axis=0)
     counts = jnp.sum((key[:, None] == names[None, :]).astype(jnp.int32), axis=0)
     filled = (counts + GROUP - 1) // GROUP * GROUP
+    below = jnp.sum(jnp.where(names < split, filled, 0))
+    first_turns = (below + TURN - 1) // TURN
+    filled = filled + jnp.where(names == split - 1, first_turns * TURN - below, 0)
     base = jnp.sum(jnp.where(names[:, None] < key[None, :], filled[:, None], 0), axis=0)
     pos = jnp.where(live, base + rank, -1)
     ends = jnp.sum(jnp.where(names[:, None] <= names[None, :], filled[:, None], 0), axis=0)
-    length = -(-(key.shape[0] + keys * GROUP) // TURN) * TURN
+    length = (-(-(key.shape[0] + keys * GROUP) // TURN) + 1) * TURN
     first = jnp.arange(length // GROUP, dtype=jnp.int32) * GROUP
     group_key = jnp.sum((ends[:, None] <= first[None, :]).astype(jnp.int32), axis=0)
     turns = (jnp.sum(filled) + TURN - 1) // TURN
-    return place(pos, value, length, fill), jnp.minimum(group_key, keys - 1), turns
+    return place(pos, value, length, fill), jnp.minimum(group_key, keys - 1), turns, first_turns
 
 
 def place(pos, value, length, fill):
@@ -466,16 +470,27 @@
         return output, turned, jnp.concatenate([weight_sum, bias_sum], axis=0) * scale
 
     source = piece_index(per, home ^ mine, brow % per)
-    back_list, back_owner, back_turns = grouped(
-        bcol, live, ids * FIELD + source, slots * FIELD, col_blocks
+    unit = row_blocks // (2 * len(part_orders(per)))
+    late = source // unit % 2
+    source = source // (2 * unit) * unit + source % unit
+    back_list, back_owner, back_turns, early_turns = grouped(
+        late * col_blocks + bcol,
+        live,
+        ids * FIELD + source,
+        slots * FIELD,
+        2 * col_blocks,
+        col_blocks,
     )
-    back_span = jnp.stack([jnp.zeros_like(back_turns), back_turns])
+    back_owner = back_owner % col_blocks
+    spans = [
+        jnp.stack([jnp.zeros_like(early_turns), early_turns]),
+        jnp.stack([early_turns, back_turns]),
+    ]
     state = {"dense": None}
 
-    def build(held, start, end):
-        span = jnp.stack([back_turns * start // 4, back_turns * end // 4])
+    def build(held, half):
         state["dense"] = run_build(
-            span, back_list // FIELD, codes, held, state["dense"]
+            spans[half], back_list // FIELD, codes, held, state["dense"]
         )
 
     if by_owner:
@@ -508,25 +523,29 @@
             per, sources ^ mine, col_there % per, (col_there // per) ^ mine_row, n_row
         )
         line = sources * stride + places
-        listed, owner, turns = grouped(
-            row_here, (got > 0).reshape(-1), (line * FIELD + col_there).reshape(-1), (ROOM + 1) * FIELD, per
+        listed, owner, turns, _ = grouped(
+            row_here,
+            (got > 0).reshape(-1),
+            (line * FIELD + col_there).reshape(-1),
+            (ROOM + 1) * FIELD,
+            per,
+            per,
         )
         span = jnp.stack([jnp.zeros_like(turns), turns])
-        lists = [listed, owner, span, any_over]
+
+        def prepare(step, held):
+            if step == 0:
+                build(held, 0)
+            if step == 1:
+                held, state["dense"] = lax.optimization_barrier((held, state["dense"]))
+            return held
+
+        pairs = gather_pieces(features.reshape(per, 128, width), prepare)
         lines = came.reshape(n_col * stride, 128)
-        here = None
-
-        def prepare(step, held):
-            nonlocal lists, here
-            if step == 1:
-                held, lists, here = lax.optimization_barrier((held, lists, here))
-            half = jnp.stack([turns * step // 2, turns * (step + 1) // 2])
-            here = run_build(half, listed // FIELD, lines, held + lists[3:], here)
-            return held
-
-        pairs = gather_pieces(features.reshape(per, 128, width), prepare)
-        listed, owner, span, any_over = lists
-        last, here = lax.optimization_barrier(([pair[1] for pair in pairs], here))
+        here = run_build(span, listed // FIELD, lines, [], None)
+        last, here, any_over = lax.optimization_barrier(
+            ([pair[1] for pair in pairs], here, any_over)
+        )
         feat = []
         for pair in [[pair[0], x] for pair, x in zip(pairs, last)]:
             rows = [pair]
@@ -541,6 +560,7 @@
         done = tile_plan()
 
     output, turned, total = done
+    turned = with_layout_constraint(turned, Layout(major_to_minor=(0, 1, 2)))
     steps = bits_of("col")[::-1]
 
     def add_total():
@@ -552,22 +572,30 @@
         )
         if steps:
             add_total()
-        build(held, 2 + step, 3 + step)
+        if step == 1:
+            add_products(0, held)
         return held
 
+    def add_products(half, pieces):
+        pieces = [x.reshape((-1,) + x.shape[2:]) if x.ndim == 4 else x for x in pieces]
+        state["acc"] = run_backward(
+            spans[half], back_list % FIELD, back_owner, state["acc"], state["dense"], pieces
+        )
+
+    state["acc"] = jnp.zeros((col_blocks, width, 128), jnp.float32)
     state["total"] = split_rows(total)
     while len(steps) > 3:
         add_total()
-    build([turned], 0, 2)
-    grad = [x for pair in gather_pieces(turned, beside) for x in pair]
-    grad, state["total"] = lax.optimization_barrier((grad, state["total"]))
+    build([turned], 1)
+    grad = gather_pieces(turned, beside)
+    late_pieces, state["total"] = lax.optimization_barrier(
+        ([pair[1] for pair in grad], state["total"])
+    )
     while steps:
         add_total()
-    acc = run_backward(
-        back_span, back_list % FIELD, back_owner, grad, state["dense"], col_blocks
-    )
-    acc, total = lax.optimization_barrier((acc, state["total"]))
-    total = join_rows(total)
+    total = join_rows(state["total"])
+    add_products(1, late_pieces)
+    acc = state["acc"]
     back = jnp.swapaxes(acc, 1, 2).reshape(col_blocks * 128, width)
     grad_proj = scatter_sum(
         jnp.stack(

time: 127 us -> 126 us (level); the launches traced: 125 us -> 127 us
  waiting for transfers between devices: 29.4 us -> 20.8 us
  other arithmetic: 9.81 us -> 14.7 us
  starting transfers between devices: 33.1 us -> 36.1 us
  between operations: 4.47 us -> 7.08 us
    ppermute x26, waiting for transfers between devices: 27.9 us -> 20.8 us  [swap(): return lax.ppermute(x, axis, [(i, i ^ bit) for i in range(n)])]
    ppermute x26, starting transfers between devices: 26 us -> 29.1 us  [swap(): return lax.ppermute(x, axis, [(i, i ^ bit) for i in range(n)])]
    pallas_call x5 -> x3, Pallas kernels: 26.9 us -> 24 us  [run_build(): pl.pallas_call(build_kernel, out_shape=jax.ShapeDtypeStruct((order.shape[...]
    pallas_call x1 -> x2, Pallas kernels: 5.93 us -> 8.7 us  [run_backward(): pl.pallas_call(functools.partial(backward_kernel, n), out_shape=jax.Shape...]
    all_to_all x1, waiting for transfers between devices: 1.48 us -> 0.01 us  [shards(): lax.all_to_all(packed.reshape(n_col, stride, 128), 'col', split_axis=0, c...]
    reduce_sum x0 -> x2, other arithmetic: none -> 1.29 us  [grouped(): below = jnp.sum(jnp.where(names < split, filled, 0))]
  transfers between devices with their start and end apart: 27 -> 27, of which waited for: 13 -> 10; matrix products, arithmetic and copies ran while one was open for 7% -> 12% of each run, Pallas kernels for 22% -> 23%
where the time goes in v2:
time: 126 us; the launch traced here: 127 us
  Pallas kernels  45.9 us (36%)
  starting transfers between devices  36.1 us (29%)
  waiting for transfers between devices  20.8 us (17%)
  other arithmetic  14.7 us (12%)
  between operations  7.08 us (6%)
  local copies, waits for them, and re-layouts  1.83 us (1%)
    ppermute x26, starting transfers between devices, swap(): return lax.ppermute(x, axis, [(i, i ^ bit) for i in range(n)])  29.1 us
    pallas_call x3, Pallas kernels, run_build(): pl.pallas_call(build_kernel, out_shape=jax.ShapeDtypeStruct((order.shape[...  24 us
    ppermute x26, waiting for transfers between devices, swap(): return lax.ppermute(x, axis, [(i, i ^ bit) for i in range(n)])  20.8 us
    pallas_call x1, Pallas kernels, run_forward(): pl.pallas_call(functools.partial(forward_kernel, n, scale), out_shape=(ja...  11.5 us
    pallas_call x2, Pallas kernels, run_backward(): pl.pallas_call(functools.partial(backward_kernel, n), out_shape=jax.Shape...  8.7 us
    all_to_all x1, starting transfers between devices, shards(): lax.all_to_all(packed.reshape(n_col, stride, 128), 'col', split_axis=0, c...  7.01 us
  transfers between devices with their start and end apart: 27, of which 10 were waited for; matrix products, arithmetic and copies ran while one was open for 12% of the time, Pallas kernels for 23%

profile of v2, /device:TPU:0, one launch (start us, length us, event | category | flops | bytes accessed | tf_op | source)
XLA Modules:
  0.0 127.3 jit_solution(5327589179697851347)
XLA Ops:
  0.6 5.1 %collective-permute-start.6 = (bf16[4,128,128]{2,1,0:T(8,128)(2,1)}, bf16[4,128,128]{2,1,0:T(8,128)(2,1)S(1)}, u32[]{:S(2)}, u32[]{:S(2)}) collective-permute-start(bf16[4,128,128]{2,1,0:T(8,128)(2,1)} %bitcast.157), channel_id=1, source_target_pairs={{0,12},{1,13},{2,14},{3,15},{4,8},{5,9},{6,10},{7,11},{8,4},{9,5},... | collective-permute-start | bytes 393224 | tf_op jit(solution)/shard_map/ppermute | solution.py:14
  11.5 1.7 %shard_map.121 = s32[1152,128]{1,0:T(8,128)} custom-call(s32[1]{0:T(128)} %bitcast.28.meta, s32[512]{0:T(512)S(1)} %get-tuple-element.213.pos, s32[520,128]{1,0:T(8,128)S(1)} %pad.13.codes, s32[16,128]{1,0:T(8,128)S(1)} %concatenate.26.labels), custom_call_target="tpu_custom_call" | custom-call | tf_op jit(solution)/shard_map/pallas_call | solution.py:318
  13.3 7.0 %all-to-all-start = ((s32[16,72,128]{2,1,0:T(8,128)}), s32[16,72,128]{2,1,0:T(8,128)S(1)}, u32[]{:S(2)}, u32[]{:S(2)}) async-start(s32[16,72,128]{2,1,0:T(8,128)} %bitcast.29), calls=%async_computation | async-start | bytes 1179648 | tf_op jit(solution)/shard_map/all_to_all | solution.py:509
  26.8 2.0 %collective-permute-start.7 = (bf16[4,2,128,128]{3,2,1,0:T(8,128)(2,1)S(1)}, bf16[4,2,128,128]{3,2,1,0:T(8,128)(2,1)S(1)}, u32[]{:S(2)}, u32[]{:S(2)}) collective-permute-start(bf16[4,2,128,128]{3,2,1,0:T(8,128)(2,1)S(1)} %get-tuple-element.201), channel_id=1, source_target_pairs={{0,2},{1,3},{2,0},{3,1},{4,6},{5,7},{6,4},{7,5},{8,10},{9,11},{10,... | collective-permute-start | bytes 786440 | tf_op jit(solution)/shard_map/ppermute | solution.py:14
  28.8 1.5 %collective-permute-start.8 = (bf16[4,2,128,128]{3,2,1,0:T(8,128)(2,1)S(1)}, bf16[4,2,128,128]{3,2,1,0:T(8,128)(2,1)S(1)}, u32[]{:S(2)}, u32[]{:S(2)}) collective-permute-start(bf16[4,2,128,128]{3,2,1,0:T(8,128)(2,1)S(1)} %get-tuple-element.200), channel_id=1, source_target_pairs={{0,1},{1,0},{2,3},{3,2},{4,5},{5,4},{6,7},{7,6},{8,9},{9,8},{10,11... | collective-permute-start | bytes 786440 | tf_op jit(solution)/shard_map/ppermute | solution.py:14
  30.2 5.9 %shard_map.120.refs_1_ = bf16[672,128,128]{2,1,0:T(8,128)(2,1)} custom-call(s32[2]{0:T(128)S(1)} %pad_add_fusion.1.meta, s32[672]{0:T(1024)S(1)} %get-tuple-element.209.order, s32[520,128]{1,0:T(8,128)S(1)} %pad.13.codes, bf16[4,4,128,128]{3,2,1,0:T(8,128)(2,1)S(1)} %pad_maximum_fusion.1.refs_0_), custom_call_target="tpu_custom_call" | custom-call | flops 5637144576 | bytes 22020096 | tf_op jit(solution)/shard_map/pallas_call | solution.py:329
  37.9 2.5 %collective-permute-start.9 = (bf16[8,2,128,128]{3,2,1,0:T(8,128)(2,1)S(1)}, bf16[8,2,128,128]{3,2,1,0:T(8,128)(2,1)S(1)}, u32[]{:S(2)}, u32[]{:S(2)}) collective-permute-start(bf16[8,2,128,128]{3,2,1,0:T(8,128)(2,1)S(1)} %pad_maximum_fusion.2), channel_id=1, source_target_pairs={{0,1},{1,0},{2,3},{3,2},{4,5},{5,4},{6,7},{7,6},{8,9},{9,8},{10,11... | collective-permute-start | bytes 1572872 | tf_op jit(solution)/shard_map/ppermute | solution.py:14
  46.4 11.1 %shard_map.122.dense = bf16[1088,128,128]{2,1,0:T(8,128)(2,1)} custom-call(s32[2]{0:T(128)S(1)} %pad_add_fusion.meta, s32[1088]{0:T(1024)S(1)} %get-tuple-element.207.order, s32[1152,128]{1,0:T(8,128)S(1)} %bitcast.134), custom_call_target="tpu_custom_call" | custom-call | flops 9126805504 | bytes 35651584 | tf_op jit(solution)/shard_map/pallas_call | solution.py:329
  61.5 11.5 %shard_map.123 = (bf16[512,128]{1,0:T(8,128)(2,1)S(1)}, bf16[4,128,128]{2,1,0:T(8,128)(2,1)}, f32[136,128]{1,0:T(8,128)S(1)}) custom-call(s32[2]{0:T(128)S(1)} %pad_add_fusion.meta, s32[1088]{0:T(1024)S(1)} %get-tuple-element.206.col, s32[136]{0:T(256)S(1)} %broadcast_minimum_fusion.owner, bf16[128,128]{1,0:T(8,128)(2,1)S(1)} %copy-done.2, ...), custom_call_target="tpu_custom_call" | custom-call | flops 18253611008 | bytes 35651584 | tf_op jit(solution)/shard_map/pallas_call | solution.py:348
  73.2 1.5 %collective-permute-start.18 = (bf16[4,128,128]{2,1,0:T(8,128)(2,1)}, bf16[4,128,128]{2,1,0:T(8,128)(2,1)S(1)}, u32[]{:S(2)}, u32[]{:S(2)}) collective-permute-start(bf16[4,128,128]{2,1,0:T(8,128)(2,1)} %get-tuple-element.177.refs_0_), channel_id=1, source_target_pairs={{0,12},{1,13},{2,14},{3,15},{4,8},{5,9},{6,10},{7,11},{8,4},{9,5},... | collective-permute-start | bytes 393224 | tf_op jit(solution)/shard_map/ppermute | solution.py:14
  75.2 2.4 %collective-permute-start.16 = (bf16[4,128,128]{2,1,0:T(8,128)(2,1)}, bf16[4,128,128]{2,1,0:T(8,128)(2,1)S(1)}, u32[]{:S(2)}, u32[]{:S(2)}) collective-permute-start(bf16[4,128,128]{2,1,0:T(8,128)(2,1)} %get-tuple-element.177.refs_0_), channel_id=1, source_target_pairs={{0,8},{1,9},{2,10},{3,11},{4,12},{5,13},{6,14},{7,15},{8,0},{9,1},... | collective-permute-start | bytes 393224 | tf_op jit(solution)/shard_map/ppermute | solution.py:14
  78.3 7.0 %shard_map.124.dense = bf16[672,128,128]{2,1,0:T(8,128)(2,1)} custom-call(s32[2]{0:T(128)S(1)} %pad_add_fusion.2.meta, s32[672]{0:T(1024)S(1)} %get-tuple-element.209.order, s32[520,128]{1,0:T(8,128)S(1)} %pad.13.codes, bf16[4,128,128]{2,1,0:T(8,128)(2,1)} %get-tuple-element.177.refs_0_, ...), custom_call_target="tpu_custom_call", output_to_operand_aliasing={{}: (4, {})} | custom-call | flops 5637144576 | bytes 22020096 | tf_op jit(solution)/shard_map/pallas_call | solution.py:329
  85.2 3.8 %collective-permute-done.20 = f32[72,128]{1,0:T(8,128)S(1)} collective-permute-done((f32[72,128]{1,0:T(8,128)S(1)}, f32[72,128]{1,0:T(8,128)S(1)}, u32[]{:S(2)}, u32[]{:S(2)}) %collective-permute-start.20) | collective-permute-done | bytes 36896 | tf_op jit(solution)/shard_map/ppermute | solution.py:14
  90.1 2.0 %collective-permute-start.21 = (bf16[4,2,128,128]{3,2,1,0:T(8,128)(2,1)S(1)}, bf16[4,2,128,128]{3,2,1,0:T(8,128)(2,1)S(1)}, u32[]{:S(2)}, u32[]{:S(2)}) collective-permute-start(bf16[4,2,128,128]{3,2,1,0:T(8,128)(2,1)S(1)} %get-tuple-element.199), channel_id=1, source_target_pairs={{0,2},{1,3},{2,0},{3,1},{4,6},{5,7},{6,4},{7,5},{8,10},{9,11},{10,... | collective-permute-start | bytes 786440 | tf_op jit(solution)/shard_map/ppermute | solution.py:14
  92.2 1.6 %collective-permute-start.22 = (bf16[4,2,128,128]{3,2,1,0:T(8,128)(2,1)S(1)}, bf16[4,2,128,128]{3,2,1,0:T(8,128)(2,1)S(1)}, u32[]{:S(2)}, u32[]{:S(2)}) collective-permute-start(bf16[4,2,128,128]{3,2,1,0:T(8,128)(2,1)S(1)} %get-tuple-element.198), channel_id=1, source_target_pairs={{0,1},{1,0},{2,3},{3,2},{4,5},{5,4},{6,7},{7,6},{8,9},{9,8},{10,11... | collective-permute-start | bytes 786440 | tf_op jit(solution)/shard_map/ppermute | solution.py:14
  94.9 2.8 %collective-permute-done.23 = f32[72,128]{1,0:T(8,128)S(1)} collective-permute-done((f32[72,128]{1,0:T(8,128)S(1)}, f32[72,128]{1,0:T(8,128)S(1)}, u32[]{:S(2)}, u32[]{:S(2)}) %collective-permute-start.23) | collective-permute-done | bytes 36896 | tf_op jit(solution)/shard_map/ppermute | solution.py:14
  98.4 1.7 %collective-permute-done.22 = bf16[4,2,128,128]{3,2,1,0:T(8,128)(2,1)S(1)} collective-permute-done((bf16[4,2,128,128]{3,2,1,0:T(8,128)(2,1)S(1)}, bf16[4,2,128,128]{3,2,1,0:T(8,128)(2,1)S(1)}, u32[]{:S(2)}, u32[]{:S(2)}) %collective-permute-start.22) | collective-permute-done | bytes 262176 | tf_op jit(solution)/shard_map/ppermute | solution.py:14
  100.1 1.8 %collective-permute-start.24 = (bf16[8,2,128,128]{3,2,1,0:T(8,128)(2,1)S(1)}, bf16[8,2,128,128]{3,2,1,0:T(8,128)(2,1)S(1)}, u32[]{:S(2)}, u32[]{:S(2)}) collective-permute-start(bf16[8,2,128,128]{3,2,1,0:T(8,128)(2,1)S(1)} %pad_maximum_fusion.5), channel_id=1, source_target_pairs={{0,1},{1,0},{2,3},{3,2},{4,5},{5,4},{6,7},{7,6},{8,9},{9,8},{10,11... | collective-permute-start | bytes 1572872 | tf_op jit(solution)/shard_map/ppermute | solution.py:14
  102.2 1.7 %collective-permute-start.26 = (f32[72,128]{1,0:T(8,128)S(1)}, f32[72,128]{1,0:T(8,128)S(1)}, u32[]{:S(2)}, u32[]{:S(2)}) collective-permute-start(f32[72,128]{1,0:T(8,128)S(1)} %add.905), channel_id=1, source_target_pairs={{0,2},{1,3},{2,0},{3,1},{4,6},{5,7},{6,4},{7,5},{8,10},{9,11},{10,... | collective-permute-start | bytes 110600 | tf_op jit(solution)/shard_map/ppermute | solution.py:14
  104.0 4.1 %shard_map.125.before = f32[8,128,128]{2,1,0:T(8,128)S(1)} custom-call(s32[2]{0:T(128)S(1)} %pad_add_fusion.1.meta, s32[672]{0:T(1024)S(1)} %get-tuple-element.208.src, s32[84]{0:T(128)S(1)} %and_select_fusion.owner, f32[8,128,128]{2,1,0:T(8,128)S(1)} %broadcast_in_dim.198.before, bf16[672,128,128]{2,1,0:T(8,128)(2,1)} %shard_map.124.dense, ...), custom_call_target="tpu_custom_call" | custom-call | flops 11274289152 | bytes 22020096 | tf_op jit(solution)/shard_map/pallas_call | solution.py:373
  108.1 7.1 %collective-permute-done.26 = f32[72,128]{1,0:T(8,128)S(1)} collective-permute-done((f32[72,128]{1,0:T(8,128)S(1)}, f32[72,128]{1,0:T(8,128)S(1)}, u32[]{:S(2)}, u32[]{:S(2)}) %collective-permute-start.26) | collective-permute-done | bytes 36896 | tf_op jit(solution)/shard_map/ppermute | solution.py:14
  115.2 4.6 %shard_map.126 = f32[8,128,128]{2,1,0:T(8,128)S(1)} custom-call(s32[2]{0:T(128)S(1)} %pad_add_fusion.2.meta, s32[672]{0:T(1024)S(1)} %get-tuple-element.208.src, s32[84]{0:T(128)S(1)} %and_select_fusion.owner, f32[8,128,128]{2,1,0:T(8,128)S(1)} %shard_map.125.before, bf16[672,128,128]{2,1,0:T(8,128)(2,1)} %shard_map.124.dense, ...), custom_call_target="tpu_custom_call" | custom-call | flops 11274289152 | bytes 22020096 | tf_op jit(solution)/shard_map/pallas_call | solution.py:373
  120.0 2.2 %collective-permute-start.28 = (f32[72,128]{1,0:T(8,128)S(1)}, f32[72,128]{1,0:T(8,128)S(1)}, u32[]{:S(2)}, u32[]{:S(2)}) collective-permute-start(f32[72,128]{1,0:T(8,128)S(1)} %add.906), channel_id=1, source_target_pairs={{0,1},{1,0},{2,3},{3,2},{4,5},{5,4},{6,7},{7,6},{8,9},{9,8},{10,11... | collective-permute-start | bytes 110600 | tf_op jit(solution)/shard_map/ppermute | solution.py:14
  122.2 1.9 %collective-permute-done.28 = f32[72,128]{1,0:T(8,128)S(1)} collective-permute-done((f32[72,128]{1,0:T(8,128)S(1)}, f32[72,128]{1,0:T(8,128)S(1)}, u32[]{:S(2)}, u32[]{:S(2)}) %collective-permute-start.28) | collective-permute-done | bytes 36896 | tf_op jit(solution)/shard_map/ppermute | solution.py:14
  (136 shorter events, 25.9 us)
Async XLA Ops:
  0.6 25.1 %collective-permute-start.6 = (bf16[4,128,128]{2,1,0:T(8,128)(2,1)}, bf16[4,128,128]{2,1,0:T(8,128)(2,1)S(1)}, u32[]{:S(2)}, u32[]{:S(2)}) collective-permute-start(bf16[4,128,128]{2,1,0:T(8,128)(2,1)} %bitcast.157), channel_id=1, source_target_pairs={{0,12},{1,13},{2,14},{3,15},{4,8},{5,9},{6,10},{7,11},{8,4},{9,5},... | collective-permute-start | bytes 393224 | tf_op jit(solution)/shard_map/ppermute | solution.py:14
  5.7 20.0 %collective-permute-start.5 = (bf16[4,128,128]{2,1,0:T(8,128)(2,1)}, bf16[4,128,128]{2,1,0:T(8,128)(2,1)S(1)}, u32[]{:S(2)}, u32[]{:S(2)}) collective-permute-start(bf16[4,128,128]{2,1,0:T(8,128)(2,1)} %bitcast.158), channel_id=1, source_target_pairs={{0,4},{1,5},{2,6},{3,7},{4,0},{5,1},{6,2},{7,3},{8,12},{9,13},{10,... | collective-permute-start | bytes 393224 | tf_op jit(solution)/shard_map/ppermute | solution.py:14
  5.7 20.0 %collective-permute-start.4 = (bf16[4,128,128]{2,1,0:T(8,128)(2,1)}, bf16[4,128,128]{2,1,0:T(8,128)(2,1)S(1)}, u32[]{:S(2)}, u32[]{:S(2)}) collective-permute-start(bf16[4,128,128]{2,1,0:T(8,128)(2,1)} %bitcast.159), channel_id=1, source_target_pairs={{0,8},{1,9},{2,10},{3,11},{4,12},{5,13},{6,14},{7,15},{8,0},{9,1},... | collective-permute-start | bytes 393224 | tf_op jit(solution)/shard_map/ppermute | solution.py:14
  13.3 27.6 %all-to-all-start = ((s32[16,72,128]{2,1,0:T(8,128)}), s32[16,72,128]{2,1,0:T(8,128)S(1)}, u32[]{:S(2)}, u32[]{:S(2)}) async-start(s32[16,72,128]{2,1,0:T(8,128)} %bitcast.29), calls=%async_computation | async-start | bytes 1179648 | tf_op jit(solution)/shard_map/all_to_all | solution.py:509
  26.8 9.7 %collective-permute-start.7 = (bf16[4,2,128,128]{3,2,1,0:T(8,128)(2,1)S(1)}, bf16[4,2,128,128]{3,2,1,0:T(8,128)(2,1)S(1)}, u32[]{:S(2)}, u32[]{:S(2)}) collective-permute-start(bf16[4,2,128,128]{3,2,1,0:T(8,128)(2,1)S(1)} %get-tuple-element.201), channel_id=1, source_target_pairs={{0,2},{1,3},{2,0},{3,1},{4,6},{5,7},{6,4},{7,5},{8,10},{9,11},{10,... | collective-permute-start | bytes 786440 | tf_op jit(solution)/shard_map/ppermute | solution.py:14
  28.8 9.1 %collective-permute-start.8 = (bf16[4,2,128,128]{3,2,1,0:T(8,128)(2,1)S(1)}, bf16[4,2,128,128]{3,2,1,0:T(8,128)(2,1)S(1)}, u32[]{:S(2)}, u32[]{:S(2)}) collective-permute-start(bf16[4,2,128,128]{3,2,1,0:T(8,128)(2,1)S(1)} %get-tuple-element.200), channel_id=1, source_target_pairs={{0,1},{1,0},{2,3},{3,2},{4,5},{5,4},{6,7},{7,6},{8,9},{9,8},{10,11... | collective-permute-start | bytes 786440 | tf_op jit(solution)/shard_map/ppermute | solution.py:14
  37.9 20.9 %collective-permute-start.9 = (bf16[8,2,128,128]{3,2,1,0:T(8,128)(2,1)S(1)}, bf16[8,2,128,128]{3,2,1,0:T(8,128)(2,1)S(1)}, u32[]{:S(2)}, u32[]{:S(2)}) collective-permute-start(bf16[8,2,128,128]{3,2,1,0:T(8,128)(2,1)S(1)} %pad_maximum_fusion.2), channel_id=1, source_target_pairs={{0,1},{1,0},{2,3},{3,2},{4,5},{5,4},{6,7},{7,6},{8,9},{9,8},{10,11... | collective-permute-start | bytes 1572872 | tf_op jit(solution)/shard_map/ppermute | solution.py:14
  40.4 18.4 %collective-permute-start.10 = (bf16[8,2,128,128]{3,2,1,0:T(8,128)(2,1)S(1)}, bf16[8,2,128,128]{3,2,1,0:T(8,128)(2,1)S(1)}, u32[]{:S(2)}, u32[]{:S(2)}) collective-permute-start(bf16[8,2,128,128]{3,2,1,0:T(8,128)(2,1)S(1)} %pad_maximum_fusion.3), channel_id=1, source_target_pairs={{0,2},{1,3},{2,0},{3,1},{4,6},{5,7},{6,4},{7,5},{8,10},{9,11},{10,... | collective-permute-start | bytes 1572872 | tf_op jit(solution)/shard_map/ppermute | solution.py:14
  40.4 20.3 %collective-permute-start.12 = (bf16[16,128,128]{2,1,0:T(8,128)(2,1)S(1)}, bf16[16,128,128]{2,1,0:T(8,128)(2,1)S(1)}, u32[]{:S(2)}, u32[]{:S(2)}) collective-permute-start(bf16[16,128,128]{2,1,0:T(8,128)(2,1)S(1)} %bitcast.136), channel_id=1, source_target_pairs={{0,16},{16,0},{1,17},{17,1},{2,18},{18,2},{3,19},{19,3},{4,20},{20... | collective-permute-start | bytes 1572872 | tf_op jit(solution)/shard_map/ppermute | solution.py:14
  40.4 20.3 %collective-permute-start.14 = (bf16[16,128,128]{2,1,0:T(8,128)(2,1)S(1)}, bf16[16,128,128]{2,1,0:T(8,128)(2,1)}, u32[]{:S(2)}, u32[]{:S(2)}) collective-permute-start(bf16[16,128,128]{2,1,0:T(8,128)(2,1)S(1)} %bitcast.138), channel_id=1, source_target_pairs={{0,16},{16,0},{1,17},{17,1},{2,18},{18,2},{3,19},{19,3},{4,20},{20... | collective-permute-start | bytes 1572872 | tf_op jit(solution)/shard_map/ppermute | solution.py:14
  46.3 11.2 %collective-permute-start.11 = (s32[1,64]{1,0:T(1,128)}, s32[1,64]{1,0:T(1,128)S(1)}, u32[]{:S(2)}, u32[]{:S(2)}) collective-permute-start(s32[1,64]{1,0:T(1,128)} %bitcast.32), channel_id=1, source_target_pairs={{0,16},{16,0},{1,17},{17,1},{2,18},{18,2},{3,19},{19,3},{4,20},{20... | collective-permute-start | bytes 776 | tf_op jit(solution)/shard_map/ppermute | solution.py:14
  58.8 2.7 %collective-permute-start.15 = (bf16[16,128,128]{2,1,0:T(8,128)(2,1)S(1)}, bf16[16,128,128]{2,1,0:T(8,128)(2,1)S(1)}, u32[]{:S(2)}, u32[]{:S(2)}) collective-permute-start(bf16[16,128,128]{2,1,0:T(8,128)(2,1)S(1)} %bitcast.145), channel_id=1, source_target_pairs={{0,16},{16,0},{1,17},{17,1},{2,18},{18,2},{3,19},{19,3},{4,20},{20... | collective-permute-start | bytes 1572872 | tf_op jit(solution)/shard_map/ppermute | solution.py:14
  73.1 4.6 %collective-permute-start.19 = (f32[1,72,128]{2,1,0:T(8,128)S(1)}, f32[1,72,128]{2,1,0:T(8,128)S(1)}, u32[]{:S(2)}, u32[]{:S(2)}) collective-permute-start(f32[1,72,128]{2,1,0:T(8,128)S(1)} %slice_bitcast_fusion.10), channel_id=1, source_target_pairs={{0,16},{16,0},{1,17},{17,1},{2,18},{18,2},{3,19},{19,3},{4,20},{20... | collective-permute-start | bytes 110600 | tf_op jit(solution)/shard_map/ppermute | solution.py:14
  73.2 15.8 %collective-permute-start.18 = (bf16[4,128,128]{2,1,0:T(8,128)(2,1)}, bf16[4,128,128]{2,1,0:T(8,128)(2,1)S(1)}, u32[]{:S(2)}, u32[]{:S(2)}) collective-permute-start(bf16[4,128,128]{2,1,0:T(8,128)(2,1)} %get-tuple-element.177.refs_0_), channel_id=1, source_target_pairs={{0,12},{1,13},{2,14},{3,15},{4,8},{5,9},{6,10},{7,11},{8,4},{9,5},... | collective-permute-start | bytes 393224 | tf_op jit(solution)/shard_map/ppermute | solution.py:14
  74.7 14.3 %collective-permute-start.17 = (bf16[4,128,128]{2,1,0:T(8,128)(2,1)}, bf16[4,128,128]{2,1,0:T(8,128)(2,1)S(1)}, u32[]{:S(2)}, u32[]{:S(2)}) collective-permute-start(bf16[4,128,128]{2,1,0:T(8,128)(2,1)} %get-tuple-element.177.refs_0_), channel_id=1, source_target_pairs={{0,4},{1,5},{2,6},{3,7},{4,0},{5,1},{6,2},{7,3},{8,12},{9,13},{10,... | collective-permute-start | bytes 393224 | tf_op jit(solution)/shard_map/ppermute | solution.py:14
  75.2 13.8 %collective-permute-start.16 = (bf16[4,128,128]{2,1,0:T(8,128)(2,1)}, bf16[4,128,128]{2,1,0:T(8,128)(2,1)S(1)}, u32[]{:S(2)}, u32[]{:S(2)}) collective-permute-start(bf16[4,128,128]{2,1,0:T(8,128)(2,1)} %get-tuple-element.177.refs_0_), channel_id=1, source_target_pairs={{0,8},{1,9},{2,10},{3,11},{4,12},{5,13},{6,14},{7,15},{8,0},{9,1},... | collective-permute-start | bytes 393224 | tf_op jit(solution)/shard_map/ppermute | solution.py:14
  77.7 11.4 %collective-permute-start.20 = (f32[72,128]{1,0:T(8,128)S(1)}, f32[72,128]{1,0:T(8,128)S(1)}, u32[]{:S(2)}, u32[]{:S(2)}) collective-permute-start(f32[72,128]{1,0:T(8,128)S(1)} %fusion.26), channel_id=1, source_target_pairs={{0,8},{1,9},{2,10},{3,11},{4,12},{5,13},{6,14},{7,15},{8,0},{9,1},... | collective-permute-start | bytes 110600 | tf_op jit(solution)/shard_map/ppermute | solution.py:14
  90.1 8.2 %collective-permute-start.21 = (bf16[4,2,128,128]{3,2,1,0:T(8,128)(2,1)S(1)}, bf16[4,2,128,128]{3,2,1,0:T(8,128)(2,1)S(1)}, u32[]{:S(2)}, u32[]{:S(2)}) collective-permute-start(bf16[4,2,128,128]{3,2,1,0:T(8,128)(2,1)S(1)} %get-tuple-element.199), channel_id=1, source_target_pairs={{0,2},{1,3},{2,0},{3,1},{4,6},{5,7},{6,4},{7,5},{8,10},{9,11},{10,... | collective-permute-start | bytes 786440 | tf_op jit(solution)/shard_map/ppermute | solution.py:14
  92.2 7.9 %collective-permute-start.22 = (bf16[4,2,128,128]{3,2,1,0:T(8,128)(2,1)S(1)}, bf16[4,2,128,128]{3,2,1,0:T(8,128)(2,1)S(1)}, u32[]{:S(2)}, u32[]{:S(2)}) collective-permute-start(bf16[4,2,128,128]{3,2,1,0:T(8,128)(2,1)S(1)} %get-tuple-element.198), channel_id=1, source_target_pairs={{0,1},{1,0},{2,3},{3,2},{4,5},{5,4},{6,7},{7,6},{8,9},{9,8},{10,11... | collective-permute-start | bytes 786440 | tf_op jit(solution)/shard_map/ppermute | solution.py:14
  93.8 4.0 %collective-permute-start.23 = (f32[72,128]{1,0:T(8,128)S(1)}, f32[72,128]{1,0:T(8,128)S(1)}, u32[]{:S(2)}, u32[]{:S(2)}) collective-permute-start(f32[72,128]{1,0:T(8,128)S(1)} %add.904), channel_id=1, source_target_pairs={{0,4},{1,5},{2,6},{3,7},{4,0},{5,1},{6,2},{7,3},{8,12},{9,13},{10,... | collective-permute-start | bytes 110600 | tf_op jit(solution)/shard_map/ppermute | solution.py:14
  100.1 15.1 %collective-permute-start.24 = (bf16[8,2,128,128]{3,2,1,0:T(8,128)(2,1)S(1)}, bf16[8,2,128,128]{3,2,1,0:T(8,128)(2,1)S(1)}, u32[]{:S(2)}, u32[]{:S(2)}) collective-permute-start(bf16[8,2,128,128]{3,2,1,0:T(8,128)(2,1)S(1)} %pad_maximum_fusion.5), channel_id=1, source_target_pairs={{0,1},{1,0},{2,3},{3,2},{4,5},{5,4},{6,7},{7,6},{8,9},{9,8},{10,11... | collective-permute-start | bytes 1572872 | tf_op jit(solution)/shard_map/ppermute | solution.py:14
  101.9 13.3 %collective-permute-start.25 = (bf16[8,2,128,128]{3,2,1,0:T(8,128)(2,1)S(1)}, bf16[8,2,128,128]{3,2,1,0:T(8,128)(2,1)S(1)}, u32[]{:S(2)}, u32[]{:S(2)}) collective-permute-start(bf16[8,2,128,128]{3,2,1,0:T(8,128)(2,1)S(1)} %pad_maximum_fusion.6), channel_id=1, source_target_pairs={{0,2},{1,3},{2,0},{3,1},{4,6},{5,7},{6,4},{7,5},{8,10},{9,11},{10,... | collective-permute-start | bytes 1572872 | tf_op jit(solution)/shard_map/ppermute | solution.py:14
  102.2 13.0 %collective-permute-start.26 = (f32[72,128]{1,0:T(8,128)S(1)}, f32[72,128]{1,0:T(8,128)S(1)}, u32[]{:S(2)}, u32[]{:S(2)}) collective-permute-start(f32[72,128]{1,0:T(8,128)S(1)} %add.905), channel_id=1, source_target_pairs={{0,2},{1,3},{2,0},{3,1},{4,6},{5,7},{6,4},{7,5},{8,10},{9,11},{10,... | collective-permute-start | bytes 110600 | tf_op jit(solution)/shard_map/ppermute | solution.py:14
  120.0 4.1 %collective-permute-start.28 = (f32[72,128]{1,0:T(8,128)S(1)}, f32[72,128]{1,0:T(8,128)S(1)}, u32[]{:S(2)}, u32[]{:S(2)}) collective-permute-start(f32[72,128]{1,0:T(8,128)S(1)} %add.906), channel_id=1, source_target_pairs={{0,1},{1,0},{2,3},{3,2},{4,5},{5,4},{6,7},{7,6},{8,9},{9,8},{10,11... | collective-permute-start | bytes 110600 | tf_op jit(solution)/shard_map/ppermute | solution.py:14
  (11 other events, 111.3 us)

commit v3 on v2

--- a/solution.py
+++ b/solution.py
@@ -126,9 +126,9 @@
     lax.fori_loop(0, meta[0], turn, 0)
 
 
-def build_kernel(meta, order, codes, *refs):
+def build_kernel(span, marks, lists, codes, *refs):
     dense, dbuf, sems = refs[-3:]
-    start, turns = meta[0], meta[1]
+    start, turns = marks[0, span[0]], marks[0, span[1]]
     rows = tile_rows()
 
     def out_copy(i):
@@ -144,7 +144,7 @@
         def _():
             out_copy(i - DEPTH).wait()
 
-        lines = [codes[pl.ds(order[i * TURN + u], 1), :] for u in range(TURN)]
+        lines = [codes[pl.ds(lists[0, i * TURN + u], 1), :] for u in range(TURN)]
         for u in range(0, TURN, GROUP):
             blocks = [block_of(line, rows) for line in lines[u : u + GROUP]]
             for k, block in enumerate(blocks):
@@ -203,10 +203,10 @@
     for g in range(0, groups, 2):
         added = [one(g), one(g + 1)]
         for k in range(2):
-            into[owner[i * groups + g + k]] += added[k]
-
-
-def forward_kernel(n, scale, meta, col, owner, weight, bias, cotangent, dense, *refs):
+            into[owner[0, i * groups + g + k]] += added[k]
+
+
+def forward_kernel(n, scale, span, marks, lists, owner, weight, bias, cotangent, dense, *refs):
     pieces, refs = refs[:n], refs[n:]
     output, turned, local, totals, feat, proj, dbuf, piece_sems, sems = refs
     copies = fetch(pieces, feat, piece_sems)
@@ -228,7 +228,7 @@
 
     def product(i, slot):
         def one(g):
-            spots = [col[i * TURN + g * GROUP + u] for u in range(GROUP)]
+            spots = [lists[1, i * TURN + g * GROUP + u] for u in range(GROUP)]
             left = jnp.concatenate([dbuf[slot, g * GROUP + u] for u in range(GROUP)], axis=1)
             right = jnp.concatenate(
                 [jnp.concatenate([proj[c], feat[c]], axis=1) for c in spots], axis=0
@@ -237,7 +237,7 @@
 
         add_pairs(i, owner, one, totals)
 
-    read_dense(meta[0], meta[1], dense, dbuf, sems, product, prepare)
+    read_dense(marks[0, span[0]], marks[0, span[1]], dense, dbuf, sems, product, prepare)
 
     weight_sum, bias_sum = 0.0, 0.0
     for q in range(totals.shape[0]):
@@ -271,7 +271,7 @@
     lax.fori_loop(0, meta[0], turn, 0)
 
 
-def backward_kernel(n, meta, src, owner, before, dense, *refs):
+def backward_kernel(n, span, marks, lists, owner, before, dense, *refs):
     pieces, (acc, grad, dbuf, piece_sems, sems) = refs[:n], refs[n:]
     copies = fetch(pieces, grad, piece_sems)
 
@@ -282,14 +282,14 @@
 
     def product(i, slot):
         def one(g):
-            spots = [src[i * TURN + g * GROUP + u] for u in range(GROUP)]
+            spots = [lists[1, i * TURN + g * GROUP + u] for u in range(GROUP)]
             left = jnp.concatenate([grad[c] for c in spots], axis=1)
             right = dbuf[slot, pl.ds(g * GROUP, GROUP)].reshape(GROUP * 128, 128)
             return jnp.dot(left, right, preferred_element_type=jnp.float32)
 
         add_pairs(i, owner, one, acc)
 
-    read_dense(meta[0], meta[1], dense, dbuf, sems, product, prepare)
+    read_dense(marks[0, span[0]], marks[0, span[1]], dense, dbuf, sems, product, prepare)
 
 
 SMEM = pl.BlockSpec(memory_space=pltpu.SMEM)
@@ -324,11 +324,12 @@
     )(meta, pos, codes, labels)
 
 
-def run_build(meta, order, codes, after, dense):
+def run_build(span, listed, codes, after, dense):
+    lists, _, marks = listed
     others = after if dense is None else after + [dense]
     return pl.pallas_call(
-        build_kernel,
-        out_shape=jax.ShapeDtypeStruct((order.shape[0], 128, 128), jnp.bfloat16),
+        functools.partial(build_kernel, span),
+        out_shape=jax.ShapeDtypeStruct((lists.shape[1], 128, 128), jnp.bfloat16),
         in_specs=[SMEM] * 2 + [VMEM] + [HBM] * len(others),
         out_specs=HBM,
         scratch_shapes=[
@@ -337,16 +338,17 @@
         ],
         input_output_aliases={} if dense is None else {2 + len(others): 0},
         compiler_params=PARAMS,
-        cost_estimate=cost(order.shape[0], 2),
-    )(meta, order, codes, *others)
-
-
-def run_forward(scale, meta, col, owner, weight, bias, cotangent, dense, feat):
+        cost_estimate=cost(lists.shape[1], 2),
+    )(marks, lists, codes, *others)
+
+
+def run_forward(scale, span, listed, weight, bias, cotangent, dense, feat):
+    lists, owner, marks = listed
     n = len(feat)
     size, _, width = feat[0].shape
     row_blocks = cotangent.shape[0] // 128
     return pl.pallas_call(
-        functools.partial(forward_kernel, n, scale),
+        functools.partial(forward_kernel, n, scale, span),
         out_shape=(
             jax.ShapeDtypeStruct(cotangent.shape, jnp.bfloat16),
             jax.ShapeDtypeStruct((row_blocks, width, 128), jnp.bfloat16),
@@ -363,15 +365,16 @@
             pltpu.SemaphoreType.DMA((DEPTH,)),
         ],
         compiler_params=PARAMS,
-        cost_estimate=cost(col.shape[0], 4),
-    )(meta, col, owner, weight, bias, cotangent, dense, *feat)
-
-
-def run_backward(meta, src, owner, before, dense, pieces):
+        cost_estimate=cost(lists.shape[1], 4),
+    )(marks, lists, owner, weight, bias, cotangent, dense, *feat)
+
+
+def run_backward(span, listed, before, dense, pieces):
+    lists, owner, marks = listed
     n = len(pieces)
     size, width, _ = pieces[0].shape
     return pl.pallas_call(
-        functools.partial(backward_kernel, n),
+        functools.partial(backward_kernel, n, span),
         out_shape=jax.ShapeDtypeStruct(before.shape, jnp.float32),
         in_specs=[SMEM] * 3 + [VMEM] + [HBM] * (n + 1),
         out_specs=VMEM,
@@ -382,29 +385,85 @@
             pltpu.SemaphoreType.DMA((DEPTH,)),
         ],
         compiler_params=PARAMS,
-        cost_estimate=cost(src.shape[0], 4),
-    )(meta, src, owner, before, dense, *pieces)
-
-
-def grouped(key, live, value, fill, keys, split):
-    ids = jnp.arange(key.shape[0], dtype=jnp.int32)
-    names = jnp.arange(keys, dtype=jnp.int32)
-    key = jnp.where(live, key, keys)
-    before = (key[:, None] == key[None, :]) & (ids[:, None] < ids[None, :])
-    rank = jnp.sum(before.astype(jnp.int32), axis=0)
-    counts = jnp.sum((key[:, None] == names[None, :]).astype(jnp.int32), axis=0)
-    filled = (counts + GROUP - 1) // GROUP * GROUP
-    below = jnp.sum(jnp.where(names < split, filled, 0))
-    first_turns = (below + TURN - 1) // TURN
-    filled = filled + jnp.where(names == split - 1, first_turns * TURN - below, 0)
-    base = jnp.sum(jnp.where(names[:, None] < key[None, :], filled[:, None], 0), axis=0)
-    pos = jnp.where(live, base + rank, -1)
-    ends = jnp.sum(jnp.where(names[:, None] <= names[None, :], filled[:, None], 0), axis=0)
-    length = (-(-(key.shape[0] + keys * GROUP) // TURN) + 1) * TURN
-    first = jnp.arange(length // GROUP, dtype=jnp.int32) * GROUP
-    group_key = jnp.sum((ends[:, None] <= first[None, :]).astype(jnp.int32), axis=0)
-    turns = (jnp.sum(filled) + TURN - 1) // TURN
-    return place(pos, value, length, fill), jnp.minimum(group_key, keys - 1), turns, first_turns
+        cost_estimate=cost(lists.shape[1], 4),
+    )(marks, lists, owner, before, dense, *pieces)
+
+
+def column(row):
+    return jnp.broadcast_to(row, (8, row.shape[1])).T[:, :1]
+
+
+def list_kernel(keys, split, fills, key_ref, *refs):
+    value_refs, (lists, owner_ref, marks_ref) = refs[: len(fills)], refs[len(fills) :]
+    n, length = key_ref.shape[1], lists.shape[1]
+    key = key_ref[...].astype(jnp.float32)
+    key_column = column(key)
+    lanes = lax.broadcasted_iota(jnp.int32, (128, n), 1)
+    lines = lax.broadcasted_iota(jnp.int32, (128, n), 0)
+    rank = jnp.zeros((1, n), jnp.float32)
+    for t in range(0, n, 128):
+        before = (key_column[t : t + 128] == key) & (lines + t < lanes)
+        rank += jnp.sum(jnp.where(before, 1.0, 0.0), axis=0, keepdims=True)
+
+    rows = -(-keys // 8) * 8
+    names = lax.broadcasted_iota(jnp.int32, (rows, n), 0).astype(jnp.float32)
+    name = lax.broadcasted_iota(jnp.int32, (rows, 1), 0).astype(jnp.float32)
+    counts = jnp.sum(jnp.where(names == key, 1.0, 0.0), axis=1, keepdims=True)
+    filled = jnp.where(name < keys, jnp.floor((counts + (GROUP - 1)) * (1.0 / GROUP)) * GROUP, 0.0)
+    below = jnp.sum(jnp.where(name < split, filled, 0.0), axis=0, keepdims=True)
+    first = jnp.floor((below + (TURN - 1)) * (1.0 / TURN))
+    filled = filled + jnp.where(name == split - 1, first * TURN - below, 0.0)
+    turns = jnp.floor((jnp.sum(filled, axis=0, keepdims=True) + (TURN - 1)) * (1.0 / TURN))
+    base = jnp.sum(jnp.where(names < key, filled, 0.0), axis=0, keepdims=True)
+    pos_column = column(jnp.where(key < keys, base + rank, -1.0))
+
+    spots = lax.broadcasted_iota(jnp.int32, (1, length), 1).astype(jnp.float32)
+    columns = [column(ref[...].astype(jnp.float32)) for ref in value_refs]
+    sums = [jnp.zeros((1, length), jnp.float32) for _ in fills]
+    for t in range(0, n, 128):
+        hit = pos_column[t : t + 128] == spots
+        for k, fill in enumerate(fills):
+            value = columns[k][t : t + 128] - fill
+            sums[k] += jnp.sum(jnp.where(hit, value, 0.0), axis=0, keepdims=True)
+    for k, fill in enumerate(fills):
+        lists[pl.ds(k, 1), :] = (sums[k] + fill).astype(jnp.int32)
+
+    other = lax.broadcasted_iota(jnp.int32, (rows, 128), 1).astype(jnp.float32)
+    ends = column(jnp.sum(jnp.where(name <= other, filled, 0.0), axis=0, keepdims=True))[:rows]
+    starts = lax.broadcasted_iota(jnp.int32, owner_ref.shape, 1).astype(jnp.float32) * GROUP
+    passed = (ends <= starts) & (name < keys)
+    owner = jnp.sum(jnp.where(passed, 1.0, 0.0), axis=0, keepdims=True)
+    owner = jnp.minimum(owner, keys - 1.0)
+    owner_ref[...] = jnp.where(owner >= split, owner - split, owner).astype(jnp.int32)
+
+    spot = lax.broadcasted_iota(jnp.int32, (1, 128), 1)
+    marks = jnp.where(spot == FIRST, first, 0.0)
+    for k in range(1, 5):
+        marks = jnp.where(spot == FIRST + k, jnp.floor(turns * (k / 4)), marks)
+    marks_ref[...] = marks.astype(jnp.int32)
+
+
+FIRST = 1
+QUARTERS = [0, 2, 3, 4, 5]
+
+
+def make_lists(key, values, fills, keys, split):
+    n = key.size
+    length = (-(-(n + keys * GROUP) // TURN) + 1) * TURN
+    groups = -(-length // GROUP // 128) * 128
+    lists, owner, marks = pl.pallas_call(
+        functools.partial(list_kernel, keys, split, fills),
+        out_shape=(
+            jax.ShapeDtypeStruct((len(fills), length), jnp.int32),
+            jax.ShapeDtypeStruct((1, groups), jnp.int32),
+            jax.ShapeDtypeStruct((1, 128), jnp.int32),
+        ),
+        in_specs=[VMEM] * (1 + len(fills)),
+        out_specs=[VMEM] * 3,
+        compiler_params=PARAMS,
+        cost_estimate=cost(32, 2),
+    )(key.reshape(1, n), *[value.reshape(1, n) for value in values])
+    return lists, owner, marks
 
 
 def place(pos, value, length, fill):
@@ -473,25 +532,18 @@
     unit = row_blocks // (2 * len(part_orders(per)))
     late = source // unit % 2
     source = source // (2 * unit) * unit + source % unit
-    back_list, back_owner, back_turns, early_turns = grouped(
-        late * col_blocks + bcol,
-        live,
-        ids * FIELD + source,
-        slots * FIELD,
+    back = make_lists(
+        jnp.where(live, late * col_blocks + bcol, 2 * col_blocks),
+        [ids, source],
+        [slots, 0],
         2 * col_blocks,
         col_blocks,
     )
-    back_owner = back_owner % col_blocks
-    spans = [
-        jnp.stack([jnp.zeros_like(early_turns), early_turns]),
-        jnp.stack([early_turns, back_turns]),
-    ]
     state = {"dense": None}
 
-    def build(held, half):
-        state["dense"] = run_build(
-            spans[half], back_list // FIELD, codes, held, state["dense"]
-        )
+    def build(held, start, end):
+        span = (QUARTERS[start], QUARTERS[end])
+        state["dense"] = run_build(span, back, codes, held, state["dense"])
 
     if by_owner:
         same = live[:, None] & (home[:, None] == home[None, :]) & (ids[:, None] < ids[None, :])
@@ -523,26 +575,24 @@
             per, sources ^ mine, col_there % per, (col_there // per) ^ mine_row, n_row
         )
         line = sources * stride + places
-        listed, owner, turns, _ = grouped(
-            row_here,
-            (got > 0).reshape(-1),
-            (line * FIELD + col_there).reshape(-1),
-            (ROOM + 1) * FIELD,
+        listed = make_lists(
+            jnp.where(got > 0, row_here.reshape(got.shape), per),
+            [jnp.broadcast_to(line, got.shape), col_there],
+            [ROOM + 1, 0],
             per,
             per,
         )
-        span = jnp.stack([jnp.zeros_like(turns), turns])
 
         def prepare(step, held):
             if step == 0:
-                build(held, 0)
+                build(held, 0, 1)
             if step == 1:
                 held, state["dense"] = lax.optimization_barrier((held, state["dense"]))
             return held
 
         pairs = gather_pieces(features.reshape(per, 128, width), prepare)
         lines = came.reshape(n_col * stride, 128)
-        here = run_build(span, listed // FIELD, lines, [], None)
+        here = run_build((0, QUARTERS[4]), listed, lines, [], None)
         last, here, any_over = lax.optimization_barrier(
             ([pair[1] for pair in pairs], here, any_over)
         )
@@ -553,7 +603,7 @@
                 rows = rows + [[swap(x, "row", bit) for x in pair] for pair in rows]
             feat += [x for pair in rows for x in pair]
         done = run_forward(
-            scale, span, listed % FIELD, owner, weight, bias[None], cotangent, here, feat
+            scale, (0, QUARTERS[4]), listed, weight, bias[None], cotangent, here, feat
         )
         done = lax.cond(any_over[0] > 0, tile_plan, lambda: tuple(done))
     else:
@@ -572,6 +622,8 @@
         )
         if steps:
             add_total()
+        if step == 0:
+            build(held, 3, 4)
         if step == 1:
             add_products(0, held)
         return held
@@ -579,23 +631,23 @@
     def add_products(half, pieces):
         pieces = [x.reshape((-1,) + x.shape[2:]) if x.ndim == 4 else x for x in pieces]
         state["acc"] = run_backward(
-            spans[half], back_list % FIELD, back_owner, state["acc"], state["dense"], pieces
+            [(0, FIRST), (FIRST, QUARTERS[4])][half], back, state["acc"], state["dense"], pieces
         )
 
     state["acc"] = jnp.zeros((col_blocks, width, 128), jnp.float32)
     state["total"] = split_rows(total)
     while len(steps) > 3:
         add_total()
-    build([turned], 1)
+    build([turned], 1, 3)
     grad = gather_pieces(turned, beside)
     late_pieces, state["total"] = lax.optimization_barrier(
         ([pair[1] for pair in grad], state["total"])
     )
     while steps:
         add_total()
-    total = join_rows(state["total"])
     add_products(1, late_pieces)
-    acc = state["acc"]
+    acc, total = lax.optimization_barrier((state["acc"], state["total"]))
+    total = join_rows(total)
     back = jnp.swapaxes(acc, 1, 2).reshape(col_blocks * 128, width)
     grad_proj = scatter_sum(
         jnp.stack(

time: 126 us -> 116 us (0.921); the launches traced: 127 us -> 115 us
  Pallas kernels: 45.9 us -> 36.1 us
  other arithmetic: 14.7 us -> 8.59 us
  waiting for transfers between devices: 20.8 us -> 26.7 us
  between operations: 7.08 us -> 3.05 us
    pallas_call x6 -> x9, Pallas kernels: 44.2 us -> 34.6 us  [the longest x4 16.2 us: run_build(): pl.pallas_call(functools.partial(build_kernel, span), out_shape=jax.Shape...]
    ppermute x26, waiting for transfers between devices: 20.8 us -> 26.7 us  [swap(): return lax.ppermute(x, axis, [(i, i ^ bit) for i in range(n)])]
    reduce_sum x14 -> x0, other arithmetic: 4.48 us -> none  [the longest x2 1.29 us: grouped(): below = jnp.sum(jnp.where(names < split, filled, 0))]
    add x0 -> x3, other arithmetic: none -> 1.57 us  [the longest x1 0.78 us: shards(): source = source // (2 * unit) * unit + source % unit]
  transfers between devices with their start and end apart: 27 -> 27, of which waited for: 10 -> 10; matrix products, arithmetic and copies ran while one was open for 12% -> 8% of each run, Pallas kernels for 23% -> 23%
where the time goes in v3:
time: 116 us; the launch traced here: 115 us
  starting transfers between devices  37.2 us (32%)
  Pallas kernels  36.1 us (31%)
  waiting for transfers between devices  26.7 us (23%)
  other arithmetic  8.59 us (7%)
  between operations  3.05 us (3%)
  local copies, waits for them, and re-layouts  2.46 us (2%)
    ppermute x26, starting transfers between devices, swap(): return lax.ppermute(x, axis, [(i, i ^ bit) for i in range(n)])  30.2 us
    ppermute x26, waiting for transfers between devices, swap(): return lax.ppermute(x, axis, [(i, i ^ bit) for i in range(n)])  26.7 us
    pallas_call x4, Pallas kernels, run_build(): pl.pallas_call(functools.partial(build_kernel, span), out_shape=jax.Shape...  16.2 us
    pallas_call x1, Pallas kernels, run_forward(): pl.pallas_call(functools.partial(forward_kernel, n, scale, span), out_sha...  9.36 us
    all_to_all x1, starting transfers between devices, shards(): lax.all_to_all(packed.reshape(n_col, stride, 128), 'col', split_axis=0, c...  7.01 us
    pallas_call x2, Pallas kernels, run_backward(): pl.pallas_call(functools.partial(backward_kernel, n, span), out_shape=jax...  5.75 us
    pallas_call x2, Pallas kernels, make_lists(): pl.pallas_call(functools.partial(list_kernel, keys, split, fills), out_sh...  3.31 us
  transfers between devices with their start and end apart: 27, of which 10 were waited for; matrix products, arithmetic and copies ran while one was open for 8% of the time, Pallas kernels for 23%

profile of v3, /device:TPU:0, one launch (start us, length us, event | category | flops | bytes accessed | tf_op | source)
XLA Modules:
  0.0 115.2 jit_solution(7622728118944533932)
XLA Ops:
  0.6 5.1 %collective-permute-start.6 = (bf16[4,128,128]{2,1,0:T(8,128)(2,1)}, bf16[4,128,128]{2,1,0:T(8,128)(2,1)S(1)}, u32[]{:S(2)}, u32[]{:S(2)}) collective-permute-start(bf16[4,128,128]{2,1,0:T(8,128)(2,1)} %bitcast.170), channel_id=1, source_target_pairs={{0,12},{1,13},{2,14},{3,15},{4,8},{5,9},{6,10},{7,11},{8,4},{9,5},... | collective-permute-start | bytes 393224 | tf_op jit(solution)/shard_map/ppermute | solution.py:14
  10.8 1.5 %shard_map.122 = s32[1152,128]{1,0:T(8,128)} custom-call(s32[1]{0:T(128)} %bitcast.27.meta, s32[512]{0:T(512)S(1)} %get-tuple-element.216.pos, s32[520,128]{1,0:T(8,128)S(1)} %pad.13.codes, s32[16,128]{1,0:T(8,128)S(1)} %concatenate.26.labels), custom_call_target="tpu_custom_call" | custom-call | tf_op jit(solution)/shard_map/pallas_call | solution.py:318
  12.3 7.0 %all-to-all-start = ((s32[16,72,128]{2,1,0:T(8,128)}), s32[16,72,128]{2,1,0:T(8,128)S(1)}, u32[]{:S(2)}, u32[]{:S(2)}) async-start(s32[16,72,128]{2,1,0:T(8,128)} %bitcast.30), calls=%async_computation | async-start | bytes 1179648 | tf_op jit(solution)/shard_map/all_to_all | solution.py:561
  22.9 2.0 %collective-permute-start.7 = (bf16[4,2,128,128]{3,2,1,0:T(8,128)(2,1)S(1)}, bf16[4,2,128,128]{3,2,1,0:T(8,128)(2,1)S(1)}, u32[]{:S(2)}, u32[]{:S(2)}) collective-permute-start(bf16[4,2,128,128]{3,2,1,0:T(8,128)(2,1)S(1)} %get-tuple-element.208), channel_id=1, source_target_pairs={{0,2},{1,3},{2,0},{3,1},{4,6},{5,7},{6,4},{7,5},{8,10},{9,11},{10,... | collective-permute-start | bytes 786440 | tf_op jit(solution)/shard_map/ppermute | solution.py:14
  24.8 1.5 %collective-permute-start.8 = (bf16[4,2,128,128]{3,2,1,0:T(8,128)(2,1)S(1)}, bf16[4,2,128,128]{3,2,1,0:T(8,128)(2,1)S(1)}, u32[]{:S(2)}, u32[]{:S(2)}) collective-permute-start(bf16[4,2,128,128]{3,2,1,0:T(8,128)(2,1)S(1)} %get-tuple-element.207), channel_id=1, source_target_pairs={{0,1},{1,0},{2,3},{3,2},{4,5},{5,4},{6,7},{7,6},{8,9},{9,8},{10,11... | collective-permute-start | bytes 786440 | tf_op jit(solution)/shard_map/ppermute | solution.py:14
  26.3 2.5 %shard_map.121.refs_1_ = bf16[672,128,128]{2,1,0:T(8,128)(2,1)} custom-call(s32[1,128]{1,0:T(1,128)S(1)} %get-tuple-element.84.marks, s32[2,672]{1,0:T(2,128)S(1)} %get-tuple-element.85.lists, s32[520,128]{1,0:T(8,128)S(1)} %pad.13.codes, bf16[4,4,128,128]{3,2,1,0:T(8,128)(2,1)S(1)} %pad_maximum_fusion.1.refs_0_), custom_call_target="tpu_custom_call" | custom-call | flops 5637144576 | bytes 22020096 | tf_op jit(solution)/shard_map/pallas_call | solution.py:330
  28.8 4.5 %collective-permute-done.7 = bf16[4,2,128,128]{3,2,1,0:T(8,128)(2,1)S(1)} collective-permute-done((bf16[4,2,128,128]{3,2,1,0:T(8,128)(2,1)S(1)}, bf16[4,2,128,128]{3,2,1,0:T(8,128)(2,1)S(1)}, u32[]{:S(2)}, u32[]{:S(2)}) %collective-permute-start.7) | collective-permute-done | bytes 262176 | tf_op jit(solution)/shard_map/ppermute | solution.py:14
  33.3 1.8 %collective-permute-done.8 = bf16[4,2,128,128]{3,2,1,0:T(8,128)(2,1)S(1)} collective-permute-done((bf16[4,2,128,128]{3,2,1,0:T(8,128)(2,1)S(1)}, bf16[4,2,128,128]{3,2,1,0:T(8,128)(2,1)S(1)}, u32[]{:S(2)}, u32[]{:S(2)}) %collective-permute-start.8) | collective-permute-done | bytes 262176 | tf_op jit(solution)/shard_map/ppermute | solution.py:14
  38.7 2.3 %shard_map.123 = (s32[2,1088]{1,0:T(2,128)S(1)}, s32[1,256]{1,0:T(1,128)S(1)}, s32[1,128]{1,0:T(1,128)S(1)}) custom-call(s32[1,1024]{1,0:T(1,128)S(1)} %get-tuple-element.214.key_ref, s32[1,1024]{1,0:T(1,128)S(1)} %add.756.refs_0_, s32[1,1024]{1,0:T(1,128)S(1)} %get-tuple-element.213.refs_1_), custom_call_target="tpu_custom_call" | custom-call | flops 268435456 | bytes 1048576 | tf_op jit(solution)/shard_map/pallas_call | solution.py:454
  41.0 7.8 %shard_map.124.dense = bf16[1088,128,128]{2,1,0:T(8,128)(2,1)} custom-call(s32[1,128]{1,0:T(1,128)S(1)} %get-tuple-element.88.marks, s32[2,1088]{1,0:T(2,128)S(1)} %get-tuple-element.89.lists, s32[1152,128]{1,0:T(8,128)S(1)} %bitcast.147), custom_call_target="tpu_custom_call" | custom-call | flops 9126805504 | bytes 35651584 | tf_op jit(solution)/shard_map/pallas_call | solution.py:330
  50.1 3.1 %collective-permute-start.13 = (bf16[16,128,128]{2,1,0:T(8,128)(2,1)S(1)}, bf16[16,128,128]{2,1,0:T(8,128)(2,1)S(1)}, u32[]{:S(2)}, u32[]{:S(2)}) collective-permute-start(bf16[16,128,128]{2,1,0:T(8,128)(2,1)S(1)} %bitcast.156), channel_id=1, source_target_pairs={{0,16},{16,0},{1,17},{17,1},{2,18},{18,2},{3,19},{19,3},{4,20},{20... | collective-permute-start | bytes 1572872 | tf_op jit(solution)/shard_map/ppermute | solution.py:14
  55.7 9.4 %shard_map.125 = (bf16[512,128]{1,0:T(8,128)(2,1)}, bf16[4,128,128]{2,1,0:T(8,128)(2,1)}, f32[136,128]{1,0:T(8,128)S(1)}) custom-call(s32[1,128]{1,0:T(1,128)S(1)} %get-tuple-element.88.marks, s32[2,1088]{1,0:T(2,128)S(1)} %get-tuple-element.89.lists, s32[1,256]{1,0:T(1,128)S(1)} %get-tuple-element.91.owner, bf16[128,128]{1,0:T(8,128)(2,1)S(1)} %copy-done.3, ...), custom_call_target="tpu_custom_call" | custom-call | flops 18253611008 | bytes 35651584 | tf_op jit(solution)/shard_map/pallas_call | solution.py:350
  65.3 2.0 %collective-permute-start.19 = (f32[1,72,128]{2,1,0:T(8,128)S(1)}, f32[1,72,128]{2,1,0:T(8,128)S(1)}, u32[]{:S(2)}, u32[]{:S(2)}) collective-permute-start(f32[1,72,128]{2,1,0:T(8,128)S(1)} %slice_bitcast_fusion.10), channel_id=1, source_target_pairs={{0,16},{16,0},{1,17},{17,1},{2,18},{18,2},{3,19},{19,3},{4,20},{20... | collective-permute-start | bytes 110600 | tf_op jit(solution)/shard_map/ppermute | solution.py:14
  67.3 3.0 %collective-permute-start.18 = (bf16[4,128,128]{2,1,0:T(8,128)(2,1)}, bf16[4,128,128]{2,1,0:T(8,128)(2,1)S(1)}, u32[]{:S(2)}, u32[]{:S(2)}) collective-permute-start(bf16[4,128,128]{2,1,0:T(8,128)(2,1)} %get-tuple-element.193.refs_0_), channel_id=1, source_target_pairs={{0,12},{1,13},{2,14},{3,15},{4,8},{5,9},{6,10},{7,11},{8,4},{9,5},... | collective-permute-start | bytes 393224 | tf_op jit(solution)/shard_map/ppermute | solution.py:14
  71.7 1.6 %collective-permute-start.20 = (f32[72,128]{1,0:T(8,128)S(1)}, f32[72,128]{1,0:T(8,128)S(1)}, u32[]{:S(2)}, u32[]{:S(2)}) collective-permute-start(f32[72,128]{1,0:T(8,128)S(1)} %fusion.24), channel_id=1, source_target_pairs={{0,8},{1,9},{2,10},{3,11},{4,12},{5,13},{6,14},{7,15},{8,0},{9,1},... | collective-permute-start | bytes 110600 | tf_op jit(solution)/shard_map/ppermute | solution.py:14
  73.4 3.4 %shard_map.126.refs_1_ = bf16[672,128,128]{2,1,0:T(8,128)(2,1)} custom-call(s32[1,128]{1,0:T(1,128)S(1)} %get-tuple-element.84.marks, s32[2,672]{1,0:T(2,128)S(1)} %get-tuple-element.85.lists, s32[520,128]{1,0:T(8,128)S(1)} %pad.13.codes, bf16[4,128,128]{2,1,0:T(8,128)(2,1)} %get-tuple-element.193.refs_0_, ...), custom_call_target="tpu_custom_call", output_to_operand_aliasing={{}: (4, {})} | custom-call | flops 5637144576 | bytes 22020096 | tf_op jit(solution)/shard_map/pallas_call | solution.py:330
  76.8 7.0 %collective-permute-done.20 = f32[72,128]{1,0:T(8,128)S(1)} collective-permute-done((f32[72,128]{1,0:T(8,128)S(1)}, f32[72,128]{1,0:T(8,128)S(1)}, u32[]{:S(2)}, u32[]{:S(2)}) %collective-permute-start.20) | collective-permute-done | bytes 36896 | tf_op jit(solution)/shard_map/ppermute | solution.py:14
  84.9 1.5 %collective-permute-start.21 = (bf16[4,2,128,128]{3,2,1,0:T(8,128)(2,1)S(1)}, bf16[4,2,128,128]{3,2,1,0:T(8,128)(2,1)S(1)}, u32[]{:S(2)}, u32[]{:S(2)}) collective-permute-start(bf16[4,2,128,128]{3,2,1,0:T(8,128)(2,1)S(1)} %get-tuple-element.206), channel_id=1, source_target_pairs={{0,2},{1,3},{2,0},{3,1},{4,6},{5,7},{6,4},{7,5},{8,10},{9,11},{10,... | collective-permute-start | bytes 786440 | tf_op jit(solution)/shard_map/ppermute | solution.py:14
  87.2 2.5 %shard_map.127.dense = bf16[672,128,128]{2,1,0:T(8,128)(2,1)} custom-call(s32[1,128]{1,0:T(1,128)S(1)} %get-tuple-element.84.marks, s32[2,672]{1,0:T(2,128)S(1)} %get-tuple-element.85.lists, s32[520,128]{1,0:T(8,128)S(1)} %pad.13.codes, bf16[4,4,128,128]{3,2,1,0:T(8,128)(2,1)S(1)} %pad_maximum_fusion.4.refs_0_, ...), custom_call_target="tpu_custom_call", output_to_operand_aliasing={{}: (4, {})} | custom-call | flops 5637144576 | bytes 22020096 | tf_op jit(solution)/shard_map/pallas_call | solution.py:330
  91.2 1.5 %collective-permute-done.21 = bf16[4,2,128,128]{3,2,1,0:T(8,128)(2,1)S(1)} collective-permute-done((bf16[4,2,128,128]{3,2,1,0:T(8,128)(2,1)S(1)}, bf16[4,2,128,128]{3,2,1,0:T(8,128)(2,1)S(1)}, u32[]{:S(2)}, u32[]{:S(2)}) %collective-permute-start.21) | collective-permute-done | bytes 262176 | tf_op jit(solution)/shard_map/ppermute | solution.py:14
  95.2 1.7 %collective-permute-start.26 = (f32[72,128]{1,0:T(8,128)S(1)}, f32[72,128]{1,0:T(8,128)S(1)}, u32[]{:S(2)}, u32[]{:S(2)}) collective-permute-start(f32[72,128]{1,0:T(8,128)S(1)} %add.787), channel_id=1, source_target_pairs={{0,2},{1,3},{2,0},{3,1},{4,6},{5,7},{6,4},{7,5},{8,10},{9,11},{10,... | collective-permute-start | bytes 110600 | tf_op jit(solution)/shard_map/ppermute | solution.py:14
  96.9 2.9 %shard_map.128.before = f32[8,128,128]{2,1,0:T(8,128)S(1)} custom-call(s32[1,128]{1,0:T(1,128)S(1)} %get-tuple-element.84.marks, s32[2,672]{1,0:T(2,128)S(1)} %get-tuple-element.85.lists, s32[1,128]{1,0:T(1,128)S(1)} %get-tuple-element.99.owner, f32[8,128,128]{2,1,0:T(8,128)S(1)} %broadcast_in_dim.60.before, bf16[672,128,128]{2,1,0:T(8,128)(2,1)} %shard_map.127.dense, ...), custom_call_target="tpu_custom_call" | custom-call | flops 11274289152 | bytes 22020096 | tf_op jit(solution)/shard_map/pallas_call | solution.py:376
  99.8 7.8 %collective-permute-done.26 = f32[72,128]{1,0:T(8,128)S(1)} collective-permute-done((f32[72,128]{1,0:T(8,128)S(1)}, f32[72,128]{1,0:T(8,128)S(1)}, u32[]{:S(2)}, u32[]{:S(2)}) %collective-permute-start.26) | collective-permute-done | bytes 36896 | tf_op jit(solution)/shard_map/ppermute | solution.py:14
  108.8 2.9 %shard_map.129 = f32[8,128,128]{2,1,0:T(8,128)S(1)} custom-call(s32[1,128]{1,0:T(1,128)S(1)} %get-tuple-element.84.marks, s32[2,672]{1,0:T(2,128)S(1)} %get-tuple-element.85.lists, s32[1,128]{1,0:T(1,128)S(1)} %get-tuple-element.99.owner, f32[8,128,128]{2,1,0:T(8,128)S(1)} %shard_map.128.before, bf16[672,128,128]{2,1,0:T(8,128)(2,1)} %shard_map.127.dense, ...), custom_call_target="tpu_custom_call" | custom-call | flops 11274289152 | bytes 22020096 | tf_op jit(solution)/shard_map/pallas_call | solution.py:376
  (107 shorter events, 25.9 us)
Async XLA Ops:
  0.6 22.0 %collective-permute-start.6 = (bf16[4,128,128]{2,1,0:T(8,128)(2,1)}, bf16[4,128,128]{2,1,0:T(8,128)(2,1)S(1)}, u32[]{:S(2)}, u32[]{:S(2)}) collective-permute-start(bf16[4,128,128]{2,1,0:T(8,128)(2,1)} %bitcast.170), channel_id=1, source_target_pairs={{0,12},{1,13},{2,14},{3,15},{4,8},{5,9},{6,10},{7,11},{8,4},{9,5},... | collective-permute-start | bytes 393224 | tf_op jit(solution)/shard_map/ppermute | solution.py:14
  5.8 16.9 %collective-permute-start.5 = (bf16[4,128,128]{2,1,0:T(8,128)(2,1)}, bf16[4,128,128]{2,1,0:T(8,128)(2,1)S(1)}, u32[]{:S(2)}, u32[]{:S(2)}) collective-permute-start(bf16[4,128,128]{2,1,0:T(8,128)(2,1)} %bitcast.171), channel_id=1, source_target_pairs={{0,4},{1,5},{2,6},{3,7},{4,0},{5,1},{6,2},{7,3},{8,12},{9,13},{10,... | collective-permute-start | bytes 393224 | tf_op jit(solution)/shard_map/ppermute | solution.py:14
  5.8 17.0 %collective-permute-start.4 = (bf16[4,128,128]{2,1,0:T(8,128)(2,1)}, bf16[4,128,128]{2,1,0:T(8,128)(2,1)S(1)}, u32[]{:S(2)}, u32[]{:S(2)}) collective-permute-start(bf16[4,128,128]{2,1,0:T(8,128)(2,1)} %bitcast.172), channel_id=1, source_target_pairs={{0,8},{1,9},{2,10},{3,11},{4,12},{5,13},{6,14},{7,15},{8,0},{9,1},... | collective-permute-start | bytes 393224 | tf_op jit(solution)/shard_map/ppermute | solution.py:14
  12.3 25.4 %all-to-all-start = ((s32[16,72,128]{2,1,0:T(8,128)}), s32[16,72,128]{2,1,0:T(8,128)S(1)}, u32[]{:S(2)}, u32[]{:S(2)}) async-start(s32[16,72,128]{2,1,0:T(8,128)} %bitcast.30), calls=%async_computation | async-start | bytes 1179648 | tf_op jit(solution)/shard_map/all_to_all | solution.py:561
  22.9 10.4 %collective-permute-start.7 = (bf16[4,2,128,128]{3,2,1,0:T(8,128)(2,1)S(1)}, bf16[4,2,128,128]{3,2,1,0:T(8,128)(2,1)S(1)}, u32[]{:S(2)}, u32[]{:S(2)}) collective-permute-start(bf16[4,2,128,128]{3,2,1,0:T(8,128)(2,1)S(1)} %get-tuple-element.208), channel_id=1, source_target_pairs={{0,2},{1,3},{2,0},{3,1},{4,6},{5,7},{6,4},{7,5},{8,10},{9,11},{10,... | collective-permute-start | bytes 786440 | tf_op jit(solution)/shard_map/ppermute | solution.py:14
  24.8 10.3 %collective-permute-start.8 = (bf16[4,2,128,128]{3,2,1,0:T(8,128)(2,1)S(1)}, bf16[4,2,128,128]{3,2,1,0:T(8,128)(2,1)S(1)}, u32[]{:S(2)}, u32[]{:S(2)}) collective-permute-start(bf16[4,2,128,128]{3,2,1,0:T(8,128)(2,1)S(1)} %get-tuple-element.207), channel_id=1, source_target_pairs={{0,1},{1,0},{2,3},{3,2},{4,5},{5,4},{6,7},{7,6},{8,9},{9,8},{10,11... | collective-permute-start | bytes 786440 | tf_op jit(solution)/shard_map/ppermute | solution.py:14
  35.2 14.9 %collective-permute-start.9 = (bf16[8,2,128,128]{3,2,1,0:T(8,128)(2,1)S(1)}, bf16[8,2,128,128]{3,2,1,0:T(8,128)(2,1)S(1)}, u32[]{:S(2)}, u32[]{:S(2)}) collective-permute-start(bf16[8,2,128,128]{3,2,1,0:T(8,128)(2,1)S(1)} %pad_maximum_fusion.2), channel_id=1, source_target_pairs={{0,1},{1,0},{2,3},{3,2},{4,5},{5,4},{6,7},{7,6},{8,9},{9,8},{10,11... | collective-permute-start | bytes 1572872 | tf_op jit(solution)/shard_map/ppermute | solution.py:14
  36.5 13.6 %collective-permute-start.10 = (bf16[8,2,128,128]{3,2,1,0:T(8,128)(2,1)S(1)}, bf16[8,2,128,128]{3,2,1,0:T(8,128)(2,1)S(1)}, u32[]{:S(2)}, u32[]{:S(2)}) collective-permute-start(bf16[8,2,128,128]{3,2,1,0:T(8,128)(2,1)S(1)} %pad_maximum_fusion.3), channel_id=1, source_target_pairs={{0,2},{1,3},{2,0},{3,1},{4,6},{5,7},{6,4},{7,5},{8,10},{9,11},{10,... | collective-permute-start | bytes 1572872 | tf_op jit(solution)/shard_map/ppermute | solution.py:14
  37.2 17.3 %collective-permute-start.12 = (bf16[16,128,128]{2,1,0:T(8,128)(2,1)S(1)}, bf16[16,128,128]{2,1,0:T(8,128)(2,1)S(1)}, u32[]{:S(2)}, u32[]{:S(2)}) collective-permute-start(bf16[16,128,128]{2,1,0:T(8,128)(2,1)S(1)} %bitcast.149), channel_id=1, source_target_pairs={{0,16},{16,0},{1,17},{17,1},{2,18},{18,2},{3,19},{19,3},{4,20},{20... | collective-permute-start | bytes 1572872 | tf_op jit(solution)/shard_map/ppermute | solution.py:14
  37.2 17.3 %collective-permute-start.14 = (bf16[16,128,128]{2,1,0:T(8,128)(2,1)S(1)}, bf16[16,128,128]{2,1,0:T(8,128)(2,1)}, u32[]{:S(2)}, u32[]{:S(2)}) collective-permute-start(bf16[16,128,128]{2,1,0:T(8,128)(2,1)S(1)} %bitcast.151), channel_id=1, source_target_pairs={{0,16},{16,0},{1,17},{17,1},{2,18},{18,2},{3,19},{19,3},{4,20},{20... | collective-permute-start | bytes 1572872 | tf_op jit(solution)/shard_map/ppermute | solution.py:14
  38.6 10.2 %collective-permute-start.11 = (s32[1,64]{1,0:T(1,128)}, s32[1,64]{1,0:T(1,128)S(1)}, u32[]{:S(2)}, u32[]{:S(2)}) collective-permute-start(s32[1,64]{1,0:T(1,128)} %bitcast.32), channel_id=1, source_target_pairs={{0,16},{16,0},{1,17},{17,1},{2,18},{18,2},{3,19},{19,3},{4,20},{20... | collective-permute-start | bytes 776 | tf_op jit(solution)/shard_map/ppermute | solution.py:14
  50.1 4.7 %collective-permute-start.13 = (bf16[16,128,128]{2,1,0:T(8,128)(2,1)S(1)}, bf16[16,128,128]{2,1,0:T(8,128)(2,1)S(1)}, u32[]{:S(2)}, u32[]{:S(2)}) collective-permute-start(bf16[16,128,128]{2,1,0:T(8,128)(2,1)S(1)} %bitcast.156), channel_id=1, source_target_pairs={{0,16},{16,0},{1,17},{17,1},{2,18},{18,2},{3,19},{19,3},{4,20},{20... | collective-permute-start | bytes 1572872 | tf_op jit(solution)/shard_map/ppermute | solution.py:14
  65.3 6.4 %collective-permute-start.19 = (f32[1,72,128]{2,1,0:T(8,128)S(1)}, f32[1,72,128]{2,1,0:T(8,128)S(1)}, u32[]{:S(2)}, u32[]{:S(2)}) collective-permute-start(f32[1,72,128]{2,1,0:T(8,128)S(1)} %slice_bitcast_fusion.10), channel_id=1, source_target_pairs={{0,16},{16,0},{1,17},{17,1},{2,18},{18,2},{3,19},{19,3},{4,20},{20... | collective-permute-start | bytes 110600 | tf_op jit(solution)/shard_map/ppermute | solution.py:14
  67.3 16.5 %collective-permute-start.18 = (bf16[4,128,128]{2,1,0:T(8,128)(2,1)}, bf16[4,128,128]{2,1,0:T(8,128)(2,1)S(1)}, u32[]{:S(2)}, u32[]{:S(2)}) collective-permute-start(bf16[4,128,128]{2,1,0:T(8,128)(2,1)} %get-tuple-element.193.refs_0_), channel_id=1, source_target_pairs={{0,12},{1,13},{2,14},{3,15},{4,8},{5,9},{6,10},{7,11},{8,4},{9,5},... | collective-permute-start | bytes 393224 | tf_op jit(solution)/shard_map/ppermute | solution.py:14
  70.3 13.5 %collective-permute-start.17 = (bf16[4,128,128]{2,1,0:T(8,128)(2,1)}, bf16[4,128,128]{2,1,0:T(8,128)(2,1)S(1)}, u32[]{:S(2)}, u32[]{:S(2)}) collective-permute-start(bf16[4,128,128]{2,1,0:T(8,128)(2,1)} %get-tuple-element.193.refs_0_), channel_id=1, source_target_pairs={{0,4},{1,5},{2,6},{3,7},{4,0},{5,1},{6,2},{7,3},{8,12},{9,13},{10,... | collective-permute-start | bytes 393224 | tf_op jit(solution)/shard_map/ppermute | solution.py:14
  70.4 13.4 %collective-permute-start.16 = (bf16[4,128,128]{2,1,0:T(8,128)(2,1)}, bf16[4,128,128]{2,1,0:T(8,128)(2,1)S(1)}, u32[]{:S(2)}, u32[]{:S(2)}) collective-permute-start(bf16[4,128,128]{2,1,0:T(8,128)(2,1)} %get-tuple-element.193.refs_0_), channel_id=1, source_target_pairs={{0,8},{1,9},{2,10},{3,11},{4,12},{5,13},{6,14},{7,15},{8,0},{9,1},... | collective-permute-start | bytes 393224 | tf_op jit(solution)/shard_map/ppermute | solution.py:14
  71.7 12.1 %collective-permute-start.20 = (f32[72,128]{1,0:T(8,128)S(1)}, f32[72,128]{1,0:T(8,128)S(1)}, u32[]{:S(2)}, u32[]{:S(2)}) collective-permute-start(f32[72,128]{1,0:T(8,128)S(1)} %fusion.24), channel_id=1, source_target_pairs={{0,8},{1,9},{2,10},{3,11},{4,12},{5,13},{6,14},{7,15},{8,0},{9,1},... | collective-permute-start | bytes 110600 | tf_op jit(solution)/shard_map/ppermute | solution.py:14
  84.9 7.9 %collective-permute-start.21 = (bf16[4,2,128,128]{3,2,1,0:T(8,128)(2,1)S(1)}, bf16[4,2,128,128]{3,2,1,0:T(8,128)(2,1)S(1)}, u32[]{:S(2)}, u32[]{:S(2)}) collective-permute-start(bf16[4,2,128,128]{3,2,1,0:T(8,128)(2,1)S(1)} %get-tuple-element.206), channel_id=1, source_target_pairs={{0,2},{1,3},{2,0},{3,1},{4,6},{5,7},{6,4},{7,5},{8,10},{9,11},{10,... | collective-permute-start | bytes 786440 | tf_op jit(solution)/shard_map/ppermute | solution.py:14
  86.4 7.5 %collective-permute-start.22 = (bf16[4,2,128,128]{3,2,1,0:T(8,128)(2,1)S(1)}, bf16[4,2,128,128]{3,2,1,0:T(8,128)(2,1)S(1)}, u32[]{:S(2)}, u32[]{:S(2)}) collective-permute-start(bf16[4,2,128,128]{3,2,1,0:T(8,128)(2,1)S(1)} %get-tuple-element.205), channel_id=1, source_target_pairs={{0,1},{1,0},{2,3},{3,2},{4,5},{5,4},{6,7},{7,6},{8,9},{9,8},{10,11... | collective-permute-start | bytes 786440 | tf_op jit(solution)/shard_map/ppermute | solution.py:14
  87.2 4.0 %collective-permute-start.23 = (f32[72,128]{1,0:T(8,128)S(1)}, f32[72,128]{1,0:T(8,128)S(1)}, u32[]{:S(2)}, u32[]{:S(2)}) collective-permute-start(f32[72,128]{1,0:T(8,128)S(1)} %add.786), channel_id=1, source_target_pairs={{0,4},{1,5},{2,6},{3,7},{4,0},{5,1},{6,2},{7,3},{8,12},{9,13},{10,... | collective-permute-start | bytes 110600 | tf_op jit(solution)/shard_map/ppermute | solution.py:14
  93.9 13.6 %collective-permute-start.24 = (bf16[8,2,128,128]{3,2,1,0:T(8,128)(2,1)S(1)}, bf16[8,2,128,128]{3,2,1,0:T(8,128)(2,1)S(1)}, u32[]{:S(2)}, u32[]{:S(2)}) collective-permute-start(bf16[8,2,128,128]{3,2,1,0:T(8,128)(2,1)S(1)} %pad_maximum_fusion.5), channel_id=1, source_target_pairs={{0,1},{1,0},{2,3},{3,2},{4,5},{5,4},{6,7},{7,6},{8,9},{9,8},{10,11... | collective-permute-start | bytes 1572872 | tf_op jit(solution)/shard_map/ppermute | solution.py:14
  94.8 12.7 %collective-permute-start.25 = (bf16[8,2,128,128]{3,2,1,0:T(8,128)(2,1)S(1)}, bf16[8,2,128,128]{3,2,1,0:T(8,128)(2,1)S(1)}, u32[]{:S(2)}, u32[]{:S(2)}) collective-permute-start(bf16[8,2,128,128]{3,2,1,0:T(8,128)(2,1)S(1)} %pad_maximum_fusion.6), channel_id=1, source_target_pairs={{0,2},{1,3},{2,0},{3,1},{4,6},{5,7},{6,4},{7,5},{8,10},{9,11},{10,... | collective-permute-start | bytes 1572872 | tf_op jit(solution)/shard_map/ppermute | solution.py:14
  95.2 12.4 %collective-permute-start.26 = (f32[72,128]{1,0:T(8,128)S(1)}, f32[72,128]{1,0:T(8,128)S(1)}, u32[]{:S(2)}, u32[]{:S(2)}) collective-permute-start(f32[72,128]{1,0:T(8,128)S(1)} %add.787), channel_id=1, source_target_pairs={{0,2},{1,3},{2,0},{3,1},{4,6},{5,7},{6,4},{7,5},{8,10},{9,11},{10,... | collective-permute-start | bytes 110600 | tf_op jit(solution)/shard_map/ppermute | solution.py:14
  107.6 4.1 %collective-permute-start.27 = (f32[72,128]{1,0:T(8,128)S(1)}, f32[72,128]{1,0:T(8,128)S(1)}, u32[]{:S(2)}, u32[]{:S(2)}) collective-permute-start(f32[72,128]{1,0:T(8,128)S(1)} %add.788), channel_id=1, source_target_pairs={{0,1},{1,0},{2,3},{3,2},{4,5},{5,4},{6,7},{7,6},{8,9},{9,8},{10,11... | collective-permute-start | bytes 110600 | tf_op jit(solution)/shard_map/ppermute | solution.py:14
  (7 other events, 53.0 us)

commit v4 on v3

--- a/solution.py
+++ b/solution.py
@@ -96,19 +96,24 @@
     return rows.astype(jnp.float32).astype(jnp.bfloat16)
 
 
-def block_of(code, rows):
+def blocks_of(lines, rows):
+    codes = jnp.concatenate(lines, axis=0)
+    inner = ((codes >> 16) & 127).astype(jnp.float32).T
+    outer = (codes >> 23).astype(jnp.float32)
+    weight = (codes & (FIELD - 1)).astype(jnp.float32) * UNIT
+    lanes = lax.broadcasted_iota(jnp.int32, (128, 128), 1).astype(jnp.float32)
+    zero = jnp.zeros((), jnp.bfloat16)
+
     def tile(x):
-        return jnp.broadcast_to(x.astype(jnp.float32), (16, 128)).astype(jnp.bfloat16)[None]
-
-    o = code >> 16
-    zero = jnp.zeros((), jnp.bfloat16)
-    one = jnp.ones((), jnp.bfloat16)
-    w = tile((code & (FIELD - 1)).astype(jnp.float32) * UNIT)
-    left = jnp.where(rows == tile(o >> 7), w, zero).reshape(128, 128)
-    right = jnp.where(rows == tile(o & 127), one, zero).reshape(128, 128)
-    return lax.dot_general(
-        left, right, (((1,), (1,)), ((), ())), preferred_element_type=jnp.float32
-    ).astype(jnp.bfloat16)
+        return jnp.broadcast_to(x, (16, 128)).astype(jnp.bfloat16)[None]
+
+    blocks = []
+    for u in range(GROUP):
+        left = jnp.where(rows == tile(outer[u : u + 1]), tile(weight[u : u + 1]), zero)
+        right = jnp.where(inner[:, u : u + 1] == lanes, 1.0, 0.0).astype(jnp.bfloat16)
+        block = jnp.dot(left.reshape(128, 128), right, preferred_element_type=jnp.float32)
+        blocks.append(block.astype(jnp.bfloat16))
+    return blocks
 
 
 def pack_kernel(meta, pos, codes, labels, out):
@@ -146,7 +151,7 @@
 
         lines = [codes[pl.ds(lists[0, i * TURN + u], 1), :] for u in range(TURN)]
         for u in range(0, TURN, GROUP):
-            blocks = [block_of(line, rows) for line in lines[u : u + GROUP]]
+            blocks = blocks_of(lines[u : u + GROUP], rows)
             for k, block in enumerate(blocks):
                 dbuf[slot, u + k] = block
         out_copy(i).start()
@@ -211,13 +216,20 @@
     output, turned, local, totals, feat, proj, dbuf, piece_sems, sems = refs
     copies = fetch(pieces, feat, piece_sems)
     size, _, width = pieces[0].shape
-    batch = 8 if size % 8 == 0 else 1
+    batch = 8 if size % 8 == 0 else 2
+    zero = jnp.zeros_like(weight[...])
+    twice = jnp.concatenate(
+        [jnp.concatenate([weight[...], zero], 1), jnp.concatenate([zero, weight[...]], 1)], 0
+    )
 
     def project(t, _):
-        spot = pl.ds(t * batch, batch)
-        held = feat[spot].reshape(batch * 128, width)
-        low = jnp.dot(held, weight[...], preferred_element_type=jnp.float32)
-        proj[spot] = low.astype(jnp.bfloat16).reshape(batch, 128, width)
+        halves = [pl.ds(t * batch + k * batch // 2, batch // 2) for k in range(2)]
+        held = [feat[half].reshape(batch * 64, width) for half in halves]
+        low = jnp.dot(
+            jnp.concatenate(held, axis=1), twice, preferred_element_type=jnp.float32
+        ).astype(jnp.bfloat16)
+        for k, half in enumerate(halves):
+            proj[half] = low[:, k * width : (k + 1) * width].reshape(batch // 2, 128, width)
         return 0
 
     def prepare():
@@ -262,9 +274,9 @@
     totals[...] = jnp.zeros_like(totals)
 
     def turn(i, _):
-        for u in range(GROUP):
+        lines = [codes[pl.ds(order[i * GROUP + u], 1), :] for u in range(GROUP)]
+        for u, block in enumerate(blocks_of(lines, rows)):
             p = i * GROUP + u
-            block = block_of(codes[pl.ds(order[p], 1), :], rows)
             totals[dst[p]] += jnp.dot(block, panel[col[p]], preferred_element_type=jnp.float32)
         return 0
 
@@ -438,13 +450,12 @@
 
     spot = lax.broadcasted_iota(jnp.int32, (1, 128), 1)
     marks = jnp.where(spot == FIRST, first, 0.0)
-    for k in range(1, 5):
-        marks = jnp.where(spot == FIRST + k, jnp.floor(turns * (k / 4)), marks)
+    marks = jnp.where(spot == MIDDLE, jnp.floor((first + turns) * 0.5), marks)
+    marks = jnp.where(spot == ALL, turns, marks)
     marks_ref[...] = marks.astype(jnp.int32)
 
 
-FIRST = 1
-QUARTERS = [0, 2, 3, 4, 5]
+NONE, FIRST, MIDDLE, ALL = range(4)
 
 
 def make_lists(key, values, fills, keys, split):
@@ -542,8 +553,7 @@
     state = {"dense": None}
 
     def build(held, start, end):
-        span = (QUARTERS[start], QUARTERS[end])
-        state["dense"] = run_build(span, back, codes, held, state["dense"])
+        state["dense"] = run_build((start, end), back, codes, held, state["dense"])
 
     if by_owner:
         same = live[:, None] & (home[:, None] == home[None, :]) & (ids[:, None] < ids[None, :])
@@ -583,19 +593,10 @@
             per,
         )
 
-        def prepare(step, held):
-            if step == 0:
-                build(held, 0, 1)
-            if step == 1:
-                held, state["dense"] = lax.optimization_barrier((held, state["dense"]))
-            return held
-
-        pairs = gather_pieces(features.reshape(per, 128, width), prepare)
+        pairs = gather_pieces(features.reshape(per, 128, width), lambda step, held: held)
         lines = came.reshape(n_col * stride, 128)
-        here = run_build((0, QUARTERS[4]), listed, lines, [], None)
-        last, here, any_over = lax.optimization_barrier(
-            ([pair[1] for pair in pairs], here, any_over)
-        )
+        here = run_build((NONE, ALL), listed, lines, [], None)
+        last, here, back = lax.optimization_barrier(([pair[1] for pair in pairs], here, back))
         feat = []
         for pair in [[pair[0], x] for pair, x in zip(pairs, last)]:
             rows = [pair]
@@ -603,7 +604,7 @@
                 rows = rows + [[swap(x, "row", bit) for x in pair] for pair in rows]
             feat += [x for pair in rows for x in pair]
         done = run_forward(
-            scale, (0, QUARTERS[4]), listed, weight, bias[None], cotangent, here, feat
+            scale, (NONE, ALL), listed, weight, bias[None], cotangent, here, feat
         )
         done = lax.cond(any_over[0] > 0, tile_plan, lambda: tuple(done))
     else:
@@ -623,22 +624,23 @@
         if steps:
             add_total()
         if step == 0:
-            build(held, 3, 4)
+            build(held, FIRST, MIDDLE)
         if step == 1:
             add_products(0, held)
+            build(held, MIDDLE, ALL)
         return held
 
     def add_products(half, pieces):
         pieces = [x.reshape((-1,) + x.shape[2:]) if x.ndim == 4 else x for x in pieces]
         state["acc"] = run_backward(
-            [(0, FIRST), (FIRST, QUARTERS[4])][half], back, state["acc"], state["dense"], pieces
+            [(NONE, FIRST), (FIRST, ALL)][half], back, state["acc"], state["dense"], pieces
         )
 
     state["acc"] = jnp.zeros((col_blocks, width, 128), jnp.float32)
     state["total"] = split_rows(total)
     while len(steps) > 3:
         add_total()
-    build([turned], 1, 3)
+    build([turned], NONE, FIRST)
     grad = gather_pieces(turned, beside)
     late_pieces, state["total"] = lax.optimization_barrier(
         ([pair[1] for pair in grad], state["total"])

time: 116 us -> 118 us (1.017)
  the two profiles are of different devices: /device:TPU:0 before, /device:TPU:23 now
where the time goes in v4:
time: 118 us
  Pallas kernels  42.1 us (36%)
  starting transfers between devices  33.9 us (29%)
  waiting for transfers between devices  25.3 us (21%)
  other arithmetic  9.76 us (8%)
  between operations  3.12 us (3%)
  local copies, waits for them, and re-layouts  2.44 us (2%)
    ppermute x26, starting transfers between devices, swap(): return lax.ppermute(x, axis, [(i, i ^ bit) for i in range(n)])  27.2 us
    ppermute x26, waiting for transfers between devices, swap(): return lax.ppermute(x, axis, [(i, i ^ bit) for i in range(n)])  25.3 us
    pallas_call x4, Pallas kernels, run_build(): pl.pallas_call(functools.partial(build_kernel, span), out_shape=jax.Shape...  20.3 us
    pallas_call x1, Pallas kernels, run_forward(): pl.pallas_call(functools.partial(forward_kernel, n, scale, span), out_sha...  11.2 us
    all_to_all x1, starting transfers between devices, shards(): lax.all_to_all(packed.reshape(n_col, stride, 128), 'col', split_axis=0, c...  6.64 us
    pallas_call x2, Pallas kernels, run_backward(): pl.pallas_call(functools.partial(backward_kernel, n, span), out_shape=jax...  5.75 us
    pallas_call x2, Pallas kernels, make_lists(): pl.pallas_call(functools.partial(list_kernel, keys, split, fills), out_sh...  3.31 us
  transfers between devices with their start and end apart: 27, of which 7 were waited for; matrix products, arithmetic and copies ran while one was open for 9% of the time, Pallas kernels for 26%

profile of v4, /device:TPU:23, one launch (start us, length us, event | category | flops | bytes accessed | tf_op | source)
XLA Modules:
  0.0 117.6 jit_solution(5383430006749647683)
XLA Ops:
  0.9 1.2 %collective-permute-start.6 = (bf16[4,128,128]{2,1,0:T(8,128)(2,1)}, bf16[4,128,128]{2,1,0:T(8,128)(2,1)S(1)}, u32[]{:S(2)}, u32[]{:S(2)}) collective-permute-start(bf16[4,128,128]{2,1,0:T(8,128)(2,1)} %bitcast.169), channel_id=1, source_target_pairs={{0,4},{1,5},{2,6},{3,7},{4,0},{5,1},{6,2},{7,3},{8,12},{9,13},{10,... | collective-permute-start | bytes 393224 | tf_op jit(solution)/shard_map/ppermute | solution.py:14
  2.1 2.0 %collective-permute-start.5 = (bf16[4,128,128]{2,1,0:T(8,128)(2,1)}, bf16[4,128,128]{2,1,0:T(8,128)(2,1)S(1)}, u32[]{:S(2)}, u32[]{:S(2)}) collective-permute-start(bf16[4,128,128]{2,1,0:T(8,128)(2,1)} %bitcast.170), channel_id=1, source_target_pairs={{0,8},{1,9},{2,10},{3,11},{4,12},{5,13},{6,14},{7,15},{8,0},{9,1},... | collective-permute-start | bytes 393224 | tf_op jit(solution)/shard_map/ppermute | solution.py:14
  7.4 1.1 add_bitcast_fusion
  8.5 1.5 %shard_map.120 = s32[1152,128]{1,0:T(8,128)} custom-call(s32[1]{0:T(128)} %bitcast.17.meta, s32[512]{0:T(512)S(1)} %get-tuple-element.214.pos, s32[520,128]{1,0:T(8,128)S(1)} %pad.13.codes, s32[16,128]{1,0:T(8,128)S(1)} %concatenate.24.labels), custom_call_target="tpu_custom_call" | custom-call | tf_op jit(solution)/shard_map/pallas_call | solution.py:330
  10.0 6.6 %all-to-all-start = ((s32[16,72,128]{2,1,0:T(8,128)}), s32[16,72,128]{2,1,0:T(8,128)S(1)}, u32[]{:S(2)}, u32[]{:S(2)}) async-start(s32[16,72,128]{2,1,0:T(8,128)} %bitcast.21), calls=%async_computation | async-start | bytes 1179648 | tf_op jit(solution)/shard_map/all_to_all | solution.py:571
  21.1 8.9 %collective-permute-done.8 = bf16[4,2,128,128]{3,2,1,0:T(8,128)(2,1)S(1)} collective-permute-done((bf16[4,2,128,128]{3,2,1,0:T(8,128)(2,1)S(1)}, bf16[4,2,128,128]{3,2,1,0:T(8,128)(2,1)S(1)}, u32[]{:S(2)}, u32[]{:S(2)}) %collective-permute-start.8) | collective-permute-done | bytes 262176 | tf_op jit(solution)/shard_map/ppermute | solution.py:14
  30.1 2.5 %collective-permute-start.12 = (bf16[16,128,128]{2,1,0:T(8,128)(2,1)S(1)}, bf16[16,128,128]{2,1,0:T(8,128)(2,1)S(1)}, u32[]{:S(2)}, u32[]{:S(2)}) collective-permute-start(bf16[16,128,128]{2,1,0:T(8,128)(2,1)S(1)} %bitcast.149), channel_id=1, source_target_pairs={{0,16},{16,0},{1,17},{17,1},{2,18},{18,2},{3,19},{19,3},{4,20},{20... | collective-permute-start | bytes 1572872 | tf_op jit(solution)/shard_map/ppermute | solution.py:14
  35.8 2.3 %shard_map.121 = (s32[2,1088]{1,0:T(2,128)S(1)}, s32[1,256]{1,0:T(1,128)S(1)}, s32[1,128]{1,0:T(1,128)S(1)}) custom-call(s32[1,1024]{1,0:T(1,128)S(1)} %get-tuple-element.212.key_ref, s32[1,1024]{1,0:T(1,128)S(1)} %add.739.refs_0_, s32[1,1024]{1,0:T(1,128)S(1)} %get-tuple-element.211.refs_1_), custom_call_target="tpu_custom_call" | custom-call | flops 268435456 | bytes 1048576 | tf_op jit(solution)/shard_map/pallas_call | solution.py:465
  38.2 11.4 %shard_map.122.dense = bf16[1088,128,128]{2,1,0:T(8,128)(2,1)} custom-call(s32[1,128]{1,0:T(1,128)S(1)} %get-tuple-element.83.marks, s32[2,1088]{1,0:T(2,128)S(1)} %get-tuple-element.84.lists, s32[1152,128]{1,0:T(8,128)S(1)} %bitcast.145), custom_call_target="tpu_custom_call" | custom-call | flops 9126805504 | bytes 35651584 | tf_op jit(solution)/shard_map/pallas_call | solution.py:342
  51.7 1.3 %add_reduce_fusion.1 = s32[]{:T(128)} fusion(s32[1,64]{1,0:T(1,128)S(1)} %collective-permute-done.4, s32[64]{0:T(128)} %get-tuple-element.193), kind=kLoop, calls=%fused_computation.178 | loop fusion | flops 127 | bytes 516 | tf_op jit(solution)/shard_map/reduce_max | solution.py:577
  53.7 11.2 %shard_map.124 = (bf16[512,128]{1,0:T(8,128)(2,1)}, bf16[4,128,128]{2,1,0:T(8,128)(2,1)}, f32[136,128]{1,0:T(8,128)S(1)}) custom-call(s32[1,128]{1,0:T(1,128)S(1)} %get-tuple-element.83.marks, s32[2,1088]{1,0:T(2,128)S(1)} %get-tuple-element.84.lists, s32[1,256]{1,0:T(1,128)S(1)} %get-tuple-element.85.owner, bf16[128,128]{1,0:T(8,128)(2,1)S(1)} %copy-done.2, ...), custom_call_target="tpu_custom_call" | custom-call | flops 18253611008 | bytes 35651584 | tf_op jit(solution)/shard_map/pallas_call | solution.py:362
  65.4 2.6 %collective-permute-start.16 = (bf16[4,128,128]{2,1,0:T(8,128)(2,1)}, bf16[4,128,128]{2,1,0:T(8,128)(2,1)S(1)}, u32[]{:S(2)}, u32[]{:S(2)}) collective-permute-start(bf16[4,128,128]{2,1,0:T(8,128)(2,1)} %get-tuple-element.191.refs_0_), channel_id=1, source_target_pairs={{0,8},{1,9},{2,10},{3,11},{4,12},{5,13},{6,14},{7,15},{8,0},{9,1},... | collective-permute-start | bytes 393224 | tf_op jit(solution)/shard_map/ppermute | solution.py:14
  68.1 3.6 %shard_map.125.refs_1_ = bf16[672,128,128]{2,1,0:T(8,128)(2,1)} custom-call(s32[1,128]{1,0:T(1,128)S(1)} %get-tuple-element.96.marks, s32[2,672]{1,0:T(2,128)S(1)} %get-tuple-element.97.lists, s32[520,128]{1,0:T(8,128)S(1)} %pad.13.codes, bf16[4,128,128]{2,1,0:T(8,128)(2,1)} %get-tuple-element.191.refs_0_), custom_call_target="tpu_custom_call" | custom-call | flops 5637144576 | bytes 22020096 | tf_op jit(solution)/shard_map/pallas_call | solution.py:342
  71.7 5.8 %collective-permute-done.20 = f32[72,128]{1,0:T(8,128)S(1)} collective-permute-done((f32[72,128]{1,0:T(8,128)S(1)}, f32[72,128]{1,0:T(8,128)S(1)}, u32[]{:S(2)}, u32[]{:S(2)}) %collective-permute-start.20) | collective-permute-done | bytes 36896 | tf_op jit(solution)/shard_map/ppermute | solution.py:14
  78.5 4.3 %collective-permute-start.23 = (f32[72,128]{1,0:T(8,128)S(1)}, f32[72,128]{1,0:T(8,128)S(1)}, u32[]{:S(2)}, u32[]{:S(2)}) collective-permute-start(f32[72,128]{1,0:T(8,128)S(1)} %add.786), channel_id=1, source_target_pairs={{0,4},{1,5},{2,6},{3,7},{4,0},{5,1},{6,2},{7,3},{8,12},{9,13},{10,... | collective-permute-start | bytes 110600 | tf_op jit(solution)/shard_map/ppermute | solution.py:14
  83.6 2.7 %shard_map.126.dense.refs_2_ = bf16[672,128,128]{2,1,0:T(8,128)(2,1)} custom-call(s32[1,128]{1,0:T(1,128)S(1)} %get-tuple-element.96.marks, s32[2,672]{1,0:T(2,128)S(1)} %get-tuple-element.97.lists, s32[520,128]{1,0:T(8,128)S(1)} %pad.13.codes, bf16[4,4,128,128]{3,2,1,0:T(8,128)(2,1)S(1)} %pad_maximum_fusion.4.refs_0_, ...), custom_call_target="tpu_custom_call", output_to_operand_aliasing={{}: (4, {})} | custom-call | flops 5637144576 | bytes 22020096 | tf_op jit(solution)/shard_map/pallas_call | solution.py:342
  86.3 3.6 %collective-permute-done.22 = bf16[4,2,128,128]{3,2,1,0:T(8,128)(2,1)S(1)} collective-permute-done((bf16[4,2,128,128]{3,2,1,0:T(8,128)(2,1)S(1)}, bf16[4,2,128,128]{3,2,1,0:T(8,128)(2,1)S(1)}, u32[]{:S(2)}, u32[]{:S(2)}) %collective-permute-start.22) | collective-permute-done | bytes 262176 | tf_op jit(solution)/shard_map/ppermute | solution.py:14
  90.8 1.1 collective-permute-start.24
  92.7 2.9 %shard_map.127.before = f32[8,128,128]{2,1,0:T(8,128)S(1)} custom-call(s32[1,128]{1,0:T(1,128)S(1)} %get-tuple-element.96.marks, s32[2,672]{1,0:T(2,128)S(1)} %get-tuple-element.97.lists, s32[1,128]{1,0:T(1,128)S(1)} %get-tuple-element.98.owner, f32[8,128,128]{2,1,0:T(8,128)S(1)} %broadcast_in_dim.60.before, ...), custom_call_target="tpu_custom_call" | custom-call | flops 11274289152 | bytes 22020096 | tf_op jit(solution)/shard_map/pallas_call | solution.py:388
  95.6 2.6 %shard_map.128.dense = bf16[672,128,128]{2,1,0:T(8,128)(2,1)} custom-call(s32[1,128]{1,0:T(1,128)S(1)} %get-tuple-element.96.marks, s32[2,672]{1,0:T(2,128)S(1)} %get-tuple-element.97.lists, s32[520,128]{1,0:T(8,128)S(1)} %pad.13.codes, bf16[8,2,128,128]{3,2,1,0:T(8,128)(2,1)S(1)} %pad_maximum_fusion.5.refs_0_, ...), custom_call_target="tpu_custom_call", output_to_operand_aliasing={{}: (5, {})} | custom-call | flops 5637144576 | bytes 22020096 | tf_op jit(solution)/shard_map/pallas_call | solution.py:342
  98.2 4.1 %collective-permute-done.24 = bf16[8,2,128,128]{3,2,1,0:T(8,128)(2,1)S(1)} collective-permute-done((bf16[8,2,128,128]{3,2,1,0:T(8,128)(2,1)S(1)}, bf16[8,2,128,128]{3,2,1,0:T(8,128)(2,1)S(1)}, u32[]{:S(2)}, u32[]{:S(2)}) %collective-permute-start.24) | collective-permute-done | bytes 524320 | tf_op jit(solution)/shard_map/ppermute | solution.py:14
  102.3 1.3 %collective-permute-done.25 = bf16[8,2,128,128]{3,2,1,0:T(8,128)(2,1)S(1)} collective-permute-done((bf16[8,2,128,128]{3,2,1,0:T(8,128)(2,1)S(1)}, bf16[8,2,128,128]{3,2,1,0:T(8,128)(2,1)S(1)}, u32[]{:S(2)}, u32[]{:S(2)}) %collective-permute-start.25) | collective-permute-done | bytes 524320 | tf_op jit(solution)/shard_map/ppermute | solution.py:14
  104.3 2.9 %shard_map.129 = f32[8,128,128]{2,1,0:T(8,128)S(1)} custom-call(s32[1,128]{1,0:T(1,128)S(1)} %get-tuple-element.96.marks, s32[2,672]{1,0:T(2,128)S(1)} %get-tuple-element.97.lists, s32[1,128]{1,0:T(1,128)S(1)} %get-tuple-element.98.owner, f32[8,128,128]{2,1,0:T(8,128)S(1)} %shard_map.127.before, bf16[672,128,128]{2,1,0:T(8,128)(2,1)} %shard_map.128.dense, ...), custom_call_target="tpu_custom_call" | custom-call | flops 11274289152 | bytes 22020096 | tf_op jit(solution)/shard_map/pallas_call | solution.py:388
  107.4 7.3 %collective-permute-start.29 = (f32[72,128]{1,0:T(8,128)S(1)}, f32[72,128]{1,0:T(8,128)S(1)}, u32[]{:S(2)}, u32[]{:S(2)}) collective-permute-start(f32[72,128]{1,0:T(8,128)S(1)} %add.789), channel_id=1, source_target_pairs={{0,16},{16,0},{1,17},{17,1},{2,18},{18,2},{3,19},{19,3},{4,20},{20... | collective-permute-start | bytes 110600 | tf_op jit(solution)/shard_map/ppermute | solution.py:14
  (105 shorter events, 19.7 us)
Async XLA Ops:
  0.6 17.1 %collective-permute-start.7 = (bf16[4,128,128]{2,1,0:T(8,128)(2,1)}, bf16[4,128,128]{2,1,0:T(8,128)(2,1)S(1)}, u32[]{:S(2)}, u32[]{:S(2)}) collective-permute-start(bf16[4,128,128]{2,1,0:T(8,128)(2,1)} %bitcast.168), channel_id=1, source_target_pairs={{0,12},{1,13},{2,14},{3,15},{4,8},{5,9},{6,10},{7,11},{8,4},{9,5},... | collective-permute-start | bytes 393224 | tf_op jit(solution)/shard_map/ppermute | solution.py:14
  0.9 16.9 %collective-permute-start.6 = (bf16[4,128,128]{2,1,0:T(8,128)(2,1)}, bf16[4,128,128]{2,1,0:T(8,128)(2,1)S(1)}, u32[]{:S(2)}, u32[]{:S(2)}) collective-permute-start(bf16[4,128,128]{2,1,0:T(8,128)(2,1)} %bitcast.169), channel_id=1, source_target_pairs={{0,4},{1,5},{2,6},{3,7},{4,0},{5,1},{6,2},{7,3},{8,12},{9,13},{10,... | collective-permute-start | bytes 393224 | tf_op jit(solution)/shard_map/ppermute | solution.py:14
  2.1 15.7 %collective-permute-start.5 = (bf16[4,128,128]{2,1,0:T(8,128)(2,1)}, bf16[4,128,128]{2,1,0:T(8,128)(2,1)S(1)}, u32[]{:S(2)}, u32[]{:S(2)}) collective-permute-start(bf16[4,128,128]{2,1,0:T(8,128)(2,1)} %bitcast.170), channel_id=1, source_target_pairs={{0,8},{1,9},{2,10},{3,11},{4,12},{5,13},{6,14},{7,15},{8,0},{9,1},... | collective-permute-start | bytes 393224 | tf_op jit(solution)/shard_map/ppermute | solution.py:14
  10.0 24.9 %all-to-all-start = ((s32[16,72,128]{2,1,0:T(8,128)}), s32[16,72,128]{2,1,0:T(8,128)S(1)}, u32[]{:S(2)}, u32[]{:S(2)}) async-start(s32[16,72,128]{2,1,0:T(8,128)} %bitcast.21), calls=%async_computation | async-start | bytes 1179648 | tf_op jit(solution)/shard_map/all_to_all | solution.py:571
  18.8 11.2 %collective-permute-start.8 = (bf16[4,2,128,128]{3,2,1,0:T(8,128)(2,1)S(1)}, bf16[4,2,128,128]{3,2,1,0:T(8,128)(2,1)S(1)}, u32[]{:S(2)}, u32[]{:S(2)}) collective-permute-start(bf16[4,2,128,128]{3,2,1,0:T(8,128)(2,1)S(1)} %get-tuple-element.206), channel_id=1, source_target_pairs={{0,2},{1,3},{2,0},{3,1},{4,6},{5,7},{6,4},{7,5},{8,10},{9,11},{10,... | collective-permute-start | bytes 786440 | tf_op jit(solution)/shard_map/ppermute | solution.py:14
  19.2 13.5 %collective-permute-start.10 = (bf16[4,2,128,128]{3,2,1,0:T(8,128)(2,1)S(1)}, bf16[4,2,128,128]{3,2,1,0:T(8,128)(2,1)}, u32[]{:S(2)}, u32[]{:S(2)}) collective-permute-start(bf16[4,2,128,128]{3,2,1,0:T(8,128)(2,1)S(1)} %get-tuple-element.205), channel_id=1, source_target_pairs={{0,1},{1,0},{2,3},{3,2},{4,5},{5,4},{6,7},{7,6},{8,9},{9,8},{10,11... | collective-permute-start | bytes 786440 | tf_op jit(solution)/shard_map/ppermute | solution.py:14
  30.1 19.5 %collective-permute-start.9 = (bf16[8,2,128,128]{3,2,1,0:T(8,128)(2,1)S(1)}, bf16[8,2,128,128]{3,2,1,0:T(8,128)(2,1)S(1)}, u32[]{:S(2)}, u32[]{:S(2)}) collective-permute-start(bf16[8,2,128,128]{3,2,1,0:T(8,128)(2,1)S(1)} %pad_maximum_fusion.2), channel_id=1, source_target_pairs={{0,1},{1,0},{2,3},{3,2},{4,5},{5,4},{6,7},{7,6},{8,9},{9,8},{10,11... | collective-permute-start | bytes 1572872 | tf_op jit(solution)/shard_map/ppermute | solution.py:14
  30.1 23.5 %collective-permute-start.12 = (bf16[16,128,128]{2,1,0:T(8,128)(2,1)S(1)}, bf16[16,128,128]{2,1,0:T(8,128)(2,1)S(1)}, u32[]{:S(2)}, u32[]{:S(2)}) collective-permute-start(bf16[16,128,128]{2,1,0:T(8,128)(2,1)S(1)} %bitcast.149), channel_id=1, source_target_pairs={{0,16},{16,0},{1,17},{17,1},{2,18},{18,2},{3,19},{19,3},{4,20},{20... | collective-permute-start | bytes 1572872 | tf_op jit(solution)/shard_map/ppermute | solution.py:14
  33.7 15.9 %collective-permute-start.11 = (bf16[8,2,128,128]{3,2,1,0:T(8,128)(2,1)S(1)}, bf16[8,2,128,128]{3,2,1,0:T(8,128)(2,1)S(1)}, u32[]{:S(2)}, u32[]{:S(2)}) collective-permute-start(bf16[8,2,128,128]{3,2,1,0:T(8,128)(2,1)S(1)} %pad_maximum_fusion.3), channel_id=1, source_target_pairs={{0,2},{1,3},{2,0},{3,1},{4,6},{5,7},{6,4},{7,5},{8,10},{9,11},{10,... | collective-permute-start | bytes 1572872 | tf_op jit(solution)/shard_map/ppermute | solution.py:14
  34.6 19.0 %collective-permute-start.14 = (bf16[16,128,128]{2,1,0:T(8,128)(2,1)S(1)}, bf16[16,128,128]{2,1,0:T(8,128)(2,1)}, u32[]{:S(2)}, u32[]{:S(2)}) collective-permute-start(bf16[16,128,128]{2,1,0:T(8,128)(2,1)S(1)} %bitcast.151), channel_id=1, source_target_pairs={{0,16},{16,0},{1,17},{17,1},{2,18},{18,2},{3,19},{19,3},{4,20},{20... | collective-permute-start | bytes 1572872 | tf_op jit(solution)/shard_map/ppermute | solution.py:14
  49.6 4.0 %collective-permute-start.13 = (bf16[16,128,128]{2,1,0:T(8,128)(2,1)S(1)}, bf16[16,128,128]{2,1,0:T(8,128)(2,1)S(1)}, u32[]{:S(2)}, u32[]{:S(2)}) collective-permute-start(bf16[16,128,128]{2,1,0:T(8,128)(2,1)S(1)} %bitcast.154), channel_id=1, source_target_pairs={{0,16},{16,0},{1,17},{17,1},{2,18},{18,2},{3,19},{19,3},{4,20},{20... | collective-permute-start | bytes 1572872 | tf_op jit(solution)/shard_map/ppermute | solution.py:14
  49.7 4.0 %collective-permute-start.15 = (bf16[16,128,128]{2,1,0:T(8,128)(2,1)S(1)}, bf16[16,128,128]{2,1,0:T(8,128)(2,1)}, u32[]{:S(2)}, u32[]{:S(2)}) collective-permute-start(bf16[16,128,128]{2,1,0:T(8,128)(2,1)S(1)} %bitcast.156), channel_id=1, source_target_pairs={{0,16},{16,0},{1,17},{17,1},{2,18},{18,2},{3,19},{19,3},{4,20},{20... | collective-permute-start | bytes 1572872 | tf_op jit(solution)/shard_map/ppermute | solution.py:14
  65.2 12.2 %collective-permute-start.18 = (bf16[4,128,128]{2,1,0:T(8,128)(2,1)}, bf16[4,128,128]{2,1,0:T(8,128)(2,1)S(1)}, u32[]{:S(2)}, u32[]{:S(2)}) collective-permute-start(bf16[4,128,128]{2,1,0:T(8,128)(2,1)} %get-tuple-element.191.refs_0_), channel_id=1, source_target_pairs={{0,12},{1,13},{2,14},{3,15},{4,8},{5,9},{6,10},{7,11},{8,4},{9,5},... | collective-permute-start | bytes 393224 | tf_op jit(solution)/shard_map/ppermute | solution.py:14
  65.3 12.1 %collective-permute-start.17 = (bf16[4,128,128]{2,1,0:T(8,128)(2,1)}, bf16[4,128,128]{2,1,0:T(8,128)(2,1)S(1)}, u32[]{:S(2)}, u32[]{:S(2)}) collective-permute-start(bf16[4,128,128]{2,1,0:T(8,128)(2,1)} %get-tuple-element.191.refs_0_), channel_id=1, source_target_pairs={{0,4},{1,5},{2,6},{3,7},{4,0},{5,1},{6,2},{7,3},{8,12},{9,13},{10,... | collective-permute-start | bytes 393224 | tf_op jit(solution)/shard_map/ppermute | solution.py:14
  65.4 12.1 %collective-permute-start.16 = (bf16[4,128,128]{2,1,0:T(8,128)(2,1)}, bf16[4,128,128]{2,1,0:T(8,128)(2,1)S(1)}, u32[]{:S(2)}, u32[]{:S(2)}) collective-permute-start(bf16[4,128,128]{2,1,0:T(8,128)(2,1)} %get-tuple-element.191.refs_0_), channel_id=1, source_target_pairs={{0,8},{1,9},{2,10},{3,11},{4,12},{5,13},{6,14},{7,15},{8,0},{9,1},... | collective-permute-start | bytes 393224 | tf_op jit(solution)/shard_map/ppermute | solution.py:14
  68.0 9.5 %collective-permute-start.20 = (f32[72,128]{1,0:T(8,128)S(1)}, f32[72,128]{1,0:T(8,128)S(1)}, u32[]{:S(2)}, u32[]{:S(2)}) collective-permute-start(f32[72,128]{1,0:T(8,128)S(1)} %fusion.24), channel_id=1, source_target_pairs={{0,8},{1,9},{2,10},{3,11},{4,12},{5,13},{6,14},{7,15},{8,0},{9,1},... | collective-permute-start | bytes 110600 | tf_op jit(solution)/shard_map/ppermute | solution.py:14
  78.5 7.7 %collective-permute-start.23 = (f32[72,128]{1,0:T(8,128)S(1)}, f32[72,128]{1,0:T(8,128)S(1)}, u32[]{:S(2)}, u32[]{:S(2)}) collective-permute-start(f32[72,128]{1,0:T(8,128)S(1)} %add.786), channel_id=1, source_target_pairs={{0,4},{1,5},{2,6},{3,7},{4,0},{5,1},{6,2},{7,3},{8,12},{9,13},{10,... | collective-permute-start | bytes 110600 | tf_op jit(solution)/shard_map/ppermute | solution.py:14
  82.8 7.1 %collective-permute-start.22 = (bf16[4,2,128,128]{3,2,1,0:T(8,128)(2,1)S(1)}, bf16[4,2,128,128]{3,2,1,0:T(8,128)(2,1)S(1)}, u32[]{:S(2)}, u32[]{:S(2)}) collective-permute-start(bf16[4,2,128,128]{3,2,1,0:T(8,128)(2,1)S(1)} %get-tuple-element.203), channel_id=1, source_target_pairs={{0,1},{1,0},{2,3},{3,2},{4,5},{5,4},{6,7},{7,6},{8,9},{9,8},{10,11... | collective-permute-start | bytes 786440 | tf_op jit(solution)/shard_map/ppermute | solution.py:14
  82.8 7.1 %collective-permute-start.21 = (bf16[4,2,128,128]{3,2,1,0:T(8,128)(2,1)S(1)}, bf16[4,2,128,128]{3,2,1,0:T(8,128)(2,1)S(1)}, u32[]{:S(2)}, u32[]{:S(2)}) collective-permute-start(bf16[4,2,128,128]{3,2,1,0:T(8,128)(2,1)S(1)} %get-tuple-element.204), channel_id=1, source_target_pairs={{0,2},{1,3},{2,0},{3,1},{4,6},{5,7},{6,4},{7,5},{8,10},{9,11},{10,... | collective-permute-start | bytes 786440 | tf_op jit(solution)/shard_map/ppermute | solution.py:14
  90.0 8.2 %collective-permute-start.26 = (f32[72,128]{1,0:T(8,128)S(1)}, f32[72,128]{1,0:T(8,128)S(1)}, u32[]{:S(2)}, u32[]{:S(2)}) collective-permute-start(f32[72,128]{1,0:T(8,128)S(1)} %add.787), channel_id=1, source_target_pairs={{0,2},{1,3},{2,0},{3,1},{4,6},{5,7},{6,4},{7,5},{8,10},{9,11},{10,... | collective-permute-start | bytes 110600 | tf_op jit(solution)/shard_map/ppermute | solution.py:14
  90.8 11.5 %collective-permute-start.24 = (bf16[8,2,128,128]{3,2,1,0:T(8,128)(2,1)S(1)}, bf16[8,2,128,128]{3,2,1,0:T(8,128)(2,1)S(1)}, u32[]{:S(2)}, u32[]{:S(2)}) collective-permute-start(bf16[8,2,128,128]{3,2,1,0:T(8,128)(2,1)S(1)} %pad_maximum_fusion.5.refs_0_), channel_id=1, source_target_pairs={{0,1},{1,0},{2,3},{3,2},{4,5},{5,4},{6,7},{7,6},{8,9},{9,8},{10,11... | collective-permute-start | bytes 1572872 | tf_op jit(solution)/shard_map/ppermute | solution.py:14
  91.9 11.7 %collective-permute-start.25 = (bf16[8,2,128,128]{3,2,1,0:T(8,128)(2,1)S(1)}, bf16[8,2,128,128]{3,2,1,0:T(8,128)(2,1)S(1)}, u32[]{:S(2)}, u32[]{:S(2)}) collective-permute-start(bf16[8,2,128,128]{3,2,1,0:T(8,128)(2,1)S(1)} %pad_maximum_fusion.6.refs_1_), channel_id=1, source_target_pairs={{0,2},{1,3},{2,0},{3,1},{4,6},{5,7},{6,4},{7,5},{8,10},{9,11},{10,... | collective-permute-start | bytes 1572872 | tf_op jit(solution)/shard_map/ppermute | solution.py:14
  103.6 3.6 %collective-permute-start.27 = (f32[72,128]{1,0:T(8,128)S(1)}, f32[72,128]{1,0:T(8,128)S(1)}, u32[]{:S(2)}, u32[]{:S(2)}) collective-permute-start(f32[72,128]{1,0:T(8,128)S(1)} %add.788), channel_id=1, source_target_pairs={{0,1},{1,0},{2,3},{3,2},{4,5},{5,4},{6,7},{7,6},{8,9},{9,8},{10,11... | collective-permute-start | bytes 110600 | tf_op jit(solution)/shard_map/ppermute | solution.py:14
  107.4 8.1 %collective-permute-start.29 = (f32[72,128]{1,0:T(8,128)S(1)}, f32[72,128]{1,0:T(8,128)S(1)}, u32[]{:S(2)}, u32[]{:S(2)}) collective-permute-start(f32[72,128]{1,0:T(8,128)S(1)} %add.789), channel_id=1, source_target_pairs={{0,16},{16,0},{1,17},{17,1},{2,18},{18,2},{3,19},{19,3},{4,20},{20... | collective-permute-start | bytes 110600 | tf_op jit(solution)/shard_map/ppermute | solution.py:14
  (6 other events, 42.5 us)

commit v5 on v3

--- a/solution.py
+++ b/solution.py
@@ -96,19 +96,38 @@
     return rows.astype(jnp.float32).astype(jnp.bfloat16)
 
 
-def block_of(code, rows):
+def blocks_of(lines, rows):
+    zero = jnp.zeros((), jnp.bfloat16)
+    one = jnp.ones((), jnp.bfloat16)
+    empty = jnp.zeros((128, 128), jnp.bfloat16)
+
     def tile(x):
         return jnp.broadcast_to(x.astype(jnp.float32), (16, 128)).astype(jnp.bfloat16)[None]
 
-    o = code >> 16
-    zero = jnp.zeros((), jnp.bfloat16)
-    one = jnp.ones((), jnp.bfloat16)
-    w = tile((code & (FIELD - 1)).astype(jnp.float32) * UNIT)
-    left = jnp.where(rows == tile(o >> 7), w, zero).reshape(128, 128)
-    right = jnp.where(rows == tile(o & 127), one, zero).reshape(128, 128)
-    return lax.dot_general(
-        left, right, (((1,), (1,)), ((), ())), preferred_element_type=jnp.float32
-    ).astype(jnp.bfloat16)
+    def factors(code):
+        o = code >> 16
+        w = tile((code & (FIELD - 1)).astype(jnp.float32) * UNIT)
+        left = jnp.where(rows == tile(o >> 7), w, zero).reshape(128, 128)
+        right = jnp.where(rows == tile(o & 127), one, zero).reshape(128, 128)
+        return left, right
+
+    blocks = []
+    for u in range(0, len(lines), 2):
+        (left, right), (left_too, right_too) = factors(lines[u]), factors(lines[u + 1])
+        both = lax.dot_general(
+            jnp.concatenate([left, left_too], axis=1),
+            jnp.concatenate(
+                [
+                    jnp.concatenate([right, empty], axis=1),
+                    jnp.concatenate([empty, right_too], axis=1),
+                ],
+                axis=0,
+            ),
+            (((1,), (1,)), ((), ())),
+            preferred_element_type=jnp.float32,
+        ).astype(jnp.bfloat16)
+        blocks += [both[:, :128], both[:, 128:]]
+    return blocks
 
 
 def pack_kernel(meta, pos, codes, labels, out):
@@ -146,7 +165,7 @@
 
         lines = [codes[pl.ds(lists[0, i * TURN + u], 1), :] for u in range(TURN)]
         for u in range(0, TURN, GROUP):
-            blocks = [block_of(line, rows) for line in lines[u : u + GROUP]]
+            blocks = blocks_of(lines[u : u + GROUP], rows)
             for k, block in enumerate(blocks):
                 dbuf[slot, u + k] = block
         out_copy(i).start()
@@ -262,9 +281,9 @@
     totals[...] = jnp.zeros_like(totals)
 
     def turn(i, _):
-        for u in range(GROUP):
+        lines = [codes[pl.ds(order[i * GROUP + u], 1), :] for u in range(GROUP)]
+        for u, block in enumerate(blocks_of(lines, rows)):
             p = i * GROUP + u
-            block = block_of(codes[pl.ds(order[p], 1), :], rows)
             totals[dst[p]] += jnp.dot(block, panel[col[p]], preferred_element_type=jnp.float32)
         return 0
 
@@ -593,9 +612,7 @@
         pairs = gather_pieces(features.reshape(per, 128, width), prepare)
         lines = came.reshape(n_col * stride, 128)
         here = run_build((0, QUARTERS[4]), listed, lines, [], None)
-        last, here, any_over = lax.optimization_barrier(
-            ([pair[1] for pair in pairs], here, any_over)
-        )
+        last, here = lax.optimization_barrier(([pair[1] for pair in pairs], here))
         feat = []
         for pair in [[pair[0], x] for pair, x in zip(pairs, last)]:
             rows = [pair]

time: 116 us -> 119 us (1.026)
  Pallas kernels: 36.1 us -> 57.2 us
  waiting for transfers between devices: 26.7 us -> 11.7 us
  starting transfers between devices: 37.2 us -> 34.3 us
    ppermute x26, waiting for transfers between devices: 26.7 us -> 11.7 us  [swap(): return lax.ppermute(x, axis, [(i, i ^ bit) for i in range(n)])]
    pallas_call x4, Pallas kernels: 16.2 us -> 29.6 us  [run_build(): pl.pallas_call(functools.partial(build_kernel, span), out_shape=jax.Shape...]
    pallas_call x2, Pallas kernels: 5.75 us -> 11.8 us  [run_backward(): pl.pallas_call(functools.partial(backward_kernel, n, span), out_shape=jax...]
    ppermute x26, starting transfers between devices: 30.2 us -> 27.6 us  [swap(): return lax.ppermute(x, axis, [(i, i ^ bit) for i in range(n)])]
  transfers between devices with their start and end apart: 27 -> 27, of which waited for: 10 -> 6; matrix products, arithmetic and copies ran while one was open for 8% -> 8% of each run, Pallas kernels for 23% -> 40%
where the time goes in v5:
time: 119 us; the launch traced here: 118 us
  Pallas kernels  57.2 us (48%)
  starting transfers between devices  34.3 us (29%)
  waiting for transfers between devices  11.7 us (10%)
  other arithmetic  7.93 us (7%)
  between operations  3.16 us (3%)
  local copies, waits for them, and re-layouts  2.47 us (2%)
    pallas_call x4, Pallas kernels, run_build(): pl.pallas_call(functools.partial(build_kernel, span), out_shape=jax.Shape...  29.6 us
    ppermute x26, starting transfers between devices, swap(): return lax.ppermute(x, axis, [(i, i ^ bit) for i in range(n)])  27.6 us
    pallas_call x2, Pallas kernels, run_backward(): pl.pallas_call(functools.partial(backward_kernel, n, span), out_shape=jax...  11.8 us
    ppermute x26, waiting for transfers between devices, swap(): return lax.ppermute(x, axis, [(i, i ^ bit) for i in range(n)])  11.7 us
    pallas_call x1, Pallas kernels, run_forward(): pl.pallas_call(functools.partial(forward_kernel, n, scale, span), out_sha...  10.4 us
    all_to_all x1, starting transfers between devices, shards(): lax.all_to_all(packed.reshape(n_col, stride, 128), 'col', split_axis=0, c...  6.69 us
    pallas_call x2, Pallas kernels, make_lists(): pl.pallas_call(functools.partial(list_kernel, keys, split, fills), out_sh...  3.31 us
  transfers between devices with their start and end apart: 27, of which 6 were waited for; matrix products, arithmetic and copies ran while one was open for 8% of the time, Pallas kernels for 40%

profile of v5, /device:TPU:0, one launch (start us, length us, event | category | flops | bytes accessed | tf_op | source)
XLA Modules:
  0.0 117.8 jit_solution(3220098042456583192)
XLA Ops:
  0.6 5.1 %collective-permute-start.7 = (bf16[4,128,128]{2,1,0:T(8,128)(2,1)}, bf16[4,128,128]{2,1,0:T(8,128)(2,1)S(1)}, u32[]{:S(2)}, u32[]{:S(2)}) collective-permute-start(bf16[4,128,128]{2,1,0:T(8,128)(2,1)} %bitcast.168), channel_id=1, source_target_pairs={{0,12},{1,13},{2,14},{3,15},{4,8},{5,9},{6,10},{7,11},{8,4},{9,5},... | collective-permute-start | bytes 393224 | tf_op jit(solution)/shard_map/ppermute | solution.py:14
  10.8 2.1 %shard_map.120 = s32[1152,128]{1,0:T(8,128)} custom-call(s32[1]{0:T(128)} %bitcast.17.meta, s32[512]{0:T(512)S(1)} %get-tuple-element.214.pos, s32[520,128]{1,0:T(8,128)S(1)} %pad.13.codes, s32[16,128]{1,0:T(8,128)S(1)} %concatenate.24.labels), custom_call_target="tpu_custom_call" | custom-call | tf_op jit(solution)/shard_map/pallas_call | solution.py:337
  12.9 6.7 %all-to-all-start = ((s32[16,72,128]{2,1,0:T(8,128)}), s32[16,72,128]{2,1,0:T(8,128)S(1)}, u32[]{:S(2)}, u32[]{:S(2)}) async-start(s32[16,72,128]{2,1,0:T(8,128)} %bitcast.21), calls=%async_computation | async-start | bytes 1179648 | tf_op jit(solution)/shard_map/all_to_all | solution.py:580
  23.1 2.0 %collective-permute-start.8 = (bf16[4,2,128,128]{3,2,1,0:T(8,128)(2,1)S(1)}, bf16[4,2,128,128]{3,2,1,0:T(8,128)(2,1)S(1)}, u32[]{:S(2)}, u32[]{:S(2)}) collective-permute-start(bf16[4,2,128,128]{3,2,1,0:T(8,128)(2,1)S(1)} %get-tuple-element.206), channel_id=1, source_target_pairs={{0,2},{1,3},{2,0},{3,1},{4,6},{5,7},{6,4},{7,5},{8,10},{9,11},{10,... | collective-permute-start | bytes 786440 | tf_op jit(solution)/shard_map/ppermute | solution.py:14
  25.1 1.5 %collective-permute-start.9 = (bf16[4,2,128,128]{3,2,1,0:T(8,128)(2,1)S(1)}, bf16[4,2,128,128]{3,2,1,0:T(8,128)(2,1)S(1)}, u32[]{:S(2)}, u32[]{:S(2)}) collective-permute-start(bf16[4,2,128,128]{3,2,1,0:T(8,128)(2,1)S(1)} %get-tuple-element.205), channel_id=1, source_target_pairs={{0,1},{1,0},{2,3},{3,2},{4,5},{5,4},{6,7},{7,6},{8,9},{9,8},{10,11... | collective-permute-start | bytes 786440 | tf_op jit(solution)/shard_map/ppermute | solution.py:14
  26.5 5.1 %shard_map.123.refs_1_ = bf16[672,128,128]{2,1,0:T(8,128)(2,1)} custom-call(s32[1,128]{1,0:T(1,128)S(1)} %get-tuple-element.86.marks, s32[2,672]{1,0:T(2,128)S(1)} %get-tuple-element.87.lists, s32[520,128]{1,0:T(8,128)S(1)} %pad.13.codes, bf16[4,4,128,128]{3,2,1,0:T(8,128)(2,1)S(1)} %pad_maximum_fusion.1.refs_0_), custom_call_target="tpu_custom_call" | custom-call | flops 5637144576 | bytes 22020096 | tf_op jit(solution)/shard_map/pallas_call | solution.py:349
  31.6 1.9 %collective-permute-done.8 = bf16[4,2,128,128]{3,2,1,0:T(8,128)(2,1)S(1)} collective-permute-done((bf16[4,2,128,128]{3,2,1,0:T(8,128)(2,1)S(1)}, bf16[4,2,128,128]{3,2,1,0:T(8,128)(2,1)S(1)}, u32[]{:S(2)}, u32[]{:S(2)}) %collective-permute-start.8) | collective-permute-done | bytes 262176 | tf_op jit(solution)/shard_map/ppermute | solution.py:14
  33.6 1.7 %collective-permute-done.9 = bf16[4,2,128,128]{3,2,1,0:T(8,128)(2,1)S(1)} collective-permute-done((bf16[4,2,128,128]{3,2,1,0:T(8,128)(2,1)S(1)}, bf16[4,2,128,128]{3,2,1,0:T(8,128)(2,1)S(1)}, u32[]{:S(2)}, u32[]{:S(2)}) %collective-permute-start.9) | collective-permute-done | bytes 262176 | tf_op jit(solution)/shard_map/ppermute | solution.py:14
  35.3 1.2 %collective-permute-start.10 = (bf16[8,2,128,128]{3,2,1,0:T(8,128)(2,1)S(1)}, bf16[8,2,128,128]{3,2,1,0:T(8,128)(2,1)S(1)}, u32[]{:S(2)}, u32[]{:S(2)}) collective-permute-start(bf16[8,2,128,128]{3,2,1,0:T(8,128)(2,1)S(1)} %pad_maximum_fusion.2), channel_id=1, source_target_pairs={{0,1},{1,0},{2,3},{3,2},{4,5},{5,4},{6,7},{7,6},{8,9},{9,8},{10,11... | collective-permute-start | bytes 1572872 | tf_op jit(solution)/shard_map/ppermute | solution.py:14
  38.7 2.3 %shard_map.121 = (s32[2,1088]{1,0:T(2,128)S(1)}, s32[1,256]{1,0:T(1,128)S(1)}, s32[1,128]{1,0:T(1,128)S(1)}) custom-call(s32[1,1024]{1,0:T(1,128)S(1)} %get-tuple-element.212.key_ref, s32[1,1024]{1,0:T(1,128)S(1)} %add.739.refs_0_, s32[1,1024]{1,0:T(1,128)S(1)} %get-tuple-element.211.refs_1_), custom_call_target="tpu_custom_call" | custom-call | flops 268435456 | bytes 1048576 | tf_op jit(solution)/shard_map/pallas_call | solution.py:473
  41.0 9.4 %shard_map.124.dense = bf16[1088,128,128]{2,1,0:T(8,128)(2,1)} custom-call(s32[1,128]{1,0:T(1,128)S(1)} %get-tuple-element.83.marks, s32[2,1088]{1,0:T(2,128)S(1)} %get-tuple-element.84.lists, s32[1152,128]{1,0:T(8,128)S(1)} %bitcast.145), custom_call_target="tpu_custom_call" | custom-call | flops 9126805504 | bytes 35651584 | tf_op jit(solution)/shard_map/pallas_call | solution.py:349
  53.7 10.4 %shard_map.125 = (bf16[512,128]{1,0:T(8,128)(2,1)}, bf16[4,128,128]{2,1,0:T(8,128)(2,1)}, f32[136,128]{1,0:T(8,128)S(1)}) custom-call(s32[1,128]{1,0:T(1,128)S(1)} %get-tuple-element.83.marks, s32[2,1088]{1,0:T(2,128)S(1)} %get-tuple-element.84.lists, s32[1,256]{1,0:T(1,128)S(1)} %get-tuple-element.85.owner, bf16[128,128]{1,0:T(8,128)(2,1)S(1)} %copy-done.3, ...), custom_call_target="tpu_custom_call" | custom-call | flops 18253611008 | bytes 35651584 | tf_op jit(solution)/shard_map/pallas_call | solution.py:369
  64.5 3.3 %collective-permute-start.18 = (bf16[4,128,128]{2,1,0:T(8,128)(2,1)}, bf16[4,128,128]{2,1,0:T(8,128)(2,1)S(1)}, u32[]{:S(2)}, u32[]{:S(2)}) collective-permute-start(bf16[4,128,128]{2,1,0:T(8,128)(2,1)} %get-tuple-element.191.refs_0_), channel_id=1, source_target_pairs={{0,12},{1,13},{2,14},{3,15},{4,8},{5,9},{6,10},{7,11},{8,4},{9,5},... | collective-permute-start | bytes 393224 | tf_op jit(solution)/shard_map/ppermute | solution.py:14
  69.0 2.9 %collective-permute-start.20 = (f32[72,128]{1,0:T(8,128)S(1)}, f32[72,128]{1,0:T(8,128)S(1)}, u32[]{:S(2)}, u32[]{:S(2)}) collective-permute-start(f32[72,128]{1,0:T(8,128)S(1)} %fusion.24), channel_id=1, source_target_pairs={{0,8},{1,9},{2,10},{3,11},{4,12},{5,13},{6,14},{7,15},{8,0},{9,1},... | collective-permute-start | bytes 110600 | tf_op jit(solution)/shard_map/ppermute | solution.py:14
  71.9 9.3 %shard_map.126.refs_1_ = bf16[672,128,128]{2,1,0:T(8,128)(2,1)} custom-call(s32[1,128]{1,0:T(1,128)S(1)} %get-tuple-element.86.marks, s32[2,672]{1,0:T(2,128)S(1)} %get-tuple-element.87.lists, s32[520,128]{1,0:T(8,128)S(1)} %pad.13.codes, bf16[4,128,128]{2,1,0:T(8,128)(2,1)} %get-tuple-element.191.refs_0_, ...), custom_call_target="tpu_custom_call", output_to_operand_aliasing={{}: (4, {})} | custom-call | flops 5637144576 | bytes 22020096 | tf_op jit(solution)/shard_map/pallas_call | solution.py:349
  81.2 1.2 %collective-permute-done.20 = f32[72,128]{1,0:T(8,128)S(1)} collective-permute-done((f32[72,128]{1,0:T(8,128)S(1)}, f32[72,128]{1,0:T(8,128)S(1)}, u32[]{:S(2)}, u32[]{:S(2)}) %collective-permute-start.20) | collective-permute-done | bytes 36896 | tf_op jit(solution)/shard_map/ppermute | solution.py:14
  83.5 1.4 %collective-permute-start.21 = (bf16[4,2,128,128]{3,2,1,0:T(8,128)(2,1)S(1)}, bf16[4,2,128,128]{3,2,1,0:T(8,128)(2,1)S(1)}, u32[]{:S(2)}, u32[]{:S(2)}) collective-permute-start(bf16[4,2,128,128]{3,2,1,0:T(8,128)(2,1)S(1)} %get-tuple-element.204), channel_id=1, source_target_pairs={{0,2},{1,3},{2,0},{3,1},{4,6},{5,7},{6,4},{7,5},{8,10},{9,11},{10,... | collective-permute-start | bytes 786440 | tf_op jit(solution)/shard_map/ppermute | solution.py:14
  84.9 2.0 %collective-permute-start.23 = (f32[72,128]{1,0:T(8,128)S(1)}, f32[72,128]{1,0:T(8,128)S(1)}, u32[]{:S(2)}, u32[]{:S(2)}) collective-permute-start(f32[72,128]{1,0:T(8,128)S(1)} %add.786), channel_id=1, source_target_pairs={{0,4},{1,5},{2,6},{3,7},{4,0},{5,1},{6,2},{7,3},{8,12},{9,13},{10,... | collective-permute-start | bytes 110600 | tf_op jit(solution)/shard_map/ppermute | solution.py:14
  86.9 5.9 %shard_map.127.dense = bf16[672,128,128]{2,1,0:T(8,128)(2,1)} custom-call(s32[1,128]{1,0:T(1,128)S(1)} %get-tuple-element.86.marks, s32[2,672]{1,0:T(2,128)S(1)} %get-tuple-element.87.lists, s32[520,128]{1,0:T(8,128)S(1)} %pad.13.codes, bf16[4,4,128,128]{3,2,1,0:T(8,128)(2,1)S(1)} %pad_maximum_fusion.4.refs_0_, ...), custom_call_target="tpu_custom_call", output_to_operand_aliasing={{}: (4, {})} | custom-call | flops 5637144576 | bytes 22020096 | tf_op jit(solution)/shard_map/pallas_call | solution.py:349
  93.3 1.4 %collective-permute-start.25 = (bf16[8,2,128,128]{3,2,1,0:T(8,128)(2,1)S(1)}, bf16[8,2,128,128]{3,2,1,0:T(8,128)(2,1)S(1)}, u32[]{:S(2)}, u32[]{:S(2)}) collective-permute-start(bf16[8,2,128,128]{3,2,1,0:T(8,128)(2,1)S(1)} %pad_maximum_fusion.6), channel_id=1, source_target_pairs={{0,2},{1,3},{2,0},{3,1},{4,6},{5,7},{6,4},{7,5},{8,10},{9,11},{10,... | collective-permute-start | bytes 1572872 | tf_op jit(solution)/shard_map/ppermute | solution.py:14
  95.4 5.9 %shard_map.128.before = f32[8,128,128]{2,1,0:T(8,128)S(1)} custom-call(s32[1,128]{1,0:T(1,128)S(1)} %get-tuple-element.86.marks, s32[2,672]{1,0:T(2,128)S(1)} %get-tuple-element.87.lists, s32[1,128]{1,0:T(1,128)S(1)} %get-tuple-element.97.owner, f32[8,128,128]{2,1,0:T(8,128)S(1)} %broadcast_in_dim.60.before, bf16[672,128,128]{2,1,0:T(8,128)(2,1)} %shard_map.127.dense, ...), custom_call_target="tpu_custom_call" | custom-call | flops 11274289152 | bytes 22020096 | tf_op jit(solution)/shard_map/pallas_call | solution.py:395
  101.3 5.6 %collective-permute-done.26 = f32[72,128]{1,0:T(8,128)S(1)} collective-permute-done((f32[72,128]{1,0:T(8,128)S(1)}, f32[72,128]{1,0:T(8,128)S(1)}, u32[]{:S(2)}, u32[]{:S(2)}) %collective-permute-start.26) | collective-permute-done | bytes 36896 | tf_op jit(solution)/shard_map/ppermute | solution.py:14
  106.9 1.5 %collective-permute-start.27 = (f32[72,128]{1,0:T(8,128)S(1)}, f32[72,128]{1,0:T(8,128)S(1)}, u32[]{:S(2)}, u32[]{:S(2)}) collective-permute-start(f32[72,128]{1,0:T(8,128)S(1)} %add.788), channel_id=1, source_target_pairs={{0,1},{1,0},{2,3},{3,2},{4,5},{5,4},{6,7},{7,6},{8,9},{9,8},{10,11... | collective-permute-start | bytes 110600 | tf_op jit(solution)/shard_map/ppermute | solution.py:14
  108.4 5.9 %shard_map.129 = f32[8,128,128]{2,1,0:T(8,128)S(1)} custom-call(s32[1,128]{1,0:T(1,128)S(1)} %get-tuple-element.86.marks, s32[2,672]{1,0:T(2,128)S(1)} %get-tuple-element.87.lists, s32[1,128]{1,0:T(1,128)S(1)} %get-tuple-element.97.owner, f32[8,128,128]{2,1,0:T(8,128)S(1)} %shard_map.128.before, bf16[672,128,128]{2,1,0:T(8,128)(2,1)} %shard_map.127.dense, ...), custom_call_target="tpu_custom_call" | custom-call | flops 11274289152 | bytes 22020096 | tf_op jit(solution)/shard_map/pallas_call | solution.py:395
  (109 shorter events, 19.0 us)
Async XLA Ops:
  0.6 22.3 %collective-permute-start.7 = (bf16[4,128,128]{2,1,0:T(8,128)(2,1)}, bf16[4,128,128]{2,1,0:T(8,128)(2,1)S(1)}, u32[]{:S(2)}, u32[]{:S(2)}) collective-permute-start(bf16[4,128,128]{2,1,0:T(8,128)(2,1)} %bitcast.168), channel_id=1, source_target_pairs={{0,12},{1,13},{2,14},{3,15},{4,8},{5,9},{6,10},{7,11},{8,4},{9,5},... | collective-permute-start | bytes 393224 | tf_op jit(solution)/shard_map/ppermute | solution.py:14
  5.8 17.2 %collective-permute-start.6 = (bf16[4,128,128]{2,1,0:T(8,128)(2,1)}, bf16[4,128,128]{2,1,0:T(8,128)(2,1)S(1)}, u32[]{:S(2)}, u32[]{:S(2)}) collective-permute-start(bf16[4,128,128]{2,1,0:T(8,128)(2,1)} %bitcast.169), channel_id=1, source_target_pairs={{0,4},{1,5},{2,6},{3,7},{4,0},{5,1},{6,2},{7,3},{8,12},{9,13},{10,... | collective-permute-start | bytes 393224 | tf_op jit(solution)/shard_map/ppermute | solution.py:14
  5.8 17.2 %collective-permute-start.5 = (bf16[4,128,128]{2,1,0:T(8,128)(2,1)}, bf16[4,128,128]{2,1,0:T(8,128)(2,1)S(1)}, u32[]{:S(2)}, u32[]{:S(2)}) collective-permute-start(bf16[4,128,128]{2,1,0:T(8,128)(2,1)} %bitcast.170), channel_id=1, source_target_pairs={{0,8},{1,9},{2,10},{3,11},{4,12},{5,13},{6,14},{7,15},{8,0},{9,1},... | collective-permute-start | bytes 393224 | tf_op jit(solution)/shard_map/ppermute | solution.py:14
  12.9 24.9 %all-to-all-start = ((s32[16,72,128]{2,1,0:T(8,128)}), s32[16,72,128]{2,1,0:T(8,128)S(1)}, u32[]{:S(2)}, u32[]{:S(2)}) async-start(s32[16,72,128]{2,1,0:T(8,128)} %bitcast.21), calls=%async_computation | async-start | bytes 1179648 | tf_op jit(solution)/shard_map/all_to_all | solution.py:580
  23.1 10.4 %collective-permute-start.8 = (bf16[4,2,128,128]{3,2,1,0:T(8,128)(2,1)S(1)}, bf16[4,2,128,128]{3,2,1,0:T(8,128)(2,1)S(1)}, u32[]{:S(2)}, u32[]{:S(2)}) collective-permute-start(bf16[4,2,128,128]{3,2,1,0:T(8,128)(2,1)S(1)} %get-tuple-element.206), channel_id=1, source_target_pairs={{0,2},{1,3},{2,0},{3,1},{4,6},{5,7},{6,4},{7,5},{8,10},{9,11},{10,... | collective-permute-start | bytes 786440 | tf_op jit(solution)/shard_map/ppermute | solution.py:14
  25.1 10.2 %collective-permute-start.9 = (bf16[4,2,128,128]{3,2,1,0:T(8,128)(2,1)S(1)}, bf16[4,2,128,128]{3,2,1,0:T(8,128)(2,1)S(1)}, u32[]{:S(2)}, u32[]{:S(2)}) collective-permute-start(bf16[4,2,128,128]{3,2,1,0:T(8,128)(2,1)S(1)} %get-tuple-element.205), channel_id=1, source_target_pairs={{0,1},{1,0},{2,3},{3,2},{4,5},{5,4},{6,7},{7,6},{8,9},{9,8},{10,11... | collective-permute-start | bytes 786440 | tf_op jit(solution)/shard_map/ppermute | solution.py:14
  35.3 15.1 %collective-permute-start.10 = (bf16[8,2,128,128]{3,2,1,0:T(8,128)(2,1)S(1)}, bf16[8,2,128,128]{3,2,1,0:T(8,128)(2,1)S(1)}, u32[]{:S(2)}, u32[]{:S(2)}) collective-permute-start(bf16[8,2,128,128]{3,2,1,0:T(8,128)(2,1)S(1)} %pad_maximum_fusion.2), channel_id=1, source_target_pairs={{0,1},{1,0},{2,3},{3,2},{4,5},{5,4},{6,7},{7,6},{8,9},{9,8},{10,11... | collective-permute-start | bytes 1572872 | tf_op jit(solution)/shard_map/ppermute | solution.py:14
  36.5 13.9 %collective-permute-start.11 = (bf16[8,2,128,128]{3,2,1,0:T(8,128)(2,1)S(1)}, bf16[8,2,128,128]{3,2,1,0:T(8,128)(2,1)S(1)}, u32[]{:S(2)}, u32[]{:S(2)}) collective-permute-start(bf16[8,2,128,128]{3,2,1,0:T(8,128)(2,1)S(1)} %pad_maximum_fusion.3), channel_id=1, source_target_pairs={{0,2},{1,3},{2,0},{3,1},{4,6},{5,7},{6,4},{7,5},{8,10},{9,11},{10,... | collective-permute-start | bytes 1572872 | tf_op jit(solution)/shard_map/ppermute | solution.py:14
  37.2 16.4 %collective-permute-start.12 = (bf16[16,128,128]{2,1,0:T(8,128)(2,1)S(1)}, bf16[16,128,128]{2,1,0:T(8,128)(2,1)S(1)}, u32[]{:S(2)}, u32[]{:S(2)}) collective-permute-start(bf16[16,128,128]{2,1,0:T(8,128)(2,1)S(1)} %bitcast.147), channel_id=1, source_target_pairs={{0,16},{16,0},{1,17},{17,1},{2,18},{18,2},{3,19},{19,3},{4,20},{20... | collective-permute-start | bytes 1572872 | tf_op jit(solution)/shard_map/ppermute | solution.py:14
  37.2 16.5 %collective-permute-start.14 = (bf16[16,128,128]{2,1,0:T(8,128)(2,1)S(1)}, bf16[16,128,128]{2,1,0:T(8,128)(2,1)}, u32[]{:S(2)}, u32[]{:S(2)}) collective-permute-start(bf16[16,128,128]{2,1,0:T(8,128)(2,1)S(1)} %bitcast.149), channel_id=1, source_target_pairs={{0,16},{16,0},{1,17},{17,1},{2,18},{18,2},{3,19},{19,3},{4,20},{20... | collective-permute-start | bytes 1572872 | tf_op jit(solution)/shard_map/ppermute | solution.py:14
  50.4 3.3 %collective-permute-start.13 = (bf16[16,128,128]{2,1,0:T(8,128)(2,1)S(1)}, bf16[16,128,128]{2,1,0:T(8,128)(2,1)S(1)}, u32[]{:S(2)}, u32[]{:S(2)}) collective-permute-start(bf16[16,128,128]{2,1,0:T(8,128)(2,1)S(1)} %bitcast.154), channel_id=1, source_target_pairs={{0,16},{16,0},{1,17},{17,1},{2,18},{18,2},{3,19},{19,3},{4,20},{20... | collective-permute-start | bytes 1572872 | tf_op jit(solution)/shard_map/ppermute | solution.py:14
  50.5 3.2 %collective-permute-start.15 = (bf16[16,128,128]{2,1,0:T(8,128)(2,1)S(1)}, bf16[16,128,128]{2,1,0:T(8,128)(2,1)}, u32[]{:S(2)}, u32[]{:S(2)}) collective-permute-start(bf16[16,128,128]{2,1,0:T(8,128)(2,1)S(1)} %bitcast.156), channel_id=1, source_target_pairs={{0,16},{16,0},{1,17},{17,1},{2,18},{18,2},{3,19},{19,3},{4,20},{20... | collective-permute-start | bytes 1572872 | tf_op jit(solution)/shard_map/ppermute | solution.py:14
  64.4 4.5 %collective-permute-start.19 = (f32[1,72,128]{2,1,0:T(8,128)S(1)}, f32[1,72,128]{2,1,0:T(8,128)S(1)}, u32[]{:S(2)}, u32[]{:S(2)}) collective-permute-start(f32[1,72,128]{2,1,0:T(8,128)S(1)} %slice_bitcast_fusion.10), channel_id=1, source_target_pairs={{0,16},{16,0},{1,17},{17,1},{2,18},{18,2},{3,19},{19,3},{4,20},{20... | collective-permute-start | bytes 110600 | tf_op jit(solution)/shard_map/ppermute | solution.py:14
  64.5 17.9 %collective-permute-start.18 = (bf16[4,128,128]{2,1,0:T(8,128)(2,1)}, bf16[4,128,128]{2,1,0:T(8,128)(2,1)S(1)}, u32[]{:S(2)}, u32[]{:S(2)}) collective-permute-start(bf16[4,128,128]{2,1,0:T(8,128)(2,1)} %get-tuple-element.191.refs_0_), channel_id=1, source_target_pairs={{0,12},{1,13},{2,14},{3,15},{4,8},{5,9},{6,10},{7,11},{8,4},{9,5},... | collective-permute-start | bytes 393224 | tf_op jit(solution)/shard_map/ppermute | solution.py:14
  67.9 14.6 %collective-permute-start.17 = (bf16[4,128,128]{2,1,0:T(8,128)(2,1)}, bf16[4,128,128]{2,1,0:T(8,128)(2,1)S(1)}, u32[]{:S(2)}, u32[]{:S(2)}) collective-permute-start(bf16[4,128,128]{2,1,0:T(8,128)(2,1)} %get-tuple-element.191.refs_0_), channel_id=1, source_target_pairs={{0,4},{1,5},{2,6},{3,7},{4,0},{5,1},{6,2},{7,3},{8,12},{9,13},{10,... | collective-permute-start | bytes 393224 | tf_op jit(solution)/shard_map/ppermute | solution.py:14
  68.9 13.5 %collective-permute-start.16 = (bf16[4,128,128]{2,1,0:T(8,128)(2,1)}, bf16[4,128,128]{2,1,0:T(8,128)(2,1)S(1)}, u32[]{:S(2)}, u32[]{:S(2)}) collective-permute-start(bf16[4,128,128]{2,1,0:T(8,128)(2,1)} %get-tuple-element.191.refs_0_), channel_id=1, source_target_pairs={{0,8},{1,9},{2,10},{3,11},{4,12},{5,13},{6,14},{7,15},{8,0},{9,1},... | collective-permute-start | bytes 393224 | tf_op jit(solution)/shard_map/ppermute | solution.py:14
  69.0 13.4 %collective-permute-start.20 = (f32[72,128]{1,0:T(8,128)S(1)}, f32[72,128]{1,0:T(8,128)S(1)}, u32[]{:S(2)}, u32[]{:S(2)}) collective-permute-start(f32[72,128]{1,0:T(8,128)S(1)} %fusion.24), channel_id=1, source_target_pairs={{0,8},{1,9},{2,10},{3,11},{4,12},{5,13},{6,14},{7,15},{8,0},{9,1},... | collective-permute-start | bytes 110600 | tf_op jit(solution)/shard_map/ppermute | solution.py:14
  83.5 9.4 %collective-permute-start.21 = (bf16[4,2,128,128]{3,2,1,0:T(8,128)(2,1)S(1)}, bf16[4,2,128,128]{3,2,1,0:T(8,128)(2,1)S(1)}, u32[]{:S(2)}, u32[]{:S(2)}) collective-permute-start(bf16[4,2,128,128]{3,2,1,0:T(8,128)(2,1)S(1)} %get-tuple-element.204), channel_id=1, source_target_pairs={{0,2},{1,3},{2,0},{3,1},{4,6},{5,7},{6,4},{7,5},{8,10},{9,11},{10,... | collective-permute-start | bytes 786440 | tf_op jit(solution)/shard_map/ppermute | solution.py:14
  84.9 8.1 %collective-permute-start.22 = (bf16[4,2,128,128]{3,2,1,0:T(8,128)(2,1)S(1)}, bf16[4,2,128,128]{3,2,1,0:T(8,128)(2,1)S(1)}, u32[]{:S(2)}, u32[]{:S(2)}) collective-permute-start(bf16[4,2,128,128]{3,2,1,0:T(8,128)(2,1)S(1)} %get-tuple-element.203), channel_id=1, source_target_pairs={{0,1},{1,0},{2,3},{3,2},{4,5},{5,4},{6,7},{7,6},{8,9},{9,8},{10,11... | collective-permute-start | bytes 786440 | tf_op jit(solution)/shard_map/ppermute | solution.py:14
  84.9 8.0 %collective-permute-start.23 = (f32[72,128]{1,0:T(8,128)S(1)}, f32[72,128]{1,0:T(8,128)S(1)}, u32[]{:S(2)}, u32[]{:S(2)}) collective-permute-start(f32[72,128]{1,0:T(8,128)S(1)} %add.786), channel_id=1, source_target_pairs={{0,4},{1,5},{2,6},{3,7},{4,0},{5,1},{6,2},{7,3},{8,12},{9,13},{10,... | collective-permute-start | bytes 110600 | tf_op jit(solution)/shard_map/ppermute | solution.py:14
  93.0 13.8 %collective-permute-start.24 = (bf16[8,2,128,128]{3,2,1,0:T(8,128)(2,1)S(1)}, bf16[8,2,128,128]{3,2,1,0:T(8,128)(2,1)S(1)}, u32[]{:S(2)}, u32[]{:S(2)}) collective-permute-start(bf16[8,2,128,128]{3,2,1,0:T(8,128)(2,1)S(1)} %pad_maximum_fusion.5), channel_id=1, source_target_pairs={{0,1},{1,0},{2,3},{3,2},{4,5},{5,4},{6,7},{7,6},{8,9},{9,8},{10,11... | collective-permute-start | bytes 1572872 | tf_op jit(solution)/shard_map/ppermute | solution.py:14
  93.3 13.6 %collective-permute-start.25 = (bf16[8,2,128,128]{3,2,1,0:T(8,128)(2,1)S(1)}, bf16[8,2,128,128]{3,2,1,0:T(8,128)(2,1)S(1)}, u32[]{:S(2)}, u32[]{:S(2)}) collective-permute-start(bf16[8,2,128,128]{3,2,1,0:T(8,128)(2,1)S(1)} %pad_maximum_fusion.6), channel_id=1, source_target_pairs={{0,2},{1,3},{2,0},{3,1},{4,6},{5,7},{6,4},{7,5},{8,10},{9,11},{10,... | collective-permute-start | bytes 1572872 | tf_op jit(solution)/shard_map/ppermute | solution.py:14
  94.7 12.1 %collective-permute-start.26 = (f32[72,128]{1,0:T(8,128)S(1)}, f32[72,128]{1,0:T(8,128)S(1)}, u32[]{:S(2)}, u32[]{:S(2)}) collective-permute-start(f32[72,128]{1,0:T(8,128)S(1)} %add.787), channel_id=1, source_target_pairs={{0,2},{1,3},{2,0},{3,1},{4,6},{5,7},{6,4},{7,5},{8,10},{9,11},{10,... | collective-permute-start | bytes 110600 | tf_op jit(solution)/shard_map/ppermute | solution.py:14
  106.9 7.4 %collective-permute-start.27 = (f32[72,128]{1,0:T(8,128)S(1)}, f32[72,128]{1,0:T(8,128)S(1)}, u32[]{:S(2)}, u32[]{:S(2)}) collective-permute-start(f32[72,128]{1,0:T(8,128)S(1)} %add.788), channel_id=1, source_target_pairs={{0,1},{1,0},{2,3},{3,2},{4,5},{5,4},{6,7},{7,6},{8,9},{9,8},{10,11... | collective-permute-start | bytes 110600 | tf_op jit(solution)/shard_map/ppermute | solution.py:14
  (8 other events, 62.5 us)
